TPU v7x, 256 devices: a whole 4x4x8 slice. The times are simulated.
256 devices in a mesh: blk: 32 (over y, z_hi, core), freq: 8 (over x, z_lo).
Axes of the slice: x: 4, y: 4, z: 8 (z_hi: 4, z_lo: 2; z = z_hi * 2 + z_lo), core: 2. Of those that a mesh axis runs over, the one named last changes fastest.
Arguments:
- forcing_hat: bfloat16 [2, 64, 2, 5, 2048, 128], P(None, 'freq', None, None, 'blk'), may hold values from -6 to 6
- mean_speed: float32 [2048, 128], P('blk'), may hold values from 0.2 to 0.9
- block_order: int32 [128], P('blk'), may hold values from 0 to 3, as said below
- block_flips: int32 [128], P('blk'), may hold values from 0 to 1
Outputs:
- response_hat: float32 [2, 64, 2, 5, 2048, 128], P(None, 'freq', None, None, 'blk')
Inputs may be any that keep to these rules, and one draw needn't show every extreme that they name: `block_order`: each aligned group of 4 entries (the blocks of one index of blk) is a permutation of 0 to 3.
All inputs are finite; a program needn't handle non-finite values.
Results may differ from a plain program's by a relative error of at most 0.0021.
Values sent between devices are 32-bit elements; how exact they have to be, the bound alone decides.
No kernel may reach another device: no remote copies, remote signals or barrier semaphores. Data moves between devices by JAX's collectives and lax.ppermute only.
A program may use at most 64 MiB of HBM per device.

v0:
```python
import math

import jax
import jax.numpy as jnp
from jax import lax
from jax.sharding import PartitionSpec as P

F = 64
STEPS = 8


time_step = 0.4
viscosity = 0.5


def padded(x, sides, width):
    for axis, dim in sides:
        peers, length = (lax.axis_size(axis), x.shape[dim])
        up = [(i, (i + 1) % peers) for i in range(peers - 1)]
        down = [(j, i) for i, j in up]
        last = lax.slice_in_dim(x, length - width, length, axis=dim)
        initial = lax.slice_in_dim(x, 0, width, axis=dim)
        before = lax.ppermute(last, axis, up)
        after = lax.ppermute(initial, axis, down)
        x = jnp.concatenate([before, x, after], axis=dim)
    return x


def flip_blocks(blocked, flip_flags):
    return jnp.where((flip_flags == 1)[:, None, None], blocked[..., ::-1], blocked)


def to_chain(values, chain_ids, flip_flags, block_count):
    blocked = values.reshape(
        values.shape[:-2] + (block_count, values.shape[-2] // block_count, values.shape[-1])
    )
    placed = jnp.take(blocked, chain_ids, axis=-3)
    placed = flip_blocks(placed, jnp.take(flip_flags, chain_ids))
    return placed.reshape(values.shape)


def from_chain(values, chain_ids, flip_flags, block_count):
    inverse = jnp.argsort(chain_ids)
    blocked = values.reshape(
        values.shape[:-2] + (block_count, values.shape[-2] // block_count, values.shape[-1])
    )
    placed = jnp.take(blocked, inverse, axis=-3)
    placed = flip_blocks(placed, flip_flags)
    return placed.reshape(values.shape)


def tendency(extended, mean_speed):
    center = extended[:, :, 1:-1, 1:-1]
    upper_row = extended[:, :, 2:, 1:-1]
    lower_row = extended[:, :, :-2, 1:-1]
    right_col = extended[:, :, 1:-1, 2:]
    left_col = extended[:, :, 1:-1, :-2]
    stream_diff = 0.5 * (upper_row - lower_row)
    cross_diff = 0.5 * (right_col - left_col)
    laplace = upper_row + lower_row + right_col + left_col - 4.0 * center
    advection = -mean_speed * stream_diff
    divergence = stream_diff[:, 1] + cross_diff[:, 2]
    rates = jnp.stack(
        [
            advection[:, 0] - divergence,
            advection[:, 1] - stream_diff[:, 3],
            advection[:, 2] - cross_diff[:, 3],
            advection[:, 3] - divergence,
            advection[:, 4],
        ],
        axis=1,
    )
    return rates + viscosity * laplace


def synthesis_table(freq_ids):
    angular = (freq_ids + 1.0) * (math.pi / F)
    times = jnp.arange(STEPS, dtype=jnp.float32)
    phase = times[:, None] * angular[None, :]
    table = jnp.stack([jnp.cos(phase), -jnp.sin(phase)], axis=1) / math.sqrt(F)
    return table.astype(jnp.bfloat16)


def analysis_table(freq_ids):
    angular = (freq_ids + 1.0) * (math.pi / F)
    times = jnp.arange(1, STEPS + 1, dtype=jnp.float32)
    phase = angular[:, None] * times[None, :]
    return jnp.stack([jnp.cos(phase), -jnp.sin(phase)], axis=0) / math.sqrt(STEPS)


def step_march(forcing, speed_rows, edges):
    fields_now = jnp.zeros((forcing.shape[0], 5) + forcing.shape[3:], jnp.float32)
    history = []
    for step_index in range(STEPS):
        extended = edges(fields_now)
        extended = jnp.pad(extended, ((0, 0), (0, 0), (0, 0), (1, 1)))
        fields_now = fields_now + time_step * (
            tendency(extended, speed_rows) + forcing[:, step_index]
        )
        history.append(fields_now)
    return jnp.stack(history, axis=1)


def local(forcing_hat, mean_speed, block_order, block_flips):
    freq_local = forcing_hat.shape[1]
    block_count = block_order.shape[0]
    freq_ids = (
        lax.axis_index("freq") * freq_local + jnp.arange(freq_local, dtype=jnp.int32)
    ).astype(jnp.float32)
    synth = synthesis_table(freq_ids)
    analysis = analysis_table(freq_ids)
    speed_chain = to_chain(mean_speed, block_order, block_flips, block_count)
    partial_sum = jnp.einsum(
        "scm,cmkvrj->ksvrj", synth, forcing_hat, preferred_element_type=jnp.float32
    )
    forcing = lax.psum(partial_sum, "freq")
    forcing = to_chain(forcing, block_order, block_flips, block_count)
    history = step_march(forcing, speed_chain, lambda state: padded(state, (("blk", 2),), 1))
    history = from_chain(history, block_order, block_flips, block_count)
    return jnp.einsum("cms,ksvrj->cmkvrj", analysis, history, precision=lax.Precision.HIGHEST)


def solution(mesh):
    placed = (P(None, "freq", None, None, "blk", None), P("blk", None), P("blk"), P("blk"))
    return jax.shard_map(
        local,
        mesh=mesh,
        in_specs=placed,
        out_specs=P(None, "freq", None, None, "blk", None),
        check_vma=False,
    )
```

profile of v0, /device:TPU:24, one launch (start us, length us, event | category | flops | bytes accessed | tf_op | source)
XLA Modules:
  0.0 269.4 jit_solution(2901165777060969498)
XLA Ops:
  6.5 2.1 collective-permute-start.1
  8.6 7.8 %collective-permute-start = (f32[2,5,1,128]{3,2,1,0:T(1,128)S(1)}, f32[2,5,1,128]{3,2,1,0:T(1,128)S(1)}, u32[]{:S(2)}, u32[]{:S(2)}) collective-permute-start(f32[2,5,1,128]{3,2,1,0:T(1,128)S(1)} %broadcast.243), channel_id=1, source_target_pairs={{8,0},{16,8},{24,16},{32,24},{40,32},{48,40},{56,48},{64,56},{72,6... | collective-permute-start | bytes 15368 | tf_op jit(solution)/shard_map/ppermute | solution.py:24
  18.1 2.0 copy.17
  23.8 126.5 %all-reduce.12.cloned.1.call-done = f32[2,8,5,4,16,128]{5,4,3,2,1,0:T(8,128)} async-done(((f32[2,8,5,4,16,128]{5,4,3,2,1,0:T(8,128)}), f32[2,8,5,4,16,128]{5,4,3,2,1,0:T(8,128)}) %all-reduce.12.cloned.1.call-update) | async-done | bytes 2621456 | tf_op jit(solution)/shard_map/psum | solution.py:116
  150.2 2.5 gather_fusion.2
  154.5 5.2 %rev.10 = f32[2,8,5,4,16,128]{5,4,2,1,0,3:T(8,128)} reverse(f32[2,8,5,4,16,128]{5,4,2,1,0,3:T(8,128)} %select_bitcast_fusion.1), dimensions={5} | reverse | bytes 5242880 | tf_op jit(solution)/shard_map/rev | solution.py:30
  159.7 2.1 broadcast_select_fusion
  162.5 4.6 %collective-permute-start.2 = (f32[2,5,1,128]{3,2,1,0:T(1,128)S(1)}, f32[2,5,1,128]{3,2,1,0:T(1,128)S(1)}, u32[]{:S(2)}, u32[]{:S(2)}) collective-permute-start(f32[2,5,1,128]{3,2,1,0:T(1,128)S(1)} %get-tuple-element.39), channel_id=1, source_target_pairs={{8,0},{16,8},{24,16},{32,24},{40,32},{48,40},{56,48},{64,56},{72,6... | collective-permute-start | bytes 15368 | tf_op jit(solution)/shard_map/ppermute | solution.py:24
  167.1 1.9 collective-permute-start.3
  169.8 5.3 %collective-permute-done.3 = f32[2,5,1,128]{3,2,1,0:T(1,128)S(1)} collective-permute-done((f32[2,5,1,128]{3,2,1,0:T(1,128)S(1)}, f32[2,5,1,128]{3,2,1,0:T(1,128)S(1)}, u32[]{:S(2)}, u32[]{:S(2)}) %collective-permute-start.3) | collective-permute-done | bytes 5152 | tf_op jit(solution)/shard_map/ppermute | solution.py:23
  176.0 1.9 collective-permute-start.4
  177.9 2.4 collective-permute-start.5
  181.1 4.8 %collective-permute-done.5 = f32[2,5,1,128]{3,2,1,0:T(1,128)S(1)} collective-permute-done((f32[2,5,1,128]{3,2,1,0:T(1,128)S(1)}, f32[2,5,1,128]{3,2,1,0:T(1,128)S(1)}, u32[]{:S(2)}, u32[]{:S(2)}) %collective-permute-start.5) | collective-permute-done | bytes 5152 | tf_op jit(solution)/shard_map/ppermute | solution.py:23
  186.8 1.9 collective-permute-start.6
  188.8 2.4 collective-permute-start.7
  191.9 4.8 %collective-permute-done.7 = f32[2,5,1,128]{3,2,1,0:T(1,128)S(1)} collective-permute-done((f32[2,5,1,128]{3,2,1,0:T(1,128)S(1)}, f32[2,5,1,128]{3,2,1,0:T(1,128)S(1)}, u32[]{:S(2)}, u32[]{:S(2)}) %collective-permute-start.7) | collective-permute-done | bytes 5152 | tf_op jit(solution)/shard_map/ppermute | solution.py:23
  197.6 1.9 collective-permute-start.8
  199.6 2.4 collective-permute-start.9
  202.7 4.8 %collective-permute-done.9 = f32[2,5,1,128]{3,2,1,0:T(1,128)S(1)} collective-permute-done((f32[2,5,1,128]{3,2,1,0:T(1,128)S(1)}, f32[2,5,1,128]{3,2,1,0:T(1,128)S(1)}, u32[]{:S(2)}, u32[]{:S(2)}) %collective-permute-start.9) | collective-permute-done | bytes 5152 | tf_op jit(solution)/shard_map/ppermute | solution.py:23
  210.4 2.4 collective-permute-start.11
  213.6 4.8 %collective-permute-done.11 = f32[2,5,1,128]{3,2,1,0:T(1,128)S(1)} collective-permute-done((f32[2,5,1,128]{3,2,1,0:T(1,128)S(1)}, f32[2,5,1,128]{3,2,1,0:T(1,128)S(1)}, u32[]{:S(2)}, u32[]{:S(2)}) %collective-permute-start.11) | collective-permute-done | bytes 5152 | tf_op jit(solution)/shard_map/ppermute | solution.py:23
  219.3 1.9 collective-permute-start.12
  221.2 2.4 collective-permute-start.13
  224.4 4.8 %collective-permute-done.13 = f32[2,5,1,128]{3,2,1,0:T(1,128)S(1)} collective-permute-done((f32[2,5,1,128]{3,2,1,0:T(1,128)S(1)}, f32[2,5,1,128]{3,2,1,0:T(1,128)S(1)}, u32[]{:S(2)}, u32[]{:S(2)}) %collective-permute-start.13) | collective-permute-done | bytes 5152 | tf_op jit(solution)/shard_map/ppermute | solution.py:23
  230.1 1.9 collective-permute-start.14
  232.0 2.6 collective-permute-start.15
  235.4 4.6 %collective-permute-done.15 = f32[2,5,1,128]{3,2,1,0:T(1,128)S(1)} collective-permute-done((f32[2,5,1,128]{3,2,1,0:T(1,128)S(1)}, f32[2,5,1,128]{3,2,1,0:T(1,128)S(1)}, u32[]{:S(2)}, u32[]{:S(2)}) %collective-permute-start.15) | collective-permute-done | bytes 5152 | tf_op jit(solution)/shard_map/ppermute | solution.py:23
  241.6 2.5 gather_fusion.3
  246.0 5.2 %rev.11 = f32[2,8,5,4,16,128]{5,4,2,1,0,3:T(8,128)} reverse(f32[2,8,5,4,16,128]{5,4,2,1,0,3:T(8,128)} %select_bitcast_fusion), dimensions={5} | reverse | bytes 5242880 | tf_op jit(solution)/shard_map/rev | solution.py:30
  251.2 2.1 broadcast_select_fusion.1
  253.6 5.5 %fusion = f32[2,8,2,5,64,128]{5,1,4,3,2,0:T(8,128)S(1)} fusion(f32[2,8,5,64,128]{4,3,2,1,0:T(8,128)S(1)} %bitcast.114, f32[1,8,8]{2,1,0:T(8,128)S(1)} %get-tuple-element.44, f32[1,8,8]{2,1,0:T(8,128)S(1)} %get-tuple-element.43), kind=kOutput, calls=%fused_computation.4 | convolution fusion | flops 125829376 | bytes 7864832 | tf_op jit(solution)/shard_map/cms,ksvrj->cmkvrj/dot_general | solution.py:120
  259.1 3.4 %copy.28 = f32[2,8,2,5,64,128]{5,4,3,2,1,0:T(8,128)} copy(f32[2,8,2,5,64,128]{5,1,4,3,2,0:T(8,128)S(1)} %fusion) | data formatting | bytes 10485760 | tf_op jit(solution)/shard_map/cms,ksvrj->cmkvrj/dot_general | solution.py:120
  (133 shorter events, 23.8 us)
Async XLA Ops:
  6.5 10.0 %copy-start = (bf16[2,8,2,5,64,128]{5,4,3,2,1,0:T(8,128)(2,1)S(1)}, bf16[2,8,2,5,64,128]{5,4,3,2,1,0:T(8,128)(2,1)}, u32[]{:S(2)}) copy-start(bf16[2,8,2,5,64,128]{5,4,3,2,1,0:T(8,128)(2,1)} %param.8) | copy-start | bytes 7864324
  6.5 143.7 %all-reduce.12.cloned.1.call-start = ((), (), s32[]{:S(2)}) async-start(), calls=%async_computation | async-start | bytes 5242880 | tf_op jit(solution)/shard_map/psum | solution.py:116
  6.5 16.7 %collective-permute-start.1 = (f32[2,5,1,128]{3,2,1,0:T(1,128)S(1)}, f32[2,5,1,128]{3,2,1,0:T(1,128)S(1)}, u32[]{:S(2)}, u32[]{:S(2)}) collective-permute-start(f32[2,5,1,128]{3,2,1,0:T(1,128)S(1)} %broadcast.243), channel_id=1, source_target_pairs={{0,8},{8,16},{16,24},{24,32},{32,40},{40,48},{48,56},{56,64},{64,7... | collective-permute-start | bytes 15368 | tf_op jit(solution)/shard_map/ppermute | solution.py:23
  8.6 14.7 %collective-permute-start = (f32[2,5,1,128]{3,2,1,0:T(1,128)S(1)}, f32[2,5,1,128]{3,2,1,0:T(1,128)S(1)}, u32[]{:S(2)}, u32[]{:S(2)}) collective-permute-start(f32[2,5,1,128]{3,2,1,0:T(1,128)S(1)} %broadcast.243), channel_id=1, source_target_pairs={{8,0},{16,8},{24,16},{32,24},{40,32},{48,40},{56,48},{64,56},{72,6... | collective-permute-start | bytes 15368 | tf_op jit(solution)/shard_map/ppermute | solution.py:24
  20.1 0.7 copy-start.2
  20.1 0.7 copy-start.4
  20.1 2.2 copy-start.3
  162.5 7.3 %collective-permute-start.2 = (f32[2,5,1,128]{3,2,1,0:T(1,128)S(1)}, f32[2,5,1,128]{3,2,1,0:T(1,128)S(1)}, u32[]{:S(2)}, u32[]{:S(2)}) collective-permute-start(f32[2,5,1,128]{3,2,1,0:T(1,128)S(1)} %get-tuple-element.39), channel_id=1, source_target_pairs={{8,0},{16,8},{24,16},{32,24},{40,32},{48,40},{56,48},{64,56},{72,6... | collective-permute-start | bytes 15368 | tf_op jit(solution)/shard_map/ppermute | solution.py:24
  167.1 7.9 %collective-permute-start.3 = (f32[2,5,1,128]{3,2,1,0:T(1,128)S(1)}, f32[2,5,1,128]{3,2,1,0:T(1,128)S(1)}, u32[]{:S(2)}, u32[]{:S(2)}) collective-permute-start(f32[2,5,1,128]{3,2,1,0:T(1,128)S(1)} %get-tuple-element.40), channel_id=1, source_target_pairs={{0,8},{8,16},{16,24},{24,32},{32,40},{40,48},{48,56},{56,64},{64,7... | collective-permute-start | bytes 15368 | tf_op jit(solution)/shard_map/ppermute | solution.py:23
  176.0 5.1 %collective-permute-start.4 = (f32[2,5,1,128]{3,2,1,0:T(1,128)S(1)}, f32[2,5,1,128]{3,2,1,0:T(1,128)S(1)}, u32[]{:S(2)}, u32[]{:S(2)}) collective-permute-start(f32[2,5,1,128]{3,2,1,0:T(1,128)S(1)} %get-tuple-element.37), channel_id=1, source_target_pairs={{8,0},{16,8},{24,16},{32,24},{40,32},{48,40},{56,48},{64,56},{72,6... | collective-permute-start | bytes 15368 | tf_op jit(solution)/shard_map/ppermute | solution.py:24
  177.9 7.9 %collective-permute-start.5 = (f32[2,5,1,128]{3,2,1,0:T(1,128)S(1)}, f32[2,5,1,128]{3,2,1,0:T(1,128)S(1)}, u32[]{:S(2)}, u32[]{:S(2)}) collective-permute-start(f32[2,5,1,128]{3,2,1,0:T(1,128)S(1)} %get-tuple-element.38), channel_id=1, source_target_pairs={{0,8},{8,16},{16,24},{24,32},{32,40},{40,48},{48,56},{56,64},{64,7... | collective-permute-start | bytes 15368 | tf_op jit(solution)/shard_map/ppermute | solution.py:23
  186.8 5.1 %collective-permute-start.6 = (f32[2,5,1,128]{3,2,1,0:T(1,128)S(1)}, f32[2,5,1,128]{3,2,1,0:T(1,128)S(1)}, u32[]{:S(2)}, u32[]{:S(2)}) collective-permute-start(f32[2,5,1,128]{3,2,1,0:T(1,128)S(1)} %get-tuple-element.35), channel_id=1, source_target_pairs={{8,0},{16,8},{24,16},{32,24},{40,32},{48,40},{56,48},{64,56},{72,6... | collective-permute-start | bytes 15368 | tf_op jit(solution)/shard_map/ppermute | solution.py:24
  188.8 7.9 %collective-permute-start.7 = (f32[2,5,1,128]{3,2,1,0:T(1,128)S(1)}, f32[2,5,1,128]{3,2,1,0:T(1,128)S(1)}, u32[]{:S(2)}, u32[]{:S(2)}) collective-permute-start(f32[2,5,1,128]{3,2,1,0:T(1,128)S(1)} %get-tuple-element.36), channel_id=1, source_target_pairs={{0,8},{8,16},{16,24},{24,32},{32,40},{40,48},{48,56},{56,64},{64,7... | collective-permute-start | bytes 15368 | tf_op jit(solution)/shard_map/ppermute | solution.py:23
  197.6 5.1 %collective-permute-start.8 = (f32[2,5,1,128]{3,2,1,0:T(1,128)S(1)}, f32[2,5,1,128]{3,2,1,0:T(1,128)S(1)}, u32[]{:S(2)}, u32[]{:S(2)}) collective-permute-start(f32[2,5,1,128]{3,2,1,0:T(1,128)S(1)} %get-tuple-element.33), channel_id=1, source_target_pairs={{8,0},{16,8},{24,16},{32,24},{40,32},{48,40},{56,48},{64,56},{72,6... | collective-permute-start | bytes 15368 | tf_op jit(solution)/shard_map/ppermute | solution.py:24
  199.6 7.9 %collective-permute-start.9 = (f32[2,5,1,128]{3,2,1,0:T(1,128)S(1)}, f32[2,5,1,128]{3,2,1,0:T(1,128)S(1)}, u32[]{:S(2)}, u32[]{:S(2)}) collective-permute-start(f32[2,5,1,128]{3,2,1,0:T(1,128)S(1)} %get-tuple-element.34), channel_id=1, source_target_pairs={{0,8},{8,16},{16,24},{24,32},{32,40},{40,48},{48,56},{56,64},{64,7... | collective-permute-start | bytes 15368 | tf_op jit(solution)/shard_map/ppermute | solution.py:23
  208.5 5.1 %collective-permute-start.10 = (f32[2,5,1,128]{3,2,1,0:T(1,128)S(1)}, f32[2,5,1,128]{3,2,1,0:T(1,128)S(1)}, u32[]{:S(2)}, u32[]{:S(2)}) collective-permute-start(f32[2,5,1,128]{3,2,1,0:T(1,128)S(1)} %get-tuple-element.31), channel_id=1, source_target_pairs={{8,0},{16,8},{24,16},{32,24},{40,32},{48,40},{56,48},{64,56},{72,6... | collective-permute-start | bytes 15368 | tf_op jit(solution)/shard_map/ppermute | solution.py:24
  210.4 7.9 %collective-permute-start.11 = (f32[2,5,1,128]{3,2,1,0:T(1,128)S(1)}, f32[2,5,1,128]{3,2,1,0:T(1,128)S(1)}, u32[]{:S(2)}, u32[]{:S(2)}) collective-permute-start(f32[2,5,1,128]{3,2,1,0:T(1,128)S(1)} %get-tuple-element.32), channel_id=1, source_target_pairs={{0,8},{8,16},{16,24},{24,32},{32,40},{40,48},{48,56},{56,64},{64,7... | collective-permute-start | bytes 15368 | tf_op jit(solution)/shard_map/ppermute | solution.py:23
  219.3 5.1 %collective-permute-start.12 = (f32[2,5,1,128]{3,2,1,0:T(1,128)S(1)}, f32[2,5,1,128]{3,2,1,0:T(1,128)S(1)}, u32[]{:S(2)}, u32[]{:S(2)}) collective-permute-start(f32[2,5,1,128]{3,2,1,0:T(1,128)S(1)} %get-tuple-element.29), channel_id=1, source_target_pairs={{8,0},{16,8},{24,16},{32,24},{40,32},{48,40},{56,48},{64,56},{72,6... | collective-permute-start | bytes 15368 | tf_op jit(solution)/shard_map/ppermute | solution.py:24
  221.2 7.9 %collective-permute-start.13 = (f32[2,5,1,128]{3,2,1,0:T(1,128)S(1)}, f32[2,5,1,128]{3,2,1,0:T(1,128)S(1)}, u32[]{:S(2)}, u32[]{:S(2)}) collective-permute-start(f32[2,5,1,128]{3,2,1,0:T(1,128)S(1)} %get-tuple-element.30), channel_id=1, source_target_pairs={{0,8},{8,16},{16,24},{24,32},{32,40},{40,48},{48,56},{56,64},{64,7... | collective-permute-start | bytes 15368 | tf_op jit(solution)/shard_map/ppermute | solution.py:23
  230.1 5.3 %collective-permute-start.14 = (f32[2,5,1,128]{3,2,1,0:T(1,128)S(1)}, f32[2,5,1,128]{3,2,1,0:T(1,128)S(1)}, u32[]{:S(2)}, u32[]{:S(2)}) collective-permute-start(f32[2,5,1,128]{3,2,1,0:T(1,128)S(1)} %get-tuple-element.27), channel_id=1, source_target_pairs={{8,0},{16,8},{24,16},{32,24},{40,32},{48,40},{56,48},{64,56},{72,6... | collective-permute-start | bytes 15368 | tf_op jit(solution)/shard_map/ppermute | solution.py:24
  232.0 7.9 %collective-permute-start.15 = (f32[2,5,1,128]{3,2,1,0:T(1,128)S(1)}, f32[2,5,1,128]{3,2,1,0:T(1,128)S(1)}, u32[]{:S(2)}, u32[]{:S(2)}) collective-permute-start(f32[2,5,1,128]{3,2,1,0:T(1,128)S(1)} %get-tuple-element.28), channel_id=1, source_target_pairs={{0,8},{8,16},{16,24},{24,32},{32,40},{40,48},{48,56},{56,64},{64,7... | collective-permute-start | bytes 15368 | tf_op jit(solution)/shard_map/ppermute | solution.py:23
  259.1 3.4 %copy-start.1 = (bf16[2,8,2,5,64,128]{5,4,3,2,1,0:T(8,128)(2,1)S(1)}, bf16[2,8,2,5,64,128]{5,4,3,2,1,0:T(8,128)(2,1)}, u32[]{:S(2)}) copy-start(bf16[2,8,2,5,64,128]{5,4,3,2,1,0:T(8,128)(2,1)} %param.8) | copy-start | bytes 7864324
Sparse Core Ops, SparseCore 0:
  20.2 129.9 all-reduce.11
where the time goes:
time: 270 us; the launch traced here: 269 us
  waiting for transfers between devices  160 us (59%)
  starting transfers between devices  42.6 us (16%)
  local copies, waits for them, and re-layouts  29.5 us (11%)
  other arithmetic  15.8 us (6%)
  between operations  14.2 us (5%)
  matrix products  7.08 us (3%)
    psum x1, waiting for transfers between devices, local(): forcing = lax.psum(partial_sum, 'freq')  126 us
    ppermute x8, waiting for transfers between devices, padded(): before = lax.ppermute(last, axis, up)  33.7 us
    ppermute x8, starting transfers between devices, padded(): after = lax.ppermute(initial, axis, down)  24 us
    ppermute x8, starting transfers between devices, padded(): before = lax.ppermute(last, axis, up)  18.6 us
    rev x3, local copies, waits for them, and re-layouts, flip_blocks(): blocked[..., ::-1]  10.5 us
    unnamed x17, local copies, waits for them, and re-layouts  5.94 us
    dot_general x1, matrix products, local(): jnp.einsum('cms,ksvrj->cmkvrj', analysis, history, precision=lax.Precisio...  5.51 us
  transfers between devices with their start and end apart: 17, of which 8 were waited for; matrix products, arithmetic and copies ran while one was open for 4% of the time, Pallas kernels for 0%

commit v1 on v0

v1 whole, which is shorter than its diff:
```python
import functools
import math

import jax
import jax.numpy as jnp
from jax import lax
from jax.experimental import pallas as pl
from jax.experimental.pallas import tpu as pltpu
from jax.sharding import PartitionSpec as P

F = 64
STEPS = 8
K = 2
FIELDS = 5
BLOCK_ROWS = 16
TILE = 8
TIME_STEP = 0.4
FOLD = 0.2
X_PAIR, X_CROSS, Z_PAIR = 2, 6, 1


def flipped(tile, lanes):
    return jnp.take_along_axis(tile, lanes, axis=1, mode="promise_in_bounds")


def lane_order(flag, rows):
    lane = lax.broadcasted_iota(jnp.int32, (rows, 128), 1)
    return jnp.where(flag == 1, 127 - lane, lane)


def edge_kernel(order, flips, forcing, speed, low, high):
    for out, place, start in ((low, 0, 0), (high, -1, BLOCK_ROWS - TILE)):
        block = order[place % order.shape[0]]
        lanes = lane_order(flips[block], TILE)
        rows = pl.ds(pl.multiple_of(block * BLOCK_ROWS + start, TILE), TILE)
        for k in range(K):
            for s in range(STEPS - 1):
                for v in range(FIELDS):
                    out[(k * (STEPS - 1) + s) * FIELDS + v] = flipped(forcing[k, s, v, rows, :], lanes)
        out[K * (STEPS - 1) * FIELDS] = flipped(speed[rows, :], lanes)


def step_kernel(k, order, flips, inside, forcing, speed, below, above, history, ext):
    blocks = order.shape[0]
    inner = blocks * BLOCK_ROWS
    rows = inner + 2 * TILE
    lanes = [lane_order(flips[order[p]], BLOCK_ROWS) for p in range(blocks)]
    at = [pl.ds(pl.multiple_of(order[p] * BLOCK_ROWS, BLOCK_ROWS), BLOCK_ROWS) for p in range(blocks)]
    last = K * (STEPS - 1) * FIELDS
    speed_ext = jnp.concatenate(
        [below[last]] + [flipped(speed[at[p], :], lanes[p]) for p in range(blocks)] + [above[last]], axis=0
    )
    with_up, with_down = 1.0 - speed_ext, 1.0 + speed_ext
    lane = lax.broadcasted_iota(jnp.int32, (rows, 128), 1)
    row = lax.broadcasted_iota(jnp.int32, (rows, 128), 0)
    first_lane, last_lane = lane == 0, lane == 127
    keep_low = inside[0].astype(jnp.float32)
    keep_high = inside[1].astype(jnp.float32)
    keep = jnp.where(row < TILE, keep_low, jnp.where(row >= inner + TILE, keep_high, 1.0))

    for s in range(STEPS):
        fresh = []
        for v in range(FIELDS):
            body = [flipped(forcing[k, s, v, at[p], :], lanes[p]) for p in range(blocks)]
            if s < STEPS - 1:
                unit = (k * (STEPS - 1) + s) * FIELDS + v
                lo, hi = below[unit], above[unit]
            else:
                lo = hi = jnp.zeros((TILE, 128), jnp.float32)
            fresh.append(TIME_STEP * jnp.concatenate([lo] + body + [hi], axis=0))
        if s == 0:
            state = fresh
        else:
            state = [ext[v] for v in range(FIELDS)]
            up = [pltpu.roll(a, rows - 1, 0) for a in state]
            down = [pltpu.roll(a, 1, 0) for a in state]
            right = [jnp.where(last_lane, 0.0, pltpu.roll(a, 127, 1)) for a in state]
            left = [jnp.where(first_lane, 0.0, pltpu.roll(a, 1, 1)) for a in state]
            div = (up[1] - down[1]) + (right[2] - left[2])
            extra = [div, up[3] - down[3], right[3] - left[3], div, None]
            new = []
            for v in range(FIELDS):
                total = state[v] + left[v] + right[v] + with_up * up[v] + with_down * down[v]
                if extra[v] is not None:
                    total = total - extra[v]
                new.append((FOLD * total + fresh[v]) * keep)
            state = new
        for v in range(FIELDS):
            if s < STEPS - 1:
                ext[v] = state[v]
            for p in range(blocks):
                first = TILE + p * BLOCK_ROWS
                history[s, v, at[p], :] = flipped(state[v][first : first + BLOCK_ROWS], lanes[p])


def analysis_kernel(both, low_part, history, out):
    tiles = history.shape[1]
    for pair in range(0, tiles, 2):
        x = history[:, pair : pair + 2].reshape(STEPS, 2 * TILE, 128)
        hi = x.astype(jnp.bfloat16)
        lo = (x - hi.astype(jnp.float32)).astype(jnp.bfloat16)
        hi = hi.reshape(STEPS * 2 * TILE, 128)
        lo = lo.reshape(STEPS * 2 * TILE, 128)
        y = jnp.dot(both[...], jnp.concatenate([hi, lo], axis=0), preferred_element_type=jnp.float32)
        y = y + jnp.dot(low_part[...], hi, preferred_element_type=jnp.float32)
        out[:, pair : pair + 2] = y.reshape(16, 2, TILE, 128)


def synthesis_table(freq_ids):
    angular = (freq_ids + 1.0) * (math.pi / F)
    times = jnp.arange(STEPS, dtype=jnp.float32)
    phase = times[:, None] * angular[None, :]
    table = jnp.stack([jnp.cos(phase), -jnp.sin(phase)], axis=1) / math.sqrt(F)
    return table.astype(jnp.bfloat16)


def analysis_table(freq_ids):
    angular = (freq_ids + 1.0) * (math.pi / F)
    times = jnp.arange(1, STEPS + 1, dtype=jnp.float32)
    phase = angular[:, None] * times[None, :]
    return jnp.stack([jnp.cos(phase), -jnp.sin(phase)], axis=0) / math.sqrt(STEPS)


def swap(x, mask):
    return lax.ppermute(x, "freq", [(i, i ^ mask) for i in range(lax.axis_size("freq"))])


def halves(x, bit):
    half = x.shape[1] // 2
    keep = lax.dynamic_slice_in_dim(x, bit * half, half, 1)
    send = lax.dynamic_slice_in_dim(x, (1 - bit) * half, half, 1)
    return keep, send


def joined(mine, other, bit):
    return jnp.concatenate([jnp.where(bit == 0, mine, other), jnp.where(bit == 0, other, mine)], axis=1)


def group_sum(x, order, bits):
    a, b, c = order
    keep, send = halves(x, bits[a])
    x = keep + swap(send, a)
    keep, send = halves(x, bits[b])
    x = keep + swap(send, b)
    x = x + swap(x, c)
    x = joined(x, swap(x, b), bits[b])
    return joined(x, swap(x, a), bits[a])


def smem():
    return pl.BlockSpec(memory_space=pltpu.SMEM)


def vmem():
    return pl.BlockSpec(memory_space=pltpu.VMEM)


def local(forcing_hat, mean_speed, block_order, block_flips):
    freq_local = forcing_hat.shape[1]
    rows = mean_speed.shape[0]
    freq = lax.axis_index("freq")
    x_at = freq // 2
    bits = {X_PAIR: (x_at % 2) ^ (x_at // 2), X_CROSS: x_at // 2, Z_PAIR: freq % 2}
    freq_ids = (freq * freq_local + jnp.arange(freq_local, dtype=jnp.int32)).astype(jnp.float32)
    synth = synthesis_table(freq_ids)
    forcing = jnp.einsum("scm,cmkvrj->ksvrj", synth, forcing_hat, preferred_element_type=jnp.float32)

    edge_units = K * (STEPS - 1) * FIELDS + 1
    low, high = pl.pallas_call(
        edge_kernel,
        out_shape=[jax.ShapeDtypeStruct((edge_units, TILE, 128), jnp.float32)] * 2,
        in_specs=[smem(), smem(), vmem(), vmem()],
        out_specs=[vmem(), vmem()],
        name="edges",
    )(block_order, block_flips, forcing, mean_speed)
    peers = lax.axis_size("blk")
    below = lax.ppermute(high, "blk", [(i, i + 1) for i in range(peers - 1)])
    above = lax.ppermute(low, "blk", [(i + 1, i) for i in range(peers - 1)])
    here = lax.axis_index("blk")
    inside = jnp.stack([here > 0, here < peers - 1]).astype(jnp.int32)

    table = analysis_table(freq_ids).reshape(2 * freq_local, STEPS)
    table_hi = table.astype(jnp.bfloat16)
    table_lo = (table - table_hi.astype(jnp.float32)).astype(jnp.bfloat16)
    eye = jnp.eye(2 * TILE, dtype=jnp.bfloat16)

    def spread(t):
        return (t[:, None, :, None] * eye[None, :, None, :]).reshape(2 * freq_local * 2 * TILE, STEPS * 2 * TILE)

    wide_hi, wide_lo = spread(table_hi), spread(table_lo)
    both = jnp.concatenate([wide_hi, wide_hi], axis=1)

    tiles = FIELDS * rows // TILE
    links = (X_PAIR, X_CROSS, Z_PAIR)
    sums = []
    for k in range(K):
        history = pl.pallas_call(
            functools.partial(step_kernel, k),
            out_shape=jax.ShapeDtypeStruct((STEPS, FIELDS, rows, 128), jnp.float32),
            in_specs=[smem(), smem(), smem(), vmem(), vmem(), vmem(), vmem()],
            out_specs=vmem(),
            scratch_shapes=[pltpu.VMEM((FIELDS, rows + 2 * TILE, 128), jnp.float32)],
            name=f"march{k}",
        )(block_order, block_flips, inside, forcing, mean_speed, below, above)
        history = history.reshape(STEPS, tiles, TILE, 128)
        cuts = [16, 12, 12] if k == 0 else [12, 16, 12]
        done, parts = 0, []
        for i, cut in enumerate(cuts):
            part = history[:, done : done + cut]
            parts.append(group_sum(part, [links[(i + j) % 3] for j in range(3)], bits))
            done += cut
        sums.append(jnp.concatenate(parts, axis=1))
    total = jnp.concatenate(sums, axis=1)

    group = 8
    out = pl.pallas_call(
        analysis_kernel,
        out_shape=jax.ShapeDtypeStruct((2 * freq_local, K * tiles, TILE, 128), jnp.float32),
        grid=(K * tiles // group,),
        in_specs=[
            vmem(),
            vmem(),
            pl.BlockSpec((STEPS, group, TILE, 128), lambda i: (0, i, 0, 0)),
        ],
        out_specs=pl.BlockSpec((2 * freq_local, group, TILE, 128), lambda i: (0, i, 0, 0)),
        name="analysis",
    )(both, wide_lo, total)
    return out.reshape(2, freq_local, K, FIELDS, rows, 128)


def solution(mesh):
    placed = (P(None, "freq", None, None, "blk", None), P("blk", None), P("blk"), P("blk"))
    return jax.shard_map(
        local,
        mesh=mesh,
        in_specs=placed,
        out_specs=P(None, "freq", None, None, "blk", None),
        check_vma=False,
    )
```

time: 270 us -> 122 us (0.45)
  waiting for transfers between devices: 160 us -> 24.7 us
  Pallas kernels: 0 us -> 23.8 us
  local copies, waits for them, and re-layouts: 29.5 us -> 11.8 us
  between operations: 14.2 us -> 0.42 us
  matrix products: 7.08 us -> 1.57 us
  other arithmetic: 15.8 us -> 11.7 us
  starting transfers between devices: 42.6 us -> 46.7 us
    psum x1 -> x0, waiting for transfers between devices: 126 us -> none  [local(): forcing = lax.psum(partial_sum, 'freq')]
    pallas_call x0 -> x4, Pallas kernels: none -> 23.8 us  [the longest x2 12.2 us: local(): pl.pallas_call(functools.partial(step_kernel, k), out_shape=jax.ShapeDtyp...]
    rev x3 -> x0, local copies, waits for them, and re-layouts: 10.5 us -> none  [flip_blocks(): blocked[..., ::-1]]
    ppermute x16 -> x32, waiting for transfers between devices: 33.7 us -> 24.7 us  [the longest x30 22.1 us: swap(): lax.ppermute(x, 'freq', [(i, i ^ mask) for i in range(lax.axis_size('freq...]
    select_n x7 -> x6, other arithmetic: 8.01 us -> 0.1 us  [joined(): jnp.where(bit == 0, mine, other)]
    unnamed x32 -> x11, other arithmetic: 0.43 us -> 8.02 us
    gather x4 -> x0, local copies, waits for them, and re-layouts: 6.15 us -> none  [the longest x2 3.03 us: to_chain(): placed = jnp.take(blocked, chain_ids, axis=-3)]
    dot_general x1 -> x0, matrix products: 5.51 us -> none  [local(): jnp.einsum('cms,ksvrj->cmkvrj', analysis, history, precision=lax.Precisio...]
  transfers between devices with their start and end apart: 17 -> 32, of which waited for: 8 -> 13; matrix products, arithmetic and copies ran while one was open for 4% -> 11% of each run, Pallas kernels for 0% -> 0%
where the time goes in v1:
time: 122 us; the launch traced here: 121 us
  starting transfers between devices  46.7 us (38%)
  waiting for transfers between devices  24.7 us (20%)
  Pallas kernels  23.8 us (20%)
  local copies, waits for them, and re-layouts  11.8 us (10%)
  other arithmetic  11.7 us (10%)
  matrix products  1.57 us (1%)
    ppermute x30, starting transfers between devices, swap(): lax.ppermute(x, 'freq', [(i, i ^ mask) for i in range(lax.axis_size('freq...  36.9 us
    ppermute x30, waiting for transfers between devices, swap(): lax.ppermute(x, 'freq', [(i, i ^ mask) for i in range(lax.axis_size('freq...  22.1 us
    pallas_call x2, Pallas kernels, local(): pl.pallas_call(functools.partial(step_kernel, k), out_shape=jax.ShapeDtyp...  12.2 us
    pallas_call x1, Pallas kernels, local(): pl.pallas_call(analysis_kernel, out_shape=jax.ShapeDtypeStruct((2 * freq_...  8.84 us
    unnamed x11, other arithmetic  8.02 us
    ppermute x1, starting transfers between devices, local(): above = lax.ppermute(low, 'blk', [(i + 1, i) for i in range(peers - 1)])  7.83 us
    slice x4, local copies, waits for them, and re-layouts, local(): part = history[:, done:done + cut]  5.31 us
    pallas_call x1, Pallas kernels, local(): pl.pallas_call(edge_kernel, out_shape=[jax.ShapeDtypeStruct((edge_units,...  2.75 us
  transfers between devices with their start and end apart: 32, of which 13 were waited for; matrix products, arithmetic and copies ran while one was open for 11% of the time, Pallas kernels for 0%

profile of v1, /device:TPU:24, one launch (start us, length us, event | category | flops | bytes accessed | tf_op | source)
XLA Modules:
  0.0 120.7 jit_solution(11842342457206159851)
XLA Ops:
  0.1 1.7 %copy-done = bf16[2,8,2,5,64,128]{5,4,3,2,1,0:T(8,128)(2,1)S(1)} copy-done((bf16[2,8,2,5,64,128]{5,4,3,2,1,0:T(8,128)(2,1)S(1)}, bf16[2,8,2,5,64,128]{5,4,3,2,1,0:T(8,128)(2,1)}, u32[]{:S(2)}) %copy-start) | copy-done | bytes 2621464
  1.7 1.6 %fusion.2 = f32[8,2,5,64,128]{4,0,3,2,1:T(8,128)S(1)} fusion(bf16[2,8,2,5,64,128]{5,4,3,2,1,0:T(8,128)(2,1)S(1)} %copy-done, f32[8,1,8]{2,0,1:T(8,128)S(1)} %get-tuple-element.32, f32[8,1,8]{2,0,1:T(8,128)S(1)} %get-tuple-element.31), kind=kOutput, calls=%fused_computation.3 | convolution fusion | flops 20971904 | bytes 5243392 | tf_op jit(solution)/shard_map/scm,cmkvrj->ksvrj/dot_general | solution.py:166
  3.3 2.0 %copy.22 = f32[8,2,5,64,128]{4,3,2,0,1:T(8,128)} copy(f32[8,2,5,64,128]{4,0,3,2,1:T(8,128)S(1)} %fusion.2) | data formatting | bytes 5242880 | tf_op jit(solution)/shard_map/scm,cmkvrj->ksvrj/dot_general | solution.py:166
  5.3 2.8 %edges.1 = (f32[71,8,128]{2,1,0:T(8,128)}, f32[71,8,128]{2,1,0:T(8,128)}) custom-call(s32[4]{0:T(128)} %order.5, s32[4]{0:T(128)} %flips.5, f32[2,8,5,64,128]{4,3,2,1,0:T(8,128)} %bitcast.22, f32[64,128]{1,0:T(8,128)} %speed.5), custom_call_target="tpu_custom_call" | custom-call | tf_op jit(solution)/shard_map/edges/pallas_call | solution.py:169
  8.1 1.9 %collective-permute-start = (f32[71,8,128]{2,1,0:T(8,128)}, f32[71,8,128]{2,1,0:T(8,128)S(1)}, u32[]{:S(2)}, u32[]{:S(2)}) collective-permute-start(f32[71,8,128]{2,1,0:T(8,128)} %get-tuple-element.7), channel_id=1, source_target_pairs={{0,8},{8,16},{16,24},{24,32},{32,40},{40,48},{48,56},{56,64},{64,7... | collective-permute-start | bytes 872456 | tf_op jit(solution)/shard_map/ppermute | solution.py:177
  10.0 7.8 %collective-permute-start.1 = (f32[71,8,128]{2,1,0:T(8,128)}, f32[71,8,128]{2,1,0:T(8,128)}, u32[]{:S(2)}, u32[]{:S(2)}) collective-permute-start(f32[71,8,128]{2,1,0:T(8,128)} %get-tuple-element.8), channel_id=1, source_target_pairs={{8,0},{16,8},{24,16},{32,24},{40,32},{48,40},{56,48},{64,56},{72,6... | collective-permute-start | bytes 872456 | tf_op jit(solution)/shard_map/ppermute | solution.py:178
  19.1 1.4 %mul.169 = bf16[256,128]{1,0:T(8,128)(2,1)S(1)} reshape(bf16[16,16,8,16]{3,2,1,0:T(8,128)(2,1)} %get-tuple-element.28) | data formatting | bytes 131072 | tf_op jit(solution)/shard_map/mul | solution.py:188
  22.9 2.6 %collective-permute-done.1.above = f32[71,8,128]{2,1,0:T(8,128)} collective-permute-done((f32[71,8,128]{2,1,0:T(8,128)}, f32[71,8,128]{2,1,0:T(8,128)}, u32[]{:S(2)}, u32[]{:S(2)}) %collective-permute-start.1) | collective-permute-done | bytes 290848 | tf_op jit(solution)/shard_map/ppermute | solution.py:178
  25.4 6.1 %march1.1 = f32[8,5,64,128]{3,2,1,0:T(8,128)} custom-call(s32[4]{0:T(128)} %order.5, s32[4]{0:T(128)} %flips.5, s32[2]{0:T(128)} %add_convert_fusion.inside, f32[2,8,5,64,128]{4,3,2,1,0:T(8,128)} %bitcast.23, f32[64,128]{1,0:T(8,128)} %speed.5, f32[71,8,128]{2,1,0:T(8,128)} %copy-done.2, f32[71,8,128]{2,1,0:T(8,128)} %collective-permute-done.1.above), custom_call_target="tpu_custom_call" | custom-call | tf_op jit(solution)/shard_map/march1/pallas_call | solution.py:197
  31.5 1.9 %fusion.15 = (f32[8,12,8,128]{3,2,1,0:T(8,128)}, f32[8,12,8,128]{3,2,1,0:T(8,128)S(1)}) fusion(f32[8,40,8,128]{3,2,1,0:T(8,128)} %bitcast.27), kind=kLoop, calls=%fused_computation.81 | loop fusion | bytes 1572864 | tf_op jit(solution)/shard_map/slice | solution.py:209
  34.5 6.1 %march0.1 = f32[8,5,64,128]{3,2,1,0:T(8,128)} custom-call(s32[4]{0:T(128)} %order.5, s32[4]{0:T(128)} %flips.5, s32[2]{0:T(128)} %add_convert_fusion.inside, f32[2,8,5,64,128]{4,3,2,1,0:T(8,128)} %bitcast.24, f32[64,128]{1,0:T(8,128)} %speed.5, f32[71,8,128]{2,1,0:T(8,128)} %copy-done.2, f32[71,8,128]{2,1,0:T(8,128)} %collective-permute-done.1.above), custom_call_target="tpu_custom_call" | custom-call | tf_op jit(solution)/shard_map/march0/pallas_call | solution.py:197
  43.2 2.8 %collective-permute-start.22 = (f32[8,8,8,128]{3,2,1,0:T(8,128)S(1)}, f32[8,8,8,128]{3,2,1,0:T(8,128)S(1)}, u32[]{:S(2)}, u32[]{:S(2)}) collective-permute-start(f32[8,8,8,128]{3,2,1,0:T(8,128)S(1)} %constant_dynamic-slice_fusion.3), channel_id=1, source_target_pairs={{0,6},{1,7},{2,4},{3,5},{4,2},{5,3},{6,0},{7,1},{8,14},{9,15},{10,... | collective-permute-start | bytes 786440 | tf_op jit(solution)/shard_map/ppermute | solution.py:125
  46.3 2.1 %collective-permute-start.12 = (f32[8,6,8,128]{3,2,1,0:T(8,128)S(1)}, f32[8,6,8,128]{3,2,1,0:T(8,128)S(1)}, u32[]{:S(2)}, u32[]{:S(2)}) collective-permute-start(f32[8,6,8,128]{3,2,1,0:T(8,128)S(1)} %constant_dynamic-slice_fusion.7), channel_id=1, source_target_pairs={{0,1},{1,0},{2,3},{3,2},{4,5},{5,4},{6,7},{7,6},{8,9},{9,8},{10,11... | collective-permute-start | bytes 589832 | tf_op jit(solution)/shard_map/ppermute | solution.py:125
  48.4 1.2 %collective-permute-start.7 = (f32[8,6,8,128]{3,2,1,0:T(8,128)S(1)}, f32[8,6,8,128]{3,2,1,0:T(8,128)S(1)}, u32[]{:S(2)}, u32[]{:S(2)}) collective-permute-start(f32[8,6,8,128]{3,2,1,0:T(8,128)S(1)} %constant_dynamic-slice_fusion.9), channel_id=1, source_target_pairs={{0,6},{1,7},{2,4},{3,5},{4,2},{5,3},{6,0},{7,1},{8,14},{9,15},{10,... | collective-permute-start | bytes 589832 | tf_op jit(solution)/shard_map/ppermute | solution.py:125
  50.8 1.5 %collective-permute-start.2 = (f32[8,8,8,128]{3,2,1,0:T(8,128)S(1)}, f32[8,8,8,128]{3,2,1,0:T(8,128)S(1)}, u32[]{:S(2)}, u32[]{:S(2)}) collective-permute-start(f32[8,8,8,128]{3,2,1,0:T(8,128)S(1)} %constant_dynamic-slice_fusion.11), channel_id=1, source_target_pairs={{0,2},{1,3},{2,0},{3,1},{4,6},{5,7},{6,4},{7,5},{8,10},{9,11},{10,... | collective-permute-start | bytes 786440 | tf_op jit(solution)/shard_map/ppermute | solution.py:125
  54.4 2.8 %collective-permute-start.18 = (f32[8,3,8,128]{3,2,1,0:T(8,128)S(1)}, f32[8,3,8,128]{3,2,1,0:T(8,128)S(1)}, u32[]{:S(2)}, u32[]{:S(2)}) collective-permute-start(f32[8,3,8,128]{3,2,1,0:T(8,128)S(1)} %constant_dynamic-slice_fusion.4), channel_id=1, source_target_pairs={{0,6},{1,7},{2,4},{3,5},{4,2},{5,3},{6,0},{7,1},{8,14},{9,15},{10,... | collective-permute-start | bytes 294920 | tf_op jit(solution)/shard_map/ppermute | solution.py:125
  57.6 2.4 %collective-permute-start.8 = (f32[8,3,8,128]{3,2,1,0:T(8,128)S(1)}, f32[8,3,8,128]{3,2,1,0:T(8,128)S(1)}, u32[]{:S(2)}, u32[]{:S(2)}) collective-permute-start(f32[8,3,8,128]{3,2,1,0:T(8,128)S(1)} %constant_dynamic-slice_fusion.8), channel_id=1, source_target_pairs={{0,1},{1,0},{2,3},{3,2},{4,5},{5,4},{6,7},{7,6},{8,9},{9,8},{10,11... | collective-permute-start | bytes 294920 | tf_op jit(solution)/shard_map/ppermute | solution.py:125
  60.1 1.4 %collective-permute-start.23 = (f32[8,4,8,128]{3,2,1,0:T(8,128)S(1)}, f32[8,4,8,128]{3,2,1,0:T(8,128)S(1)}, u32[]{:S(2)}, u32[]{:S(2)}) collective-permute-start(f32[8,4,8,128]{3,2,1,0:T(8,128)S(1)} %constant_dynamic-slice_fusion.2), channel_id=1, source_target_pairs={{0,1},{1,0},{2,3},{3,2},{4,5},{5,4},{6,7},{7,6},{8,9},{9,8},{10,11... | collective-permute-start | bytes 393224 | tf_op jit(solution)/shard_map/ppermute | solution.py:125
  61.7 1.9 %collective-permute-start.29 = (f32[8,3,8,128]{3,2,1,0:T(8,128)S(1)}, f32[8,3,8,128]{3,2,1,0:T(8,128)S(1)}, u32[]{:S(2)}, u32[]{:S(2)}) collective-permute-start(f32[8,3,8,128]{3,2,1,0:T(8,128)S(1)} %dynamic-slice_add_fusion.8), channel_id=1, source_target_pairs={{0,6},{1,7},{2,4},{3,5},{4,2},{5,3},{6,0},{7,1},{8,14},{9,15},{10,... | collective-permute-start | bytes 294920 | tf_op jit(solution)/shard_map/ppermute | solution.py:125
  64.8 2.2 %collective-permute-start.14 = (f32[8,3,8,128]{3,2,1,0:T(8,128)S(1)}, f32[8,3,8,128]{3,2,1,0:T(8,128)S(1)}, u32[]{:S(2)}, u32[]{:S(2)}) collective-permute-start(f32[8,3,8,128]{3,2,1,0:T(8,128)S(1)} %dynamic-slice_add_fusion.10), channel_id=1, source_target_pairs={{0,6},{1,7},{2,4},{3,5},{4,2},{5,3},{6,0},{7,1},{8,14},{9,15},{10,... | collective-permute-start | bytes 294920 | tf_op jit(solution)/shard_map/ppermute | solution.py:125
  67.1 1.4 %collective-permute-done.29 = f32[8,3,8,128]{3,2,1,0:T(8,128)S(1)} collective-permute-done((f32[8,3,8,128]{3,2,1,0:T(8,128)S(1)}, f32[8,3,8,128]{3,2,1,0:T(8,128)S(1)}, u32[]{:S(2)}, u32[]{:S(2)}) %collective-permute-start.29) | collective-permute-done | bytes 98336 | tf_op jit(solution)/shard_map/ppermute | solution.py:125
  68.5 2.0 %collective-permute-start.3 = (f32[8,4,8,128]{3,2,1,0:T(8,128)S(1)}, f32[8,4,8,128]{3,2,1,0:T(8,128)S(1)}, u32[]{:S(2)}, u32[]{:S(2)}) collective-permute-start(f32[8,4,8,128]{3,2,1,0:T(8,128)S(1)} %constant_dynamic-slice_fusion.10), channel_id=1, source_target_pairs={{0,6},{1,7},{2,4},{3,5},{4,2},{5,3},{6,0},{7,1},{8,14},{9,15},{10,... | collective-permute-start | bytes 393224 | tf_op jit(solution)/shard_map/ppermute | solution.py:125
  70.8 2.0 %collective-permute-start.20 = (f32[8,3,8,128]{3,2,1,0:T(8,128)S(1)}, f32[8,3,8,128]{3,2,1,0:T(8,128)S(1)}, u32[]{:S(2)}, u32[]{:S(2)}) collective-permute-start(f32[8,3,8,128]{3,2,1,0:T(8,128)S(1)} %add.193), channel_id=1, source_target_pairs={{0,6},{1,7},{2,4},{3,5},{4,2},{5,3},{6,0},{7,1},{8,14},{9,15},{10,... | collective-permute-start | bytes 294920 | tf_op jit(solution)/shard_map/ppermute | solution.py:125
  74.7 1.6 %collective-permute-start.24 = (f32[8,4,8,128]{3,2,1,0:T(8,128)S(1)}, f32[8,4,8,128]{3,2,1,0:T(8,128)S(1)}, u32[]{:S(2)}, u32[]{:S(2)}) collective-permute-start(f32[8,4,8,128]{3,2,1,0:T(8,128)S(1)} %dynamic-slice_add_fusion.6), channel_id=1, source_target_pairs={{0,2},{1,3},{2,0},{3,1},{4,6},{5,7},{6,4},{7,5},{8,10},{9,11},{10,... | collective-permute-start | bytes 393224 | tf_op jit(solution)/shard_map/ppermute | solution.py:125
  79.2 3.5 %collective-permute-done.4 = f32[8,4,8,128]{3,2,1,0:T(8,128)S(1)} collective-permute-done((f32[8,4,8,128]{3,2,1,0:T(8,128)S(1)}, f32[8,4,8,128]{3,2,1,0:T(8,128)S(1)}, u32[]{:S(2)}, u32[]{:S(2)}) %collective-permute-start.4) | collective-permute-done | bytes 131104 | tf_op jit(solution)/shard_map/ppermute | solution.py:125
  83.8 1.3 %collective-permute-start.5 = (f32[8,4,8,128]{3,2,1,0:T(8,128)S(1)}, f32[8,4,8,128]{3,2,1,0:T(8,128)S(1)}, u32[]{:S(2)}, u32[]{:S(2)}) collective-permute-start(f32[8,4,8,128]{3,2,1,0:T(8,128)S(1)} %add.171), channel_id=1, source_target_pairs={{0,6},{1,7},{2,4},{3,5},{4,2},{5,3},{6,0},{7,1},{8,14},{9,15},{10,... | collective-permute-start | bytes 393224 | tf_op jit(solution)/shard_map/ppermute | solution.py:125
  85.2 2.1 %collective-permute-start.11 = (f32[8,6,8,128]{3,2,1,0:T(8,128)S(1)}, f32[8,6,8,128]{3,2,1,0:T(8,128)S(1)}, u32[]{:S(2)}, u32[]{:S(2)}) collective-permute-start(f32[8,6,8,128]{3,2,1,0:T(8,128)S(1)} %pad_maximum_fusion.2), channel_id=1, source_target_pairs={{0,6},{1,7},{2,4},{3,5},{4,2},{5,3},{6,0},{7,1},{8,14},{9,15},{10,... | collective-permute-start | bytes 589832 | tf_op jit(solution)/shard_map/ppermute | solution.py:125
  87.3 2.8 %collective-permute-done.5 = f32[8,4,8,128]{3,2,1,0:T(8,128)S(1)} collective-permute-done((f32[8,4,8,128]{3,2,1,0:T(8,128)S(1)}, f32[8,4,8,128]{3,2,1,0:T(8,128)S(1)}, u32[]{:S(2)}, u32[]{:S(2)}) %collective-permute-start.5) | collective-permute-done | bytes 131104 | tf_op jit(solution)/shard_map/ppermute | solution.py:125
  91.1 4.0 %collective-permute-done.25 = f32[8,4,8,128]{3,2,1,0:T(8,128)S(1)} collective-permute-done((f32[8,4,8,128]{3,2,1,0:T(8,128)S(1)}, f32[8,4,8,128]{3,2,1,0:T(8,128)S(1)}, u32[]{:S(2)}, u32[]{:S(2)}) %collective-permute-start.25) | collective-permute-done | bytes 131104 | tf_op jit(solution)/shard_map/ppermute | solution.py:125
  95.1 6.3 %collective-permute-done.6 = f32[8,8,8,128]{3,2,1,0:T(8,128)S(1)} collective-permute-done((f32[8,8,8,128]{3,2,1,0:T(8,128)S(1)}, f32[8,8,8,128]{3,2,1,0:T(8,128)S(1)}, u32[]{:S(2)}, u32[]{:S(2)}) %collective-permute-start.6) | collective-permute-done | bytes 262176 | tf_op jit(solution)/shard_map/ppermute | solution.py:125
  101.4 1.3 %collective-permute-start.26 = (f32[8,8,8,128]{3,2,1,0:T(8,128)S(1)}, f32[8,8,8,128]{3,2,1,0:T(8,128)S(1)}, u32[]{:S(2)}, u32[]{:S(2)}) collective-permute-start(f32[8,8,8,128]{3,2,1,0:T(8,128)S(1)} %pad_maximum_fusion.1), channel_id=1, source_target_pairs={{0,6},{1,7},{2,4},{3,5},{4,2},{5,3},{6,0},{7,1},{8,14},{9,15},{10,... | collective-permute-start | bytes 786440 | tf_op jit(solution)/shard_map/ppermute | solution.py:125
  111.9 8.8 %analysis.1 = f32[16,80,8,128]{3,2,1,0:T(8,128)} custom-call(bf16[256,256]{1,0:T(8,128)(2,1)} %pad_maximum_fusion.6.both, bf16[256,128]{1,0:T(8,128)(2,1)} %mul.172.low_part, f32[8,80,8,128]{3,2,1,0:T(8,128)} %select_dynamic-update-slice_fusion.4.history), custom_call_target="tpu_custom_call" | custom-call | tf_op jit(solution)/shard_map/analysis/pallas_call | solution.py:216
  (116 shorter events, 29.1 us)
Async XLA Ops:
  8.1 14.8 %collective-permute-start = (f32[71,8,128]{2,1,0:T(8,128)}, f32[71,8,128]{2,1,0:T(8,128)S(1)}, u32[]{:S(2)}, u32[]{:S(2)}) collective-permute-start(f32[71,8,128]{2,1,0:T(8,128)} %get-tuple-element.7), channel_id=1, source_target_pairs={{0,8},{8,16},{16,24},{24,32},{32,40},{40,48},{48,56},{56,64},{64,7... | collective-permute-start | bytes 872456 | tf_op jit(solution)/shard_map/ppermute | solution.py:177
  10.0 15.4 %collective-permute-start.1 = (f32[71,8,128]{2,1,0:T(8,128)}, f32[71,8,128]{2,1,0:T(8,128)}, u32[]{:S(2)}, u32[]{:S(2)}) collective-permute-start(f32[71,8,128]{2,1,0:T(8,128)} %get-tuple-element.8), channel_id=1, source_target_pairs={{8,0},{16,8},{24,16},{32,24},{40,32},{48,40},{56,48},{64,56},{72,6... | collective-permute-start | bytes 872456 | tf_op jit(solution)/shard_map/ppermute | solution.py:178
  43.0 7.8 %collective-permute-start.27 = (f32[8,6,8,128]{3,2,1,0:T(8,128)S(1)}, f32[8,6,8,128]{3,2,1,0:T(8,128)S(1)}, u32[]{:S(2)}, u32[]{:S(2)}) collective-permute-start(f32[8,6,8,128]{3,2,1,0:T(8,128)S(1)} %constant_dynamic-slice_fusion.1), channel_id=1, source_target_pairs={{0,1},{1,0},{2,3},{3,2},{4,5},{5,4},{6,7},{7,6},{8,9},{9,8},{10,11... | collective-permute-start | bytes 589832 | tf_op jit(solution)/shard_map/ppermute | solution.py:125
  43.2 14.5 %collective-permute-start.22 = (f32[8,8,8,128]{3,2,1,0:T(8,128)S(1)}, f32[8,8,8,128]{3,2,1,0:T(8,128)S(1)}, u32[]{:S(2)}, u32[]{:S(2)}) collective-permute-start(f32[8,8,8,128]{3,2,1,0:T(8,128)S(1)} %constant_dynamic-slice_fusion.3), channel_id=1, source_target_pairs={{0,6},{1,7},{2,4},{3,5},{4,2},{5,3},{6,0},{7,1},{8,14},{9,15},{10,... | collective-permute-start | bytes 786440 | tf_op jit(solution)/shard_map/ppermute | solution.py:125
  46.0 7.5 %collective-permute-start.17 = (f32[8,6,8,128]{3,2,1,0:T(8,128)S(1)}, f32[8,6,8,128]{3,2,1,0:T(8,128)S(1)}, u32[]{:S(2)}, u32[]{:S(2)}) collective-permute-start(f32[8,6,8,128]{3,2,1,0:T(8,128)S(1)} %constant_dynamic-slice_fusion.5), channel_id=1, source_target_pairs={{0,2},{1,3},{2,0},{3,1},{4,6},{5,7},{6,4},{7,5},{8,10},{9,11},{10,... | collective-permute-start | bytes 589832 | tf_op jit(solution)/shard_map/ppermute | solution.py:125
  46.3 8.1 %collective-permute-start.12 = (f32[8,6,8,128]{3,2,1,0:T(8,128)S(1)}, f32[8,6,8,128]{3,2,1,0:T(8,128)S(1)}, u32[]{:S(2)}, u32[]{:S(2)}) collective-permute-start(f32[8,6,8,128]{3,2,1,0:T(8,128)S(1)} %constant_dynamic-slice_fusion.7), channel_id=1, source_target_pairs={{0,1},{1,0},{2,3},{3,2},{4,5},{5,4},{6,7},{7,6},{8,9},{9,8},{10,11... | collective-permute-start | bytes 589832 | tf_op jit(solution)/shard_map/ppermute | solution.py:125
  48.4 8.8 %collective-permute-start.7 = (f32[8,6,8,128]{3,2,1,0:T(8,128)S(1)}, f32[8,6,8,128]{3,2,1,0:T(8,128)S(1)}, u32[]{:S(2)}, u32[]{:S(2)}) collective-permute-start(f32[8,6,8,128]{3,2,1,0:T(8,128)S(1)} %constant_dynamic-slice_fusion.9), channel_id=1, source_target_pairs={{0,6},{1,7},{2,4},{3,5},{4,2},{5,3},{6,0},{7,1},{8,14},{9,15},{10,... | collective-permute-start | bytes 589832 | tf_op jit(solution)/shard_map/ppermute | solution.py:125
  50.8 9.3 %collective-permute-start.2 = (f32[8,8,8,128]{3,2,1,0:T(8,128)S(1)}, f32[8,8,8,128]{3,2,1,0:T(8,128)S(1)}, u32[]{:S(2)}, u32[]{:S(2)}) collective-permute-start(f32[8,8,8,128]{3,2,1,0:T(8,128)S(1)} %constant_dynamic-slice_fusion.11), channel_id=1, source_target_pairs={{0,2},{1,3},{2,0},{3,1},{4,6},{5,7},{6,4},{7,5},{8,10},{9,11},{10,... | collective-permute-start | bytes 786440 | tf_op jit(solution)/shard_map/ppermute | solution.py:125
  53.5 8.2 %collective-permute-start.28 = (f32[8,3,8,128]{3,2,1,0:T(8,128)S(1)}, f32[8,3,8,128]{3,2,1,0:T(8,128)S(1)}, u32[]{:S(2)}, u32[]{:S(2)}) collective-permute-start(f32[8,3,8,128]{3,2,1,0:T(8,128)S(1)} %constant_dynamic-slice_fusion), channel_id=1, source_target_pairs={{0,2},{1,3},{2,0},{3,1},{4,6},{5,7},{6,4},{7,5},{8,10},{9,11},{10,... | collective-permute-start | bytes 294920 | tf_op jit(solution)/shard_map/ppermute | solution.py:125
  54.4 9.2 %collective-permute-start.18 = (f32[8,3,8,128]{3,2,1,0:T(8,128)S(1)}, f32[8,3,8,128]{3,2,1,0:T(8,128)S(1)}, u32[]{:S(2)}, u32[]{:S(2)}) collective-permute-start(f32[8,3,8,128]{3,2,1,0:T(8,128)S(1)} %constant_dynamic-slice_fusion.4), channel_id=1, source_target_pairs={{0,6},{1,7},{2,4},{3,5},{4,2},{5,3},{6,0},{7,1},{8,14},{9,15},{10,... | collective-permute-start | bytes 294920 | tf_op jit(solution)/shard_map/ppermute | solution.py:125
  57.3 7.5 %collective-permute-start.13 = (f32[8,3,8,128]{3,2,1,0:T(8,128)S(1)}, f32[8,3,8,128]{3,2,1,0:T(8,128)S(1)}, u32[]{:S(2)}, u32[]{:S(2)}) collective-permute-start(f32[8,3,8,128]{3,2,1,0:T(8,128)S(1)} %constant_dynamic-slice_fusion.6), channel_id=1, source_target_pairs={{0,2},{1,3},{2,0},{3,1},{4,6},{5,7},{6,4},{7,5},{8,10},{9,11},{10,... | collective-permute-start | bytes 294920 | tf_op jit(solution)/shard_map/ppermute | solution.py:125
  57.6 9.4 %collective-permute-start.8 = (f32[8,3,8,128]{3,2,1,0:T(8,128)S(1)}, f32[8,3,8,128]{3,2,1,0:T(8,128)S(1)}, u32[]{:S(2)}, u32[]{:S(2)}) collective-permute-start(f32[8,3,8,128]{3,2,1,0:T(8,128)S(1)} %constant_dynamic-slice_fusion.8), channel_id=1, source_target_pairs={{0,1},{1,0},{2,3},{3,2},{4,5},{5,4},{6,7},{7,6},{8,9},{9,8},{10,11... | collective-permute-start | bytes 294920 | tf_op jit(solution)/shard_map/ppermute | solution.py:125
  60.1 13.4 %collective-permute-start.23 = (f32[8,4,8,128]{3,2,1,0:T(8,128)S(1)}, f32[8,4,8,128]{3,2,1,0:T(8,128)S(1)}, u32[]{:S(2)}, u32[]{:S(2)}) collective-permute-start(f32[8,4,8,128]{3,2,1,0:T(8,128)S(1)} %constant_dynamic-slice_fusion.2), channel_id=1, source_target_pairs={{0,1},{1,0},{2,3},{3,2},{4,5},{5,4},{6,7},{7,6},{8,9},{9,8},{10,11... | collective-permute-start | bytes 393224 | tf_op jit(solution)/shard_map/ppermute | solution.py:125
  61.7 6.8 %collective-permute-start.29 = (f32[8,3,8,128]{3,2,1,0:T(8,128)S(1)}, f32[8,3,8,128]{3,2,1,0:T(8,128)S(1)}, u32[]{:S(2)}, u32[]{:S(2)}) collective-permute-start(f32[8,3,8,128]{3,2,1,0:T(8,128)S(1)} %dynamic-slice_add_fusion.8), channel_id=1, source_target_pairs={{0,6},{1,7},{2,4},{3,5},{4,2},{5,3},{6,0},{7,1},{8,14},{9,15},{10,... | collective-permute-start | bytes 294920 | tf_op jit(solution)/shard_map/ppermute | solution.py:125
  63.6 6.9 %collective-permute-start.19 = (f32[8,3,8,128]{3,2,1,0:T(8,128)S(1)}, f32[8,3,8,128]{3,2,1,0:T(8,128)S(1)}, u32[]{:S(2)}, u32[]{:S(2)}) collective-permute-start(f32[8,3,8,128]{3,2,1,0:T(8,128)S(1)} %dynamic-slice_add_fusion.9), channel_id=1, source_target_pairs={{0,1},{1,0},{2,3},{3,2},{4,5},{5,4},{6,7},{7,6},{8,9},{9,8},{10,11... | collective-permute-start | bytes 294920 | tf_op jit(solution)/shard_map/ppermute | solution.py:125
  64.8 6.0 %collective-permute-start.14 = (f32[8,3,8,128]{3,2,1,0:T(8,128)S(1)}, f32[8,3,8,128]{3,2,1,0:T(8,128)S(1)}, u32[]{:S(2)}, u32[]{:S(2)}) collective-permute-start(f32[8,3,8,128]{3,2,1,0:T(8,128)S(1)} %dynamic-slice_add_fusion.10), channel_id=1, source_target_pairs={{0,6},{1,7},{2,4},{3,5},{4,2},{5,3},{6,0},{7,1},{8,14},{9,15},{10,... | collective-permute-start | bytes 294920 | tf_op jit(solution)/shard_map/ppermute | solution.py:125
  67.0 5.8 %collective-permute-start.9 = (f32[8,3,8,128]{3,2,1,0:T(8,128)S(1)}, f32[8,3,8,128]{3,2,1,0:T(8,128)S(1)}, u32[]{:S(2)}, u32[]{:S(2)}) collective-permute-start(f32[8,3,8,128]{3,2,1,0:T(8,128)S(1)} %dynamic-slice_add_fusion.11), channel_id=1, source_target_pairs={{0,2},{1,3},{2,0},{3,1},{4,6},{5,7},{6,4},{7,5},{8,10},{9,11},{10,... | collective-permute-start | bytes 294920 | tf_op jit(solution)/shard_map/ppermute | solution.py:125
  68.5 6.2 %collective-permute-start.3 = (f32[8,4,8,128]{3,2,1,0:T(8,128)S(1)}, f32[8,4,8,128]{3,2,1,0:T(8,128)S(1)}, u32[]{:S(2)}, u32[]{:S(2)}) collective-permute-start(f32[8,4,8,128]{3,2,1,0:T(8,128)S(1)} %constant_dynamic-slice_fusion.10), channel_id=1, source_target_pairs={{0,6},{1,7},{2,4},{3,5},{4,2},{5,3},{6,0},{7,1},{8,14},{9,15},{10,... | collective-permute-start | bytes 393224 | tf_op jit(solution)/shard_map/ppermute | solution.py:125
  70.5 5.8 %collective-permute-start.30 = (f32[8,3,8,128]{3,2,1,0:T(8,128)S(1)}, f32[8,3,8,128]{3,2,1,0:T(8,128)S(1)}, u32[]{:S(2)}, u32[]{:S(2)}) collective-permute-start(f32[8,3,8,128]{3,2,1,0:T(8,128)S(1)} %add.203), channel_id=1, source_target_pairs={{0,2},{1,3},{2,0},{3,1},{4,6},{5,7},{6,4},{7,5},{8,10},{9,11},{10,... | collective-permute-start | bytes 294920 | tf_op jit(solution)/shard_map/ppermute | solution.py:125
  70.8 6.6 %collective-permute-start.20 = (f32[8,3,8,128]{3,2,1,0:T(8,128)S(1)}, f32[8,3,8,128]{3,2,1,0:T(8,128)S(1)}, u32[]{:S(2)}, u32[]{:S(2)}) collective-permute-start(f32[8,3,8,128]{3,2,1,0:T(8,128)S(1)} %add.193), channel_id=1, source_target_pairs={{0,6},{1,7},{2,4},{3,5},{4,2},{5,3},{6,0},{7,1},{8,14},{9,15},{10,... | collective-permute-start | bytes 294920 | tf_op jit(solution)/shard_map/ppermute | solution.py:125
  72.8 5.8 %collective-permute-start.15 = (f32[8,3,8,128]{3,2,1,0:T(8,128)S(1)}, f32[8,3,8,128]{3,2,1,0:T(8,128)S(1)}, u32[]{:S(2)}, u32[]{:S(2)}) collective-permute-start(f32[8,3,8,128]{3,2,1,0:T(8,128)S(1)} %add.186), channel_id=1, source_target_pairs={{0,2},{1,3},{2,0},{3,1},{4,6},{5,7},{6,4},{7,5},{8,10},{9,11},{10,... | collective-permute-start | bytes 294920 | tf_op jit(solution)/shard_map/ppermute | solution.py:125
  73.5 10.3 %collective-permute-start.10 = (f32[8,3,8,128]{3,2,1,0:T(8,128)S(1)}, f32[8,3,8,128]{3,2,1,0:T(8,128)S(1)}, u32[]{:S(2)}, u32[]{:S(2)}) collective-permute-start(f32[8,3,8,128]{3,2,1,0:T(8,128)S(1)} %add.179), channel_id=1, source_target_pairs={{0,1},{1,0},{2,3},{3,2},{4,5},{5,4},{6,7},{7,6},{8,9},{9,8},{10,11... | collective-permute-start | bytes 294920 | tf_op jit(solution)/shard_map/ppermute | solution.py:125
  74.7 10.5 %collective-permute-start.24 = (f32[8,4,8,128]{3,2,1,0:T(8,128)S(1)}, f32[8,4,8,128]{3,2,1,0:T(8,128)S(1)}, u32[]{:S(2)}, u32[]{:S(2)}) collective-permute-start(f32[8,4,8,128]{3,2,1,0:T(8,128)S(1)} %dynamic-slice_add_fusion.6), channel_id=1, source_target_pairs={{0,2},{1,3},{2,0},{3,1},{4,6},{5,7},{6,4},{7,5},{8,10},{9,11},{10,... | collective-permute-start | bytes 393224 | tf_op jit(solution)/shard_map/ppermute | solution.py:125
  76.3 6.4 %collective-permute-start.4 = (f32[8,4,8,128]{3,2,1,0:T(8,128)S(1)}, f32[8,4,8,128]{3,2,1,0:T(8,128)S(1)}, u32[]{:S(2)}, u32[]{:S(2)}) collective-permute-start(f32[8,4,8,128]{3,2,1,0:T(8,128)S(1)} %dynamic-slice_add_fusion.7), channel_id=1, source_target_pairs={{0,1},{1,0},{2,3},{3,2},{4,5},{5,4},{6,7},{7,6},{8,9},{9,8},{10,11... | collective-permute-start | bytes 393224 | tf_op jit(solution)/shard_map/ppermute | solution.py:125
  77.4 33.1 %collective-permute-start.31 = (f32[8,6,8,128]{3,2,1,0:T(8,128)S(1)}, f32[8,6,8,128]{3,2,1,0:T(8,128)S(1)}, u32[]{:S(2)}, u32[]{:S(2)}) collective-permute-start(f32[8,6,8,128]{3,2,1,0:T(8,128)S(1)} %pad_maximum_fusion.5), channel_id=1, source_target_pairs={{0,1},{1,0},{2,3},{3,2},{4,5},{5,4},{6,7},{7,6},{8,9},{9,8},{10,11... | collective-permute-start | bytes 589832 | tf_op jit(solution)/shard_map/ppermute | solution.py:125
  78.6 28.4 %collective-permute-start.21 = (f32[8,6,8,128]{3,2,1,0:T(8,128)S(1)}, f32[8,6,8,128]{3,2,1,0:T(8,128)S(1)}, u32[]{:S(2)}, u32[]{:S(2)}) collective-permute-start(f32[8,6,8,128]{3,2,1,0:T(8,128)S(1)} %pad_maximum_fusion.4), channel_id=1, source_target_pairs={{0,2},{1,3},{2,0},{3,1},{4,6},{5,7},{6,4},{7,5},{8,10},{9,11},{10,... | collective-permute-start | bytes 589832 | tf_op jit(solution)/shard_map/ppermute | solution.py:125
  82.7 22.9 %collective-permute-start.16 = (f32[8,6,8,128]{3,2,1,0:T(8,128)S(1)}, f32[8,6,8,128]{3,2,1,0:T(8,128)S(1)}, u32[]{:S(2)}, u32[]{:S(2)}) collective-permute-start(f32[8,6,8,128]{3,2,1,0:T(8,128)S(1)} %pad_maximum_fusion.3), channel_id=1, source_target_pairs={{0,1},{1,0},{2,3},{3,2},{4,5},{5,4},{6,7},{7,6},{8,9},{9,8},{10,11... | collective-permute-start | bytes 589832 | tf_op jit(solution)/shard_map/ppermute | solution.py:125
  83.8 6.3 %collective-permute-start.5 = (f32[8,4,8,128]{3,2,1,0:T(8,128)S(1)}, f32[8,4,8,128]{3,2,1,0:T(8,128)S(1)}, u32[]{:S(2)}, u32[]{:S(2)}) collective-permute-start(f32[8,4,8,128]{3,2,1,0:T(8,128)S(1)} %add.171), channel_id=1, source_target_pairs={{0,6},{1,7},{2,4},{3,5},{4,2},{5,3},{6,0},{7,1},{8,14},{9,15},{10,... | collective-permute-start | bytes 393224 | tf_op jit(solution)/shard_map/ppermute | solution.py:125
  85.2 19.0 %collective-permute-start.11 = (f32[8,6,8,128]{3,2,1,0:T(8,128)S(1)}, f32[8,6,8,128]{3,2,1,0:T(8,128)S(1)}, u32[]{:S(2)}, u32[]{:S(2)}) collective-permute-start(f32[8,6,8,128]{3,2,1,0:T(8,128)S(1)} %pad_maximum_fusion.2), channel_id=1, source_target_pairs={{0,6},{1,7},{2,4},{3,5},{4,2},{5,3},{6,0},{7,1},{8,14},{9,15},{10,... | collective-permute-start | bytes 589832 | tf_op jit(solution)/shard_map/ppermute | solution.py:125
  90.1 5.0 %collective-permute-start.25 = (f32[8,4,8,128]{3,2,1,0:T(8,128)S(1)}, f32[8,4,8,128]{3,2,1,0:T(8,128)S(1)}, u32[]{:S(2)}, u32[]{:S(2)}) collective-permute-start(f32[8,4,8,128]{3,2,1,0:T(8,128)S(1)} %add.200), channel_id=1, source_target_pairs={{0,1},{1,0},{2,3},{3,2},{4,5},{5,4},{6,7},{7,6},{8,9},{9,8},{10,11... | collective-permute-start | bytes 393224 | tf_op jit(solution)/shard_map/ppermute | solution.py:125
  95.0 6.4 %collective-permute-start.6 = (f32[8,8,8,128]{3,2,1,0:T(8,128)S(1)}, f32[8,8,8,128]{3,2,1,0:T(8,128)S(1)}, u32[]{:S(2)}, u32[]{:S(2)}) collective-permute-start(f32[8,8,8,128]{3,2,1,0:T(8,128)S(1)} %pad_maximum_fusion), channel_id=1, source_target_pairs={{0,2},{1,3},{2,0},{3,1},{4,6},{5,7},{6,4},{7,5},{8,10},{9,11},{10,... | collective-permute-start | bytes 786440 | tf_op jit(solution)/shard_map/ppermute | solution.py:125
  101.4 7.6 %collective-permute-start.26 = (f32[8,8,8,128]{3,2,1,0:T(8,128)S(1)}, f32[8,8,8,128]{3,2,1,0:T(8,128)S(1)}, u32[]{:S(2)}, u32[]{:S(2)}) collective-permute-start(f32[8,8,8,128]{3,2,1,0:T(8,128)S(1)} %pad_maximum_fusion.1), channel_id=1, source_target_pairs={{0,6},{1,7},{2,4},{3,5},{4,2},{5,3},{6,0},{7,1},{8,14},{9,15},{10,... | collective-permute-start | bytes 786440 | tf_op jit(solution)/shard_map/ppermute | solution.py:125
  (3 other events, 6.6 us)

commit v2 on v0

v2 whole, which is shorter than its diff:
```python
import functools
import math

import jax
import jax.numpy as jnp
from jax import lax
from jax.experimental import pallas as pl
from jax.experimental.pallas import tpu as pltpu
from jax.sharding import PartitionSpec as P

F = 64
STEPS = 8
K = 2
FIELDS = 5
BLOCK = 16
BLOCKS = 4
LOADS = (3, 2)
TILE = 8
LANES = 128
TIME_STEP = 0.4
FOLD = 0.2
EDGES = STEPS - 1
PACKED = (EDGES + 1) // 2
UNITS_PER_K = FIELDS * PACKED
EDGE_UNITS = K * UNITS_PER_K + 1
X_PAIR, X_CROSS, Z_PAIR = 2, 6, 1
SMALL = pltpu.CompilerParams(vmem_limit_bytes=12 * 2**20)


def flipped(tile, lanes):
    return jnp.take_along_axis(tile, lanes, axis=1, mode="promise_in_bounds")


def lane_order(flag, rows):
    lane = lax.broadcasted_iota(jnp.int32, (rows, LANES), 1)
    return jnp.where(flag == 1, LANES - 1 - lane, lane)


def front_kernel(
    k, masks, order_hbm, flips_hbm, small, hat_hbm, speed_hbm, *rest
):
    low_in = high_in = None
    if k:
        low_in, high_in, _ = rest[:3]
        rest = rest[3:]
    keep, send, ends, low, high, speed, table_out, meta, token = rest[:9]
    order, flips, hat, forcing, stored_speed, sems = rest[9:]
    copies = [
        pltpu.make_async_copy(order_hbm, order, sems.at[0]),
        pltpu.make_async_copy(flips_hbm, flips, sems.at[1]),
        pltpu.make_async_copy(speed_hbm, stored_speed, sems.at[2]),
    ]
    loads, done = [], 0
    for i, fields in enumerate(LOADS):
        there = hat_hbm.at[:, k, pl.ds(done, fields)]
        loads.append(pltpu.make_async_copy(there, hat.at[:, pl.ds(done, fields)], sems.at[3 + i]))
        done += fields
    for copy in copies + loads:
        copy.start()
    token[...] = jnp.zeros_like(token)
    table = spread_synthesis(small[: 2 * TILE])
    if k:
        low[: k * UNITS_PER_K] = low_in[: k * UNITS_PER_K]
        high[: k * UNITS_PER_K] = high_in[: k * UNITS_PER_K]
        table_out[...] = spread_analysis(small[2 * TILE : 4 * TILE], small[4 * TILE :])
    for copy in copies:
        copy.wait()
    flags = [flips[order[p]] for p in range(BLOCKS)]
    lanes = [lane_order(flags[p], STEPS * BLOCK) for p in range(BLOCKS)]
    at = [pl.ds(pl.multiple_of(order[p] * BLOCK, BLOCK), BLOCK) for p in range(BLOCKS)]
    for p in range(BLOCKS):
        speed[p * BLOCK : (p + 1) * BLOCK, :] = flipped(stored_speed[at[p], :], lanes[p][:BLOCK])
    if k:
        low[EDGE_UNITS - 1] = speed[:TILE, :]
        high[EDGE_UNITS - 1] = speed[BLOCKS * BLOCK - TILE :, :]
        line = lax.broadcasted_iota(jnp.int32, (TILE, LANES), 0)
        value = jnp.zeros((TILE, LANES), jnp.int32)
        for t in range(2 * BLOCKS):
            here = line == t
            value = jnp.where(here, jnp.full((TILE, LANES), order[t // 2] * 4 + t % 2 * 2 + flags[t // 2]), value)
        meta[...] = value
    row = lax.broadcasted_iota(jnp.int32, (TILE, LANES), 0)
    done = 0
    for i, fields in enumerate(LOADS):
        loads[i].wait()
        for v in range(done, done + fields):
            for p in range(0, BLOCKS, 2):
                pair = [hat[:, v, at[p + i], :].reshape(-1, LANES) for i in range(2)]
                both = jnp.dot(table, jnp.concatenate(pair, axis=1), preferred_element_type=jnp.float32)
                for i in range(2):
                    y = flipped(both[:, i * LANES : (i + 1) * LANES], lanes[p + i]).reshape(STEPS, BLOCK, LANES)
                    forcing[:, v, (p + i) * BLOCK : (p + i + 1) * BLOCK, :] = y
                    unit = k * UNITS_PER_K + v * PACKED
                    if p + i == 0:
                        ends[:, v, :BLOCK, :] = y
                        for s in range(PACKED):
                            late = pltpu.roll(y[EDGES - 1 - s, :TILE], EDGES - s, 0)
                            low[unit + s] = jnp.where(row < EDGES - s, y[s, :TILE], late)
                    if p + i == BLOCKS - 1:
                        ends[:, v, BLOCK:, :] = y
                        for s in range(PACKED):
                            late = pltpu.roll(y[EDGES - 1 - s, TILE:], s + 1, 0)
                            high[unit + s] = jnp.where(row > s, y[s, TILE:], late)
        done += fields

    rows = BLOCKS * BLOCK
    half = rows // 2 - TILE
    upper = jnp.full((half, LANES), bit_at(masks)) == 1

    def emit(s, state):
        for v in range(FIELDS):
            first, second = state[v][TILE : TILE + half], state[v][TILE + half : TILE + 2 * half]
            keep[s, v] = jnp.where(upper, second, first)
            send[s, v] = jnp.where(upper, first, second)

    march(rows, speed[...], lambda s, v: forcing[s, v], None, emit)


def one_hot(shape, rows_are, columns_are):
    row = lax.broadcasted_iota(jnp.int32, shape, 0)
    column = lax.broadcasted_iota(jnp.int32, shape, 1)
    return (rows_are(row) == columns_are(column)).astype(jnp.float32).astype(jnp.bfloat16)


def matmul(a, b):
    return jnp.dot(a, b, preferred_element_type=jnp.float32)


def widened(small, tall, wide, unit):
    rows = one_hot((tall, small.shape[0]), lambda r: r // unit, lambda c: c)
    columns = one_hot((small.shape[1], wide), lambda r: r, lambda c: c // unit)
    whole = matmul(matmul(rows, small).astype(jnp.bfloat16), columns)
    row = lax.broadcasted_iota(jnp.int32, (tall, wide), 0)
    column = lax.broadcasted_iota(jnp.int32, (tall, wide), 1)
    return jnp.where(row % unit == column % unit, whole, 0.0).astype(jnp.bfloat16)


def spread_synthesis(small):
    return widened(small, STEPS * BLOCK, BLOCK * BLOCK, BLOCK)


def spread_analysis(high, low):
    high, low = (widened(part, BLOCK * TILE, STEPS * TILE, TILE).astype(jnp.float32) for part in (high, low))
    return jnp.concatenate([high, high, low], axis=1).astype(jnp.bfloat16)


def march(rows, speed, forcing_at, keep, emit):
    with_up, with_down = 1.0 - speed, 1.0 + speed
    lane = lax.broadcasted_iota(jnp.int32, (rows, LANES), 1)
    first_lane, last_lane = lane == 0, lane == LANES - 1
    state = None
    for s in range(STEPS):
        fresh = [TIME_STEP * forcing_at(s, v) for v in range(FIELDS)]
        if s == 0:
            state = fresh
        else:
            up = [pltpu.roll(a, rows - 1, 0) for a in state]
            down = [pltpu.roll(a, 1, 0) for a in state]
            right = [jnp.where(last_lane, 0.0, pltpu.roll(a, LANES - 1, 1)) for a in state]
            left = [jnp.where(first_lane, 0.0, pltpu.roll(a, 1, 1)) for a in state]
            div = (up[1] - down[1]) + (right[2] - left[2])
            extra = [div, up[3] - down[3], right[3] - left[3], div, None]
            new = []
            for v in range(FIELDS):
                total = state[v] + left[v] + right[v] + with_up * up[v] + with_down * down[v]
                if extra[v] is not None:
                    total = total - extra[v]
                total = FOLD * total + fresh[v]
                new.append(total if keep is None else total * keep)
            state = new
        emit(s, state)


def bit_at(masks):
    freq = lax.axis_index("freq")
    x_at = freq // 2
    bit_of = {X_PAIR: (x_at + x_at // 2) % 2, X_CROSS: x_at // 2, Z_PAIR: freq % 2}
    return jnp.where(lax.axis_index("blk") % 2 == 0, bit_of[masks[0]], bit_of[masks[1]])


def edge_kernel(masks, ends0, ends1, speed, below, above, _, keep, send, token):
    token[...] = jnp.zeros_like(token)
    inner = speed.shape[0]
    row = lax.broadcasted_iota(jnp.int32, (6 * TILE, LANES), 0)
    upper = jnp.full((TILE, LANES), bit_at(masks)) == 1
    here = lax.axis_index("blk")
    has_below = (here > 0).astype(jnp.float32)
    has_above = (here < lax.axis_size("blk") - 1).astype(jnp.float32)
    inside = jnp.where(row < TILE, has_below, jnp.where(row >= 5 * TILE, has_above, 1.0))

    def windows(lo, body, hi):
        return jnp.concatenate([lo, body, hi], axis=0)

    last = EDGE_UNITS - 1
    near_ends = jnp.concatenate([speed[: 2 * TILE, :], speed[inner - 2 * TILE :, :]], axis=0)
    speeds = windows(below[last], near_ends, above[last])
    for k, ends in enumerate((ends0, ends1)):

        def forcing_at(s, v):
            unit = k * UNITS_PER_K + v * PACKED
            if s == EDGES:
                lo = hi = jnp.zeros((TILE, LANES), jnp.float32)
            elif s < PACKED:
                lo, hi = below[unit + s], above[unit + s]
            else:
                early = EDGES - 1 - s
                lo = pltpu.roll(below[unit + early], TILE - 1 - early, 0)
                hi = pltpu.roll(above[unit + early], early + 1, 0)
            return windows(lo, ends[s, v], hi)

        def emit(s, state):
            for v in range(FIELDS):
                first, second = state[v][TILE : 2 * TILE], state[v][4 * TILE : 5 * TILE]
                keep[s, k * FIELDS + v] = jnp.where(upper, second, first)
                send[s, k * FIELDS + v] = jnp.where(upper, first, second)

        march(6 * TILE, speeds, forcing_at, inside, emit)


def bit_at(masks):
    freq = lax.axis_index("freq")
    x_at = freq // 2
    bit_of = {X_PAIR: (x_at + x_at // 2) % 2, X_CROSS: x_at // 2, Z_PAIR: freq % 2}
    return jnp.where(lax.axis_index("blk") % 2 == 0, bit_of[masks[0]], bit_of[masks[1]])


def fold_kernel(masks, mine, arrived, _, keep, send, token):
    token[...] = jnp.zeros_like(token)
    half = keep.shape[0]
    upper = jnp.full(mine.shape[2:], bit_at(masks)) == 1
    for s in range(half):
        for u in range(mine.shape[1]):
            first = mine[s, u] + arrived[s, u]
            second = mine[half + s, u] + arrived[half + s, u]
            keep[s, u] = jnp.where(upper, second, first)
            send[s, u] = jnp.where(upper, first, second)


def add_kernel(mine, arrived, _, total, token):
    token[...] = jnp.zeros_like(token)
    total[...] = mine[...] + arrived[...]


def join_kernel(masks, mine, arrived, _, whole, token):
    token[...] = jnp.zeros_like(token)
    half = mine.shape[0]
    upper = jnp.full(mine.shape[2:], bit_at(masks)) == 1
    for s in range(half):
        for u in range(mine.shape[1]):
            whole[s, u] = jnp.where(upper, arrived[s, u], mine[s, u])
            whole[half + s, u] = jnp.where(upper, mine[s, u], arrived[s, u])


def analysis_kernel(first_tile, first_unit, meta, table, history, _, *rest):
    out, token, buffer, sems = rest[-4:]
    token[...] = jnp.zeros_like(token)
    units, tiles = history.shape[1], history.shape[2] // TILE
    first = first_tile()
    copies = []
    for i in range(tiles):
        stored = meta[pl.ds(first + i, 1), 0:1][0, 0]
        tile = stored // 2
        lanes = lane_order(stored % 2, STEPS * TILE)
        for start in range(0, units, FIELDS):
            for u in range(start, start + FIELDS, 2):
                pair = []
                for j in range(u, min(u + 2, start + FIELDS)):
                    x = flipped(history[:, j, i * TILE : (i + 1) * TILE, :].reshape(STEPS * TILE, LANES), lanes)
                    hi = x.astype(jnp.bfloat16)
                    lo = (x - hi.astype(jnp.float32)).astype(jnp.bfloat16)
                    pair.append(jnp.concatenate([hi, lo, hi], axis=0))
                y = jnp.dot(table[...], jnp.concatenate(pair, axis=1), preferred_element_type=jnp.float32)
                for j in range(len(pair)):
                    part = y[:, j * LANES : (j + 1) * LANES].reshape(buffer.shape[1], TILE, LANES)
                    buffer[i, :, u + j] = part
            copy = pltpu.make_async_copy(
                buffer.at[i, :, pl.ds(start, FIELDS)],
                out.at[:, pl.ds(first_unit + start, FIELDS), tile],
                sems.at[len(copies)],
            )
            copy.start()
            copies.append(copy)
    for copy in copies:
        copy.wait()


def small_tables(freq, freq_local):
    shape = (BLOCK, LANES)
    row = lax.broadcasted_iota(jnp.int32, shape, 0)
    column = lax.broadcasted_iota(jnp.int32, shape, 1)

    def entries(cm, times, scale, valid):
        angular = ((freq * freq_local + cm % freq_local).astype(jnp.float32) + 1.0) * (math.pi / F)
        phase = times.astype(jnp.float32) * angular
        value = jnp.where(cm < freq_local, jnp.cos(phase), -jnp.sin(phase)) / math.sqrt(scale)
        return jnp.where(valid, value, 0.0)

    synthesis = entries(column, row, F, (row < STEPS) & (column < 2 * freq_local))
    analysis = entries(row, column + 1, STEPS, column < STEPS)
    high = lax.reduce_precision(analysis, 8, 7)
    return jnp.concatenate([synthesis, high, analysis - high], axis=0).astype(jnp.bfloat16)


def swap(x, masks):
    blocks, freqs = lax.axis_size("blk"), lax.axis_size("freq")
    pairs = [(b * freqs + f, b * freqs + (f ^ masks[b % 2])) for b in range(blocks) for f in range(freqs)]
    return lax.ppermute(x, ("blk", "freq"), pairs)


def vmem():
    return pl.BlockSpec(memory_space=pltpu.VMEM)


def near(x):
    return pltpu.with_memory_space_constraint(x, pltpu.VMEM)


def far(x):
    return pltpu.with_memory_space_constraint(x, pltpu.HBM)


def local(forcing_hat, mean_speed, block_order, block_flips):
    freq_local = forcing_hat.shape[1]
    rows = mean_speed.shape[0]
    freq = lax.axis_index("freq")
    cm = 2 * freq_local

    masks_of = (
        ((X_PAIR, Z_PAIR), (X_CROSS, X_PAIR), (Z_PAIR, X_CROSS)),
        ((X_PAIR, Z_PAIR), (X_CROSS, X_PAIR), (Z_PAIR, X_CROSS)),
        ((X_CROSS, X_CROSS), (Z_PAIR, Z_PAIR), (X_PAIR, X_PAIR)),
    )
    half = rows // 2 - TILE
    hbm = pl.BlockSpec(memory_space=pltpu.HBM)
    token_shape = pltpu.VMEM((TILE, LANES), jnp.float32)
    edge_shape = pltpu.VMEM((EDGE_UNITS, TILE, LANES), jnp.float32)

    def call(kernel, name, shapes, *args, token=None):
        extra = [] if token is None else [token]
        return pl.pallas_call(
            kernel,
            out_shape=list(shapes) + [token_shape],
            in_specs=[vmem()] * len(args) + [pl.BlockSpec(memory_space=pl.ANY)] * len(extra),
            out_specs=[vmem()] * (len(shapes) + 1),
            compiler_params=SMALL,
            name=name,
        )(*[near(x) for x in args], *extra)

    small = small_tables(freq, freq_local)
    hat = forcing_hat.reshape(cm, K, FIELDS, rows, LANES)
    part_shape = pltpu.VMEM((STEPS, FIELDS, half, LANES), jnp.float32)
    keep, send, ends, arrived = [None] * 3, [None] * 3, [None] * K, [None] * 3
    low = high = token = None
    for k in range(K):
        extra = [near(low), near(high), token] if k else []
        keep[k], send[k], ends[k], low, high, speed, table, meta, token = pl.pallas_call(
            functools.partial(front_kernel, k, masks_of[k][0]),
            out_shape=[
                part_shape,
                part_shape,
                pltpu.VMEM((STEPS, FIELDS, 2 * BLOCK, LANES), jnp.float32),
                edge_shape,
                edge_shape,
                pltpu.VMEM((rows, LANES), jnp.float32),
                pltpu.VMEM((BLOCK * TILE, 3 * STEPS * TILE), jnp.bfloat16),
                pltpu.VMEM((TILE, LANES), jnp.int32),
                token_shape,
            ],
            in_specs=[hbm, hbm, vmem(), hbm, hbm]
            + [vmem(), vmem(), pl.BlockSpec(memory_space=pl.ANY)][: len(extra)],
            out_specs=[vmem()] * 9,
            scratch_shapes=[
                pltpu.SMEM((BLOCKS,), jnp.int32),
                pltpu.SMEM((BLOCKS,), jnp.int32),
                pltpu.VMEM((cm, FIELDS, rows, LANES), jnp.bfloat16),
                pltpu.VMEM((STEPS, FIELDS, rows, LANES), jnp.float32),
                pltpu.VMEM((rows, LANES), jnp.float32),
                pltpu.SemaphoreType.DMA((3 + len(LOADS),)),
            ],
            compiler_params=SMALL,
            name=f"front{k}",
        )(far(block_order), far(block_flips), near(small), far(hat), far(mean_speed), *extra)
        arrived[k] = swap(send[k], masks_of[k][0])

    peers = lax.axis_size("blk")
    below = lax.ppermute(high, "blk", [(i, i + 1) for i in range(peers - 1)])
    above = lax.ppermute(low, "blk", [(i + 1, i) for i in range(peers - 1)])

    def edges():
        nonlocal token
        kernel = functools.partial(edge_kernel, masks_of[2][0])
        shape = pltpu.VMEM((STEPS, K * FIELDS, TILE, LANES), jnp.float32)
        args = (*ends, speed, below, above)
        keep[2], send[2], token = call(kernel, "edges", [shape] * 2, *args, token=token)
        arrived[2] = swap(send[2], masks_of[2][0])

    whole = [None] * 3
    other = [None] * 3

    def fold(i):
        nonlocal token
        x = keep[i]
        shape = pltpu.VMEM((x.shape[0] // 2,) + x.shape[1:], x.dtype)
        kernel = functools.partial(fold_kernel, masks_of[i][1])
        keep[i], send[i], token = call(kernel, f"fold{i}", [shape] * 2, x, arrived[i], token=token)
        arrived[i] = swap(send[i], masks_of[i][1])

    def add(i, masks):
        nonlocal token
        x = keep[i]
        keep[i], token = call(add_kernel, f"add{i}", [pltpu.VMEM(x.shape, x.dtype)], x, arrived[i], token=token)
        arrived[i] = swap(keep[i], masks)

    def join(i):
        nonlocal token
        x = keep[i]
        shape = pltpu.VMEM((x.shape[0] * 2,) + x.shape[1:], x.dtype)
        kernel = functools.partial(join_kernel, masks_of[i][1])
        whole[i], token = call(kernel, f"join{i}", [shape], x, arrived[i], token=token)
        other[i] = swap(whole[i], masks_of[i][0])

    out = None
    total_tiles = rows // TILE

    def analyse(i, x, is_other):
        nonlocal out, token
        units, tiles = x.shape[1], x.shape[2] // TILE
        extra = [] if out is None else [out]

        def first_tile():
            bit = bit_at(masks_of[i][0])
            bit = 1 - bit if is_other else bit
            return 1 + bit * (half // TILE) if i < K else bit * (total_tiles - 1)

        out, token = pl.pallas_call(
            functools.partial(analysis_kernel, first_tile, i * FIELDS if i < K else 0),
            out_shape=[
                jax.ShapeDtypeStruct((cm, K * FIELDS, total_tiles, TILE, LANES), jnp.float32),
                token_shape,
            ],
            in_specs=[vmem()] * 3 + [pl.BlockSpec(memory_space=pl.ANY)] + [hbm] * len(extra),
            out_specs=[hbm, vmem()],
            scratch_shapes=[
                pltpu.VMEM((tiles, cm, units, TILE, LANES), jnp.float32),
                pltpu.SemaphoreType.DMA((tiles * units // FIELDS,)),
            ],
            input_output_aliases={4: 0} if extra else {},
            compiler_params=SMALL,
            name=f"analysis{i}",
        )(near(meta), near(table), near(x), token, *extra)

    fold(0)
    edges()
    fold(1)
    add(0, masks_of[0][2])
    add(1, masks_of[1][2])
    fold(2)
    add(0, masks_of[0][1])
    add(1, masks_of[1][1])
    add(2, masks_of[2][2])
    join(0)
    join(1)
    add(2, masks_of[2][1])
    analyse(0, whole[0], False)
    join(2)
    analyse(1, whole[1], False)
    analyse(0, other[0], True)
    analyse(2, whole[2], False)
    analyse(1, other[1], True)
    analyse(2, other[2], True)
    return out.reshape(2, freq_local, K, FIELDS, rows, LANES)


def solution(mesh):
    placed = (P(None, "freq", None, None, "blk", None), P("blk", None), P("blk"), P("blk"))
    return jax.shard_map(
        local,
        mesh=mesh,
        in_specs=placed,
        out_specs=P(None, "freq", None, None, "blk", None),
        check_vma=False,
    )
```

time: 270 us -> 75.6 us (0.28)
  waiting for transfers between devices: 160 us -> 27.9 us
  local copies, waits for them, and re-layouts: 29.5 us -> 0 us
  Pallas kernels: 0 us -> 19.9 us
  other arithmetic: 15.8 us -> 0.19 us
  starting transfers between devices: 42.6 us -> 27 us
  between operations: 14.2 us -> 0.43 us
  matrix products: 7.08 us -> 0 us
    psum x1 -> x0, waiting for transfers between devices: 126 us -> none  [local(): forcing = lax.psum(partial_sum, 'freq')]
    pallas_call x0 -> x21, Pallas kernels: none -> 19.9 us  [the longest x6 10.6 us: analyse(): pl.pallas_call(functools.partial(analysis_kernel, first_tile, i * FIELDS...]
    ppermute x16 -> x17, starting transfers between devices: 42.6 us -> 27 us  [the longest x15 17.8 us: swap(): return lax.ppermute(x, ('blk', 'freq'), pairs)]
    rev x3 -> x0, local copies, waits for them, and re-layouts: 10.5 us -> none  [flip_blocks(): blocked[..., ::-1]]
    select_n x7 -> x0, other arithmetic: 8.01 us -> none  [the longest x2 4.27 us: flip_blocks(): jnp.where((flip_flags == 1)[:, None, None], blocked[..., ::-1], blocked)]
    dot_general x2 -> x0, matrix products: 7.08 us -> none  [the longest x1 5.51 us: local(): jnp.einsum('cms,ksvrj->cmkvrj', analysis, history, precision=lax.Precisio...]
    gather x4 -> x0, local copies, waits for them, and re-layouts: 6.15 us -> none  [the longest x2 3.03 us: to_chain(): placed = jnp.take(blocked, chain_ids, axis=-3)]
    unnamed x17 -> x0, local copies, waits for them, and re-layouts: 5.94 us -> none
  transfers between devices with their start and end apart: 17 -> 17, of which waited for: 8 -> 8; matrix products, arithmetic and copies ran while one was open for 4% -> 0% of each run, Pallas kernels for 0% -> 19%
where the time goes in v2:
time: 75.6 us; the launch traced here: 75.4 us
  waiting for transfers between devices  27.9 us (37%)
  starting transfers between devices  27 us (36%)
  Pallas kernels  19.9 us (26%)
    ppermute x15, waiting for transfers between devices, swap(): return lax.ppermute(x, ('blk', 'freq'), pairs)  23.5 us
    ppermute x15, starting transfers between devices, swap(): return lax.ppermute(x, ('blk', 'freq'), pairs)  17.8 us
    pallas_call x6, Pallas kernels, analyse(): pl.pallas_call(functools.partial(analysis_kernel, first_tile, i * FIELDS...  10.6 us
    ppermute x1, starting transfers between devices, local(): above = lax.ppermute(low, 'blk', [(i + 1, i) for i in range(peers - 1)])  7.27 us
    pallas_call x2, Pallas kernels, local(): pl.pallas_call(functools.partial(front_kernel, k, masks_of[k][0]), out_sh...  7.21 us
    ppermute x1, waiting for transfers between devices, local(): below = lax.ppermute(high, 'blk', [(i, i + 1) for i in range(peers - 1)])  4.33 us
    pallas_call x13, Pallas kernels, call(): pl.pallas_call(kernel, out_shape=list(shapes) + [token_shape], in_specs=[...  2.18 us
    ppermute x1, starting transfers between devices, local(): below = lax.ppermute(high, 'blk', [(i, i + 1) for i in range(peers - 1)])  1.91 us
  transfers between devices with their start and end apart: 17, of which 8 were waited for; matrix products, arithmetic and copies ran while one was open for 0% of the time, Pallas kernels for 19%

profile of v2, /device:TPU:24, one launch (start us, length us, event | category | flops | bytes accessed | tf_op | source)
XLA Modules:
  0.0 75.4 jit_solution(3255044019923003392)
XLA Ops:
  0.1 0.2 reduce-precision_convert_fusion
  0.2 3.8 %front0.1 = (f32[8,5,24,128]{3,2,1,0:T(8,128)S(1)}, f32[8,5,24,128]{3,2,1,0:T(8,128)S(1)}, f32[8,5,32,128]{3,2,1,0:T(8,128)S(1)}, f32[41,8,128]{2,1,0:T(8,128)S(...) custom-call(s32[4]{0:T(128)} %order_hbm.3, ...), custom_call_target="tpu_custom_call" | custom-call | tf_op jit(solution)/shard_map/front0/pallas_call | solution.py:356
  4.0 1.6 %collective-permute-start.2 = (f32[8,5,24,128]{3,2,1,0:T(8,128)S(1)}, f32[8,5,24,128]{3,2,1,0:T(8,128)S(1)}, u32[]{:S(2)}, u32[]{:S(2)}) collective-permute-start(f32[8,5,24,128]{3,2,1,0:T(8,128)S(1)} %get-tuple-element.72), channel_id=1, source_target_pairs={{0,2},{1,3},{2,0},{3,1},{4,6},{5,7},{6,4},{7,5},{8,9},{9,8},{10,11... | collective-permute-start | bytes 1474568 | tf_op jit(solution)/shard_map/ppermute | solution.py:307
  5.6 3.5 %front1.1 = (f32[8,5,24,128]{3,2,1,0:T(8,128)S(1)}, f32[8,5,24,128]{3,2,1,0:T(8,128)S(1)}, f32[8,5,32,128]{3,2,1,0:T(8,128)S(1)}, f32[41,8,128]{2,1,0:T(8,128)S(...) custom-call(s32[4]{0:T(128)} %order_hbm.3, ...), custom_call_target="tpu_custom_call" | custom-call | tf_op jit(solution)/shard_map/front1/pallas_call | solution.py:356
  9.1 0.6 collective-permute-start.4
  9.7 1.9 %collective-permute-start = (f32[41,8,128]{2,1,0:T(8,128)S(1)}, f32[41,8,128]{2,1,0:T(8,128)S(1)}, u32[]{:S(2)}, u32[]{:S(2)}) collective-permute-start(f32[41,8,128]{2,1,0:T(8,128)S(1)} %get-tuple-element.69), channel_id=1, source_target_pairs={{0,8},{8,16},{16,24},{24,32},{32,40},{40,48},{48,56},{56,64},{64,7... | collective-permute-start | bytes 503816 | tf_op jit(solution)/shard_map/ppermute | solution.py:386
  11.6 7.3 %collective-permute-start.1 = (f32[41,8,128]{2,1,0:T(8,128)S(1)}, f32[41,8,128]{2,1,0:T(8,128)S(1)}, u32[]{:S(2)}, u32[]{:S(2)}) collective-permute-start(f32[41,8,128]{2,1,0:T(8,128)S(1)} %get-tuple-element.70), channel_id=1, source_target_pairs={{8,0},{16,8},{24,16},{32,24},{40,32},{48,40},{56,48},{64,56},{72,6... | collective-permute-start | bytes 503816 | tf_op jit(solution)/shard_map/ppermute | solution.py:387
  19.0 2.8 %collective-permute-start.6 = (f32[4,5,24,128]{3,2,1,0:T(8,128)S(1)}, f32[4,5,24,128]{3,2,1,0:T(8,128)S(1)}, u32[]{:S(2)}, u32[]{:S(2)}) collective-permute-start(f32[4,5,24,128]{3,2,1,0:T(8,128)S(1)} %get-tuple-element.83), channel_id=1, source_target_pairs={{0,6},{1,7},{2,4},{3,5},{4,2},{5,3},{6,0},{7,1},{8,10},{9,11},{10,... | collective-permute-start | bytes 737288 | tf_op jit(solution)/shard_map/ppermute | solution.py:307
  21.8 4.3 %collective-permute-done.below = f32[41,8,128]{2,1,0:T(8,128)S(1)} collective-permute-done((f32[41,8,128]{2,1,0:T(8,128)S(1)}, f32[41,8,128]{2,1,0:T(8,128)S(1)}, u32[]{:S(2)}, u32[]{:S(2)}) %collective-permute-start) | collective-permute-done | bytes 167968 | tf_op jit(solution)/shard_map/ppermute | solution.py:386
  26.1 1.7 %edges.1 = (f32[8,10,8,128]{3,2,1,0:T(8,128)S(1)}, f32[8,10,8,128]{3,2,1,0:T(8,128)S(1)}, f32[8,128]{1,0:T(8,128)S(1)}) custom-call(f32[8,5,32,128]{3,2,1,0:T(8,128)S(1)} %get-tuple-element.66.ends0, f32[8,5,32,128]{3,2,1,0:T(8,128)S(1)} %get-tuple-element.67.ends1, f32[64,128]{1,0:T(8,128)S(1)} %get-tuple-element.68.speed, ...), custom_call_target="tpu_custom_call" | custom-call | tf_op jit(solution)/shard_map/edges/pallas_call | solution.py:340
  27.9 2.8 %collective-permute-start.5 = (f32[4,5,24,128]{3,2,1,0:T(8,128)S(1)}, f32[4,5,24,128]{3,2,1,0:T(8,128)S(1)}, u32[]{:S(2)}, u32[]{:S(2)}) collective-permute-start(f32[4,5,24,128]{3,2,1,0:T(8,128)S(1)} %get-tuple-element.81), channel_id=1, source_target_pairs={{0,6},{1,7},{2,4},{3,5},{4,2},{5,3},{6,0},{7,1},{8,10},{9,11},{10,... | collective-permute-start | bytes 737288 | tf_op jit(solution)/shard_map/ppermute | solution.py:307
  30.8 0.5 collective-permute-start.3
  31.3 0.1 collective-permute-start.9
  31.4 6.7 %collective-permute-done.5.arrived = f32[4,5,24,128]{3,2,1,0:T(8,128)S(1)} collective-permute-done((f32[4,5,24,128]{3,2,1,0:T(8,128)S(1)}, f32[4,5,24,128]{3,2,1,0:T(8,128)S(1)}, u32[]{:S(2)}, u32[]{:S(2)}) %collective-permute-start.5) | collective-permute-done | bytes 245792 | tf_op jit(solution)/shard_map/ppermute | solution.py:307
  38.2 6.9 %collective-permute-done.3.arrived = f32[8,10,8,128]{3,2,1,0:T(8,128)S(1)} collective-permute-done((f32[8,10,8,128]{3,2,1,0:T(8,128)S(1)}, f32[8,10,8,128]{3,2,1,0:T(8,128)S(1)}, u32[]{:S(2)}, u32[]{:S(2)}) %collective-permute-start.3) | collective-permute-done | bytes 327712 | tf_op jit(solution)/shard_map/ppermute | solution.py:307
  45.3 2.9 %collective-permute-start.12 = (f32[4,5,24,128]{3,2,1,0:T(8,128)S(1)}, f32[4,5,24,128]{3,2,1,0:T(8,128)S(1)}, u32[]{:S(2)}, u32[]{:S(2)}) collective-permute-start(f32[4,5,24,128]{3,2,1,0:T(8,128)S(1)} %get-tuple-element.96.mine), channel_id=1, source_target_pairs={{0,6},{1,7},{2,4},{3,5},{4,2},{5,3},{6,0},{7,1},{8,10},{9,11},{10,... | collective-permute-start | bytes 737288 | tf_op jit(solution)/shard_map/ppermute | solution.py:307
  48.2 0.5 collective-permute-start.11
  48.7 1.8 %collective-permute-done.7.arrived = f32[4,10,8,128]{3,2,1,0:T(8,128)S(1)} collective-permute-done((f32[4,10,8,128]{3,2,1,0:T(8,128)S(1)}, f32[4,10,8,128]{3,2,1,0:T(8,128)S(1)}, u32[]{:S(2)}, u32[]{:S(2)}) %collective-permute-start.7) | collective-permute-done | bytes 163872 | tf_op jit(solution)/shard_map/ppermute | solution.py:307
  50.6 0.4 collective-permute-start.10
  51.0 1.8 %collective-permute-done.12.arrived = f32[4,5,24,128]{3,2,1,0:T(8,128)S(1)} collective-permute-done((f32[4,5,24,128]{3,2,1,0:T(8,128)S(1)}, f32[4,5,24,128]{3,2,1,0:T(8,128)S(1)}, u32[]{:S(2)}, u32[]{:S(2)}) %collective-permute-start.12) | collective-permute-done | bytes 245792 | tf_op jit(solution)/shard_map/ppermute | solution.py:307
  52.8 0.3 collective-permute-start.16
  53.1 2.6 %collective-permute-done.11.arrived = f32[4,5,24,128]{3,2,1,0:T(8,128)S(1)} collective-permute-done((f32[4,5,24,128]{3,2,1,0:T(8,128)S(1)}, f32[4,5,24,128]{3,2,1,0:T(8,128)S(1)}, u32[]{:S(2)}, u32[]{:S(2)}) %collective-permute-start.11) | collective-permute-done | bytes 245792 | tf_op jit(solution)/shard_map/ppermute | solution.py:307
  55.8 0.2 collective-permute-done.10.arrived
  56.0 1.9 %collective-permute-start.13 = (f32[4,10,8,128]{3,2,1,0:T(8,128)S(1)}, f32[4,10,8,128]{3,2,1,0:T(8,128)S(1)}, u32[]{:S(2)}, u32[]{:S(2)}) collective-permute-start(f32[4,10,8,128]{3,2,1,0:T(8,128)S(1)} %get-tuple-element.100.mine), channel_id=1, source_target_pairs={{0,1},{1,0},{2,3},{3,2},{4,5},{5,4},{6,7},{7,6},{8,9},{9,8},{10,11... | collective-permute-start | bytes 491528 | tf_op jit(solution)/shard_map/ppermute | solution.py:307
  57.9 1.8 %analysis0.2 = (f32[16,10,8,8,128]{4,3,2,1,0:T(8,128)}, f32[8,128]{1,0:T(8,128)S(1)}) custom-call(s32[8,128]{1,0:T(8,128)S(1)} %get-tuple-element.64.meta, bf16[128,192]{1,0:T(8,128)(2,1)S(1)} %get-tuple-element.65.table, f32[8,5,24,128]{3,2,1,0:T(8,128)S(1)} %get-tuple-element.101.history, f32[8,128]{1,0:T(8,128)S(1)} %get-tuple-element.102._), custom_call_target="tpu_custom_call" | custom-call | tf_op jit(solution)/shard_map/analysis0/pallas_call | solution.py:435
  59.7 3.5 %collective-permute-done.13.arrived = f32[4,10,8,128]{3,2,1,0:T(8,128)S(1)} collective-permute-done((f32[4,10,8,128]{3,2,1,0:T(8,128)S(1)}, f32[4,10,8,128]{3,2,1,0:T(8,128)S(1)}, u32[]{:S(2)}, u32[]{:S(2)}) %collective-permute-start.13) | collective-permute-done | bytes 163872 | tf_op jit(solution)/shard_map/ppermute | solution.py:307
  63.3 3.2 %collective-permute-start.14 = (f32[8,10,8,128]{3,2,1,0:T(8,128)S(1)}, f32[8,10,8,128]{3,2,1,0:T(8,128)S(1)}, u32[]{:S(2)}, u32[]{:S(2)}) collective-permute-start(f32[8,10,8,128]{3,2,1,0:T(8,128)S(1)} %get-tuple-element.104.history), channel_id=1, source_target_pairs={{0,6},{1,7},{2,4},{3,5},{4,2},{5,3},{6,0},{7,1},{8,14},{9,15},{10,... | collective-permute-start | bytes 983048 | tf_op jit(solution)/shard_map/ppermute | solution.py:307
  66.4 1.8 %analysis1.2 = (f32[16,10,8,8,128]{4,3,2,1,0:T(8,128)}, f32[8,128]{1,0:T(8,128)S(1)}) custom-call(s32[8,128]{1,0:T(8,128)S(1)} %get-tuple-element.64.meta, bf16[128,192]{1,0:T(8,128)(2,1)S(1)} %get-tuple-element.65.table, f32[8,5,24,128]{3,2,1,0:T(8,128)S(1)} %get-tuple-element.105.history, ...), custom_call_target="tpu_custom_call", output_to_operand_aliasing={{0}: (4, {})} | custom-call | tf_op jit(solution)/shard_map/analysis1/pallas_call | solution.py:435
  68.2 1.8 %analysis0.3 = (f32[16,10,8,8,128]{4,3,2,1,0:T(8,128)}, f32[8,128]{1,0:T(8,128)S(1)}) custom-call(s32[8,128]{1,0:T(8,128)S(1)} %get-tuple-element.64.meta, bf16[128,192]{1,0:T(8,128)(2,1)S(1)} %get-tuple-element.65.table, f32[8,5,24,128]{3,2,1,0:T(8,128)S(1)} %collective-permute-done.16.history, ...), custom_call_target="tpu_custom_call", output_to_operand_aliasing={{0}: (4, {})} | custom-call | tf_op jit(solution)/shard_map/analysis0/pallas_call | solution.py:435
  70.0 1.4 %analysis2.2 = (f32[16,10,8,8,128]{4,3,2,1,0:T(8,128)}, f32[8,128]{1,0:T(8,128)S(1)}) custom-call(s32[8,128]{1,0:T(8,128)S(1)} %get-tuple-element.64.meta, bf16[128,192]{1,0:T(8,128)(2,1)S(1)} %get-tuple-element.65.table, f32[8,10,8,128]{3,2,1,0:T(8,128)S(1)} %get-tuple-element.104.history, ...), custom_call_target="tpu_custom_call", output_to_operand_aliasing={{0}: (4, {})} | custom-call | tf_op jit(solution)/shard_map/analysis2/pallas_call | solution.py:435
  71.5 1.8 %analysis1.3 = (f32[16,10,8,8,128]{4,3,2,1,0:T(8,128)}, f32[8,128]{1,0:T(8,128)S(1)}) custom-call(s32[8,128]{1,0:T(8,128)S(1)} %get-tuple-element.64.meta, bf16[128,192]{1,0:T(8,128)(2,1)S(1)} %get-tuple-element.65.table, f32[8,5,24,128]{3,2,1,0:T(8,128)S(1)} %collective-permute-done.15.history, ...), custom_call_target="tpu_custom_call", output_to_operand_aliasing={{0}: (4, {})} | custom-call | tf_op jit(solution)/shard_map/analysis1/pallas_call | solution.py:435
  73.3 2.0 %analysis2.3 = (f32[16,10,8,8,128]{4,3,2,1,0:T(8,128)}, f32[8,128]{1,0:T(8,128)}) custom-call(s32[8,128]{1,0:T(8,128)S(1)} %get-tuple-element.64.meta, bf16[128,192]{1,0:T(8,128)(2,1)S(1)} %get-tuple-element.65.table, f32[8,10,8,128]{3,2,1,0:T(8,128)S(1)} %collective-permute-done.14.history, ...), custom_call_target="tpu_custom_call", output_to_operand_aliasing={{0}: (4, {})} | custom-call | tf_op jit(solution)/shard_map/analysis2/pallas_call | solution.py:435
  (32 shorter events, 0.7 us)
Async XLA Ops:
  4.0 14.9 %collective-permute-start.2 = (f32[8,5,24,128]{3,2,1,0:T(8,128)S(1)}, f32[8,5,24,128]{3,2,1,0:T(8,128)S(1)}, u32[]{:S(2)}, u32[]{:S(2)}) collective-permute-start(f32[8,5,24,128]{3,2,1,0:T(8,128)S(1)} %get-tuple-element.72), channel_id=1, source_target_pairs={{0,2},{1,3},{2,0},{3,1},{4,6},{5,7},{6,4},{7,5},{8,9},{9,8},{10,11... | collective-permute-start | bytes 1474568 | tf_op jit(solution)/shard_map/ppermute | solution.py:307
  9.1 18.8 %collective-permute-start.4 = (f32[8,5,24,128]{3,2,1,0:T(8,128)S(1)}, f32[8,5,24,128]{3,2,1,0:T(8,128)S(1)}, u32[]{:S(2)}, u32[]{:S(2)}) collective-permute-start(f32[8,5,24,128]{3,2,1,0:T(8,128)S(1)} %get-tuple-element.78), channel_id=1, source_target_pairs={{0,2},{1,3},{2,0},{3,1},{4,6},{5,7},{6,4},{7,5},{8,9},{9,8},{10,11... | collective-permute-start | bytes 1474568 | tf_op jit(solution)/shard_map/ppermute | solution.py:307
  9.7 16.5 %collective-permute-start = (f32[41,8,128]{2,1,0:T(8,128)S(1)}, f32[41,8,128]{2,1,0:T(8,128)S(1)}, u32[]{:S(2)}, u32[]{:S(2)}) collective-permute-start(f32[41,8,128]{2,1,0:T(8,128)S(1)} %get-tuple-element.69), channel_id=1, source_target_pairs={{0,8},{8,16},{16,24},{24,32},{32,40},{40,48},{48,56},{56,64},{64,7... | collective-permute-start | bytes 503816 | tf_op jit(solution)/shard_map/ppermute | solution.py:386
  11.6 14.5 %collective-permute-start.1 = (f32[41,8,128]{2,1,0:T(8,128)S(1)}, f32[41,8,128]{2,1,0:T(8,128)S(1)}, u32[]{:S(2)}, u32[]{:S(2)}) collective-permute-start(f32[41,8,128]{2,1,0:T(8,128)S(1)} %get-tuple-element.70), channel_id=1, source_target_pairs={{8,0},{16,8},{24,16},{32,24},{40,32},{48,40},{56,48},{64,56},{72,6... | collective-permute-start | bytes 503816 | tf_op jit(solution)/shard_map/ppermute | solution.py:387
  19.0 12.3 %collective-permute-start.6 = (f32[4,5,24,128]{3,2,1,0:T(8,128)S(1)}, f32[4,5,24,128]{3,2,1,0:T(8,128)S(1)}, u32[]{:S(2)}, u32[]{:S(2)}) collective-permute-start(f32[4,5,24,128]{3,2,1,0:T(8,128)S(1)} %get-tuple-element.83), channel_id=1, source_target_pairs={{0,6},{1,7},{2,4},{3,5},{4,2},{5,3},{6,0},{7,1},{8,10},{9,11},{10,... | collective-permute-start | bytes 737288 | tf_op jit(solution)/shard_map/ppermute | solution.py:307
  27.9 10.2 %collective-permute-start.5 = (f32[4,5,24,128]{3,2,1,0:T(8,128)S(1)}, f32[4,5,24,128]{3,2,1,0:T(8,128)S(1)}, u32[]{:S(2)}, u32[]{:S(2)}) collective-permute-start(f32[4,5,24,128]{3,2,1,0:T(8,128)S(1)} %get-tuple-element.81), channel_id=1, source_target_pairs={{0,6},{1,7},{2,4},{3,5},{4,2},{5,3},{6,0},{7,1},{8,10},{9,11},{10,... | collective-permute-start | bytes 737288 | tf_op jit(solution)/shard_map/ppermute | solution.py:307
  30.8 14.3 %collective-permute-start.3 = (f32[8,10,8,128]{3,2,1,0:T(8,128)S(1)}, f32[8,10,8,128]{3,2,1,0:T(8,128)S(1)}, u32[]{:S(2)}, u32[]{:S(2)}) collective-permute-start(f32[8,10,8,128]{3,2,1,0:T(8,128)S(1)} %get-tuple-element.76), channel_id=1, source_target_pairs={{0,6},{1,7},{2,4},{3,5},{4,2},{5,3},{6,0},{7,1},{8,14},{9,15},{10,... | collective-permute-start | bytes 983048 | tf_op jit(solution)/shard_map/ppermute | solution.py:307
  31.3 14.0 %collective-permute-start.9 = (f32[4,5,24,128]{3,2,1,0:T(8,128)S(1)}, f32[4,5,24,128]{3,2,1,0:T(8,128)S(1)}, u32[]{:S(2)}, u32[]{:S(2)}) collective-permute-start(f32[4,5,24,128]{3,2,1,0:T(8,128)S(1)} %get-tuple-element.90.mine), channel_id=1, source_target_pairs={{0,1},{1,0},{2,3},{3,2},{4,5},{5,4},{6,7},{7,6},{8,14},{9,15},{10,... | collective-permute-start | bytes 737288 | tf_op jit(solution)/shard_map/ppermute | solution.py:307
  38.1 10.1 %collective-permute-start.8 = (f32[4,5,24,128]{3,2,1,0:T(8,128)S(1)}, f32[4,5,24,128]{3,2,1,0:T(8,128)S(1)}, u32[]{:S(2)}, u32[]{:S(2)}) collective-permute-start(f32[4,5,24,128]{3,2,1,0:T(8,128)S(1)} %get-tuple-element.89.mine), channel_id=1, source_target_pairs={{0,1},{1,0},{2,3},{3,2},{4,5},{5,4},{6,7},{7,6},{8,14},{9,15},{10,... | collective-permute-start | bytes 737288 | tf_op jit(solution)/shard_map/ppermute | solution.py:307
  45.1 5.4 %collective-permute-start.7 = (f32[4,10,8,128]{3,2,1,0:T(8,128)S(1)}, f32[4,10,8,128]{3,2,1,0:T(8,128)S(1)}, u32[]{:S(2)}, u32[]{:S(2)}) collective-permute-start(f32[4,10,8,128]{3,2,1,0:T(8,128)S(1)} %get-tuple-element.88), channel_id=1, source_target_pairs={{0,1},{1,0},{2,3},{3,2},{4,5},{5,4},{6,7},{7,6},{8,9},{9,8},{10,11... | collective-permute-start | bytes 491528 | tf_op jit(solution)/shard_map/ppermute | solution.py:307
  45.3 7.5 %collective-permute-start.12 = (f32[4,5,24,128]{3,2,1,0:T(8,128)S(1)}, f32[4,5,24,128]{3,2,1,0:T(8,128)S(1)}, u32[]{:S(2)}, u32[]{:S(2)}) collective-permute-start(f32[4,5,24,128]{3,2,1,0:T(8,128)S(1)} %get-tuple-element.96.mine), channel_id=1, source_target_pairs={{0,6},{1,7},{2,4},{3,5},{4,2},{5,3},{6,0},{7,1},{8,10},{9,11},{10,... | collective-permute-start | bytes 737288 | tf_op jit(solution)/shard_map/ppermute | solution.py:307
  48.2 7.5 %collective-permute-start.11 = (f32[4,5,24,128]{3,2,1,0:T(8,128)S(1)}, f32[4,5,24,128]{3,2,1,0:T(8,128)S(1)}, u32[]{:S(2)}, u32[]{:S(2)}) collective-permute-start(f32[4,5,24,128]{3,2,1,0:T(8,128)S(1)} %get-tuple-element.95.mine), channel_id=1, source_target_pairs={{0,6},{1,7},{2,4},{3,5},{4,2},{5,3},{6,0},{7,1},{8,10},{9,11},{10,... | collective-permute-start | bytes 737288 | tf_op jit(solution)/shard_map/ppermute | solution.py:307
  50.6 5.4 %collective-permute-start.10 = (f32[4,10,8,128]{3,2,1,0:T(8,128)S(1)}, f32[4,10,8,128]{3,2,1,0:T(8,128)S(1)}, u32[]{:S(2)}, u32[]{:S(2)}) collective-permute-start(f32[4,10,8,128]{3,2,1,0:T(8,128)S(1)} %get-tuple-element.94.mine), channel_id=1, source_target_pairs={{0,2},{1,3},{2,0},{3,1},{4,6},{5,7},{6,4},{7,5},{8,10},{9,11},{10,... | collective-permute-start | bytes 491528 | tf_op jit(solution)/shard_map/ppermute | solution.py:307
  52.8 15.4 %collective-permute-start.16 = (f32[8,5,24,128]{3,2,1,0:T(8,128)S(1)}, f32[8,5,24,128]{3,2,1,0:T(8,128)S(1)}, u32[]{:S(2)}, u32[]{:S(2)}) collective-permute-start(f32[8,5,24,128]{3,2,1,0:T(8,128)S(1)} %get-tuple-element.101.history), channel_id=1, source_target_pairs={{0,2},{1,3},{2,0},{3,1},{4,6},{5,7},{6,4},{7,5},{8,9},{9,8},{10,11... | collective-permute-start | bytes 1474568 | tf_op jit(solution)/shard_map/ppermute | solution.py:307
  56.0 7.2 %collective-permute-start.13 = (f32[4,10,8,128]{3,2,1,0:T(8,128)S(1)}, f32[4,10,8,128]{3,2,1,0:T(8,128)S(1)}, u32[]{:S(2)}, u32[]{:S(2)}) collective-permute-start(f32[4,10,8,128]{3,2,1,0:T(8,128)S(1)} %get-tuple-element.100.mine), channel_id=1, source_target_pairs={{0,1},{1,0},{2,3},{3,2},{4,5},{5,4},{6,7},{7,6},{8,9},{9,8},{10,11... | collective-permute-start | bytes 491528 | tf_op jit(solution)/shard_map/ppermute | solution.py:307
  57.9 13.5 %collective-permute-start.15 = (f32[8,5,24,128]{3,2,1,0:T(8,128)S(1)}, f32[8,5,24,128]{3,2,1,0:T(8,128)S(1)}, u32[]{:S(2)}, u32[]{:S(2)}) collective-permute-start(f32[8,5,24,128]{3,2,1,0:T(8,128)S(1)} %get-tuple-element.105.history), channel_id=1, source_target_pairs={{0,2},{1,3},{2,0},{3,1},{4,6},{5,7},{6,4},{7,5},{8,9},{9,8},{10,11... | collective-permute-start | bytes 1474568 | tf_op jit(solution)/shard_map/ppermute | solution.py:307
  63.3 10.0 %collective-permute-start.14 = (f32[8,10,8,128]{3,2,1,0:T(8,128)S(1)}, f32[8,10,8,128]{3,2,1,0:T(8,128)S(1)}, u32[]{:S(2)}, u32[]{:S(2)}) collective-permute-start(f32[8,10,8,128]{3,2,1,0:T(8,128)S(1)} %get-tuple-element.104.history), channel_id=1, source_target_pairs={{0,6},{1,7},{2,4},{3,5},{4,2},{5,3},{6,0},{7,1},{8,14},{9,15},{10,... | collective-permute-start | bytes 983048 | tf_op jit(solution)/shard_map/ppermute | solution.py:307

commit v3 on v2

--- a/solution.py
+++ b/solution.py
@@ -14,15 +14,14 @@
 FIELDS = 5
 BLOCK = 16
 BLOCKS = 4
-LOADS = (3, 2)
+LOADS = tuple((k, start, fields) for k in range(K) for start, fields in ((0, 3), (3, 2)))
 TILE = 8
 LANES = 128
 TIME_STEP = 0.4
 FOLD = 0.2
 EDGES = STEPS - 1
 PACKED = (EDGES + 1) // 2
-UNITS_PER_K = FIELDS * PACKED
-EDGE_UNITS = K * UNITS_PER_K + 1
+EDGE_UNITS = K * FIELDS * PACKED + 1
 X_PAIR, X_CROSS, Z_PAIR = 2, 6, 1
 SMALL = pltpu.CompilerParams(vmem_limit_bytes=12 * 2**20)
 
@@ -36,33 +35,24 @@
     return jnp.where(flag == 1, LANES - 1 - lane, lane)
 
 
-def front_kernel(
-    k, masks, order_hbm, flips_hbm, small, hat_hbm, speed_hbm, *rest
+def synth_kernel(
+    order_hbm, flips_hbm, small, hat_hbm, speed_hbm, forcing, chip_edge, far_edge, speed, table_out, meta, token, *scratch
 ):
-    low_in = high_in = None
-    if k:
-        low_in, high_in, _ = rest[:3]
-        rest = rest[3:]
-    keep, send, ends, low, high, speed, table_out, meta, token = rest[:9]
-    order, flips, hat, forcing, stored_speed, sems = rest[9:]
+    order, flips, hat, stored_speed, sems = scratch
     copies = [
         pltpu.make_async_copy(order_hbm, order, sems.at[0]),
         pltpu.make_async_copy(flips_hbm, flips, sems.at[1]),
         pltpu.make_async_copy(speed_hbm, stored_speed, sems.at[2]),
     ]
-    loads, done = [], 0
-    for i, fields in enumerate(LOADS):
-        there = hat_hbm.at[:, k, pl.ds(done, fields)]
-        loads.append(pltpu.make_async_copy(there, hat.at[:, pl.ds(done, fields)], sems.at[3 + i]))
-        done += fields
+    loads = []
+    for k, start, fields in LOADS:
+        part = (slice(None), k, pl.ds(start, fields))
+        loads.append(pltpu.make_async_copy(hat_hbm.at[part], hat.at[part], sems.at[3 + len(loads)]))
     for copy in copies + loads:
         copy.start()
     token[...] = jnp.zeros_like(token)
     table = spread_synthesis(small[: 2 * TILE])
-    if k:
-        low[: k * UNITS_PER_K] = low_in[: k * UNITS_PER_K]
-        high[: k * UNITS_PER_K] = high_in[: k * UNITS_PER_K]
-        table_out[...] = spread_analysis(small[2 * TILE : 4 * TILE], small[4 * TILE :])
+    table_out[...] = spread_analysis(small[2 * TILE : 4 * TILE], small[4 * TILE :])
     for copy in copies:
         copy.wait()
     flags = [flips[order[p]] for p in range(BLOCKS)]
@@ -70,40 +60,43 @@
     at = [pl.ds(pl.multiple_of(order[p] * BLOCK, BLOCK), BLOCK) for p in range(BLOCKS)]
     for p in range(BLOCKS):
         speed[p * BLOCK : (p + 1) * BLOCK, :] = flipped(stored_speed[at[p], :], lanes[p][:BLOCK])
-    if k:
-        low[EDGE_UNITS - 1] = speed[:TILE, :]
-        high[EDGE_UNITS - 1] = speed[BLOCKS * BLOCK - TILE :, :]
-        line = lax.broadcasted_iota(jnp.int32, (TILE, LANES), 0)
-        value = jnp.zeros((TILE, LANES), jnp.int32)
-        for t in range(2 * BLOCKS):
-            here = line == t
-            value = jnp.where(here, jnp.full((TILE, LANES), order[t // 2] * 4 + t % 2 * 2 + flags[t // 2]), value)
-        meta[...] = value
-    row = lax.broadcasted_iota(jnp.int32, (TILE, LANES), 0)
-    done = 0
-    for i, fields in enumerate(LOADS):
-        loads[i].wait()
-        for v in range(done, done + fields):
+    second = jnp.full((TILE, LANES), lax.axis_index("blk") % 2) == 1
+
+    def put(unit, low, high):
+        chip_edge[unit] = jnp.where(second, low, high)
+        far_edge[unit] = jnp.where(second, high, low)
+
+    put(EDGE_UNITS - 1, speed[:TILE, :], speed[BLOCKS * BLOCK - TILE :, :])
+    line = lax.broadcasted_iota(jnp.int32, (TILE, LANES), 0)
+    value = jnp.zeros((TILE, LANES), jnp.int32)
+    for t in range(2 * BLOCKS):
+        value = jnp.where(line == t, jnp.full((TILE, LANES), order[t // 2] * 4 + t % 2 * 2 + flags[t // 2]), value)
+    meta[...] = value
+    for load, (k, start, fields) in zip(loads, LOADS):
+        load.wait()
+        for v in range(start, start + fields):
+            lows, highs = [], []
             for p in range(0, BLOCKS, 2):
-                pair = [hat[:, v, at[p + i], :].reshape(-1, LANES) for i in range(2)]
-                both = jnp.dot(table, jnp.concatenate(pair, axis=1), preferred_element_type=jnp.float32)
+                pair = [hat[:, k, v, at[p + i], :].reshape(-1, LANES) for i in range(2)]
+                both = matmul(table, jnp.concatenate(pair, axis=1))
                 for i in range(2):
                     y = flipped(both[:, i * LANES : (i + 1) * LANES], lanes[p + i]).reshape(STEPS, BLOCK, LANES)
-                    forcing[:, v, (p + i) * BLOCK : (p + i + 1) * BLOCK, :] = y
-                    unit = k * UNITS_PER_K + v * PACKED
+                    forcing[k, :, v, (p + i) * BLOCK : (p + i + 1) * BLOCK, :] = y
                     if p + i == 0:
-                        ends[:, v, :BLOCK, :] = y
                         for s in range(PACKED):
                             late = pltpu.roll(y[EDGES - 1 - s, :TILE], EDGES - s, 0)
-                            low[unit + s] = jnp.where(row < EDGES - s, y[s, :TILE], late)
+                            lows.append(jnp.where(line < EDGES - s, y[s, :TILE], late))
                     if p + i == BLOCKS - 1:
-                        ends[:, v, BLOCK:, :] = y
                         for s in range(PACKED):
                             late = pltpu.roll(y[EDGES - 1 - s, TILE:], s + 1, 0)
-                            high[unit + s] = jnp.where(row > s, y[s, TILE:], late)
-        done += fields
-
-    rows = BLOCKS * BLOCK
+                            highs.append(jnp.where(line > s, y[s, TILE:], late))
+            for s in range(PACKED):
+                put((k * FIELDS + v) * PACKED + s, lows[s], highs[s])
+
+
+def inner_kernel(k, masks, forcing, speed, _, keep, send, token):
+    token[...] = jnp.zeros_like(token)
+    rows = speed.shape[0]
     half = rows // 2 - TILE
     upper = jnp.full((half, LANES), bit_at(masks)) == 1
 
@@ -113,7 +106,7 @@
             keep[s, v] = jnp.where(upper, second, first)
             send[s, v] = jnp.where(upper, first, second)
 
-    march(rows, speed[...], lambda s, v: forcing[s, v], None, emit)
+    march(rows, speed[...], lambda s, v: forcing[k, s, v], None, emit)
 
 
 def one_hot(shape, rows_are, columns_are):
@@ -178,7 +171,7 @@
     return jnp.where(lax.axis_index("blk") % 2 == 0, bit_of[masks[0]], bit_of[masks[1]])
 
 
-def edge_kernel(masks, ends0, ends1, speed, below, above, _, keep, send, token):
+def edge_kernel(masks, forcing, speed, from_chip, from_far, _, keep, send, token):
     token[...] = jnp.zeros_like(token)
     inner = speed.shape[0]
     row = lax.broadcasted_iota(jnp.int32, (6 * TILE, LANES), 0)
@@ -188,25 +181,33 @@
     has_above = (here < lax.axis_size("blk") - 1).astype(jnp.float32)
     inside = jnp.where(row < TILE, has_below, jnp.where(row >= 5 * TILE, has_above, 1.0))
 
+    second = jnp.full((TILE, LANES), here % 2) == 1
+
+    def halos(unit):
+        chip, far = from_chip[unit], from_far[unit]
+        return jnp.where(second, chip, far), jnp.where(second, far, chip)
+
     def windows(lo, body, hi):
         return jnp.concatenate([lo, body, hi], axis=0)
 
-    last = EDGE_UNITS - 1
+    below, above = halos(EDGE_UNITS - 1)
     near_ends = jnp.concatenate([speed[: 2 * TILE, :], speed[inner - 2 * TILE :, :]], axis=0)
-    speeds = windows(below[last], near_ends, above[last])
-    for k, ends in enumerate((ends0, ends1)):
+    speeds = windows(below, near_ends, above)
+    for k in range(K):
 
         def forcing_at(s, v):
-            unit = k * UNITS_PER_K + v * PACKED
+            unit = (k * FIELDS + v) * PACKED
             if s == EDGES:
                 lo = hi = jnp.zeros((TILE, LANES), jnp.float32)
             elif s < PACKED:
-                lo, hi = below[unit + s], above[unit + s]
+                lo, hi = halos(unit + s)
             else:
                 early = EDGES - 1 - s
-                lo = pltpu.roll(below[unit + early], TILE - 1 - early, 0)
-                hi = pltpu.roll(above[unit + early], early + 1, 0)
-            return windows(lo, ends[s, v], hi)
+                lo, hi = halos(unit + early)
+                lo = pltpu.roll(lo, TILE - 1 - early, 0)
+                hi = pltpu.roll(hi, early + 1, 0)
+            ends = [forcing[k, s, v, : 2 * TILE], forcing[k, s, v, inner - 2 * TILE :]]
+            return windows(lo, jnp.concatenate(ends, axis=0), hi)
 
         def emit(s, state):
             for v in range(FIELDS):
@@ -325,15 +326,12 @@
     freq = lax.axis_index("freq")
     cm = 2 * freq_local
 
-    masks_of = (
-        ((X_PAIR, Z_PAIR), (X_CROSS, X_PAIR), (Z_PAIR, X_CROSS)),
-        ((X_PAIR, Z_PAIR), (X_CROSS, X_PAIR), (Z_PAIR, X_CROSS)),
-        ((X_CROSS, X_CROSS), (Z_PAIR, Z_PAIR), (X_PAIR, X_PAIR)),
-    )
+    inner_masks = ((X_PAIR, X_CROSS), (Z_PAIR, Z_PAIR), (X_CROSS, X_PAIR))
+    edge_masks = ((X_PAIR, X_CROSS), (Z_PAIR, Z_PAIR), (X_CROSS, X_PAIR))
+    masks_of = (inner_masks, inner_masks, edge_masks)
     half = rows // 2 - TILE
     hbm = pl.BlockSpec(memory_space=pltpu.HBM)
     token_shape = pltpu.VMEM((TILE, LANES), jnp.float32)
-    edge_shape = pltpu.VMEM((EDGE_UNITS, TILE, LANES), jnp.float32)
 
     def call(kernel, name, shapes, *args, token=None):
         extra = [] if token is None else [token]
@@ -348,49 +346,48 @@
 
     small = small_tables(freq, freq_local)
     hat = forcing_hat.reshape(cm, K, FIELDS, rows, LANES)
-    part_shape = pltpu.VMEM((STEPS, FIELDS, half, LANES), jnp.float32)
-    keep, send, ends, arrived = [None] * 3, [None] * 3, [None] * K, [None] * 3
-    low = high = token = None
+    edge_shape = pltpu.VMEM((EDGE_UNITS, TILE, LANES), jnp.float32)
+    forcing, chip_edge, far_edge, speed, table, meta, token = pl.pallas_call(
+        synth_kernel,
+        out_shape=[
+            pltpu.VMEM((K, STEPS, FIELDS, rows, LANES), jnp.float32),
+            edge_shape,
+            edge_shape,
+            pltpu.VMEM((rows, LANES), jnp.float32),
+            pltpu.VMEM((BLOCK * TILE, 3 * STEPS * TILE), jnp.bfloat16),
+            pltpu.VMEM((TILE, LANES), jnp.int32),
+            token_shape,
+        ],
+        in_specs=[hbm, hbm, vmem(), hbm, hbm],
+        out_specs=[vmem()] * 7,
+        scratch_shapes=[
+            pltpu.SMEM((BLOCKS,), jnp.int32),
+            pltpu.SMEM((BLOCKS,), jnp.int32),
+            pltpu.VMEM((cm, K, FIELDS, rows, LANES), jnp.bfloat16),
+            pltpu.VMEM((rows, LANES), jnp.float32),
+            pltpu.SemaphoreType.DMA((3 + len(LOADS),)),
+        ],
+        compiler_params=SMALL,
+        name="synthesis",
+    )(far(block_order), far(block_flips), near(small), far(hat), far(mean_speed))
+
+    peers = lax.axis_size("blk")
+    from_chip = lax.ppermute(chip_edge, "blk", [(i, i ^ 1) for i in range(peers)])
+    joints = [(i, i + 1) for i in range(1, peers - 1, 2)]
+    from_far = lax.ppermute(far_edge, "blk", joints + [(j, i) for i, j in joints])
+
+    keep, send, arrived = [None] * 3, [None] * 3, [None] * 3
     for k in range(K):
-        extra = [near(low), near(high), token] if k else []
-        keep[k], send[k], ends[k], low, high, speed, table, meta, token = pl.pallas_call(
-            functools.partial(front_kernel, k, masks_of[k][0]),
-            out_shape=[
-                part_shape,
-                part_shape,
-                pltpu.VMEM((STEPS, FIELDS, 2 * BLOCK, LANES), jnp.float32),
-                edge_shape,
-                edge_shape,
-                pltpu.VMEM((rows, LANES), jnp.float32),
-                pltpu.VMEM((BLOCK * TILE, 3 * STEPS * TILE), jnp.bfloat16),
-                pltpu.VMEM((TILE, LANES), jnp.int32),
-                token_shape,
-            ],
-            in_specs=[hbm, hbm, vmem(), hbm, hbm]
-            + [vmem(), vmem(), pl.BlockSpec(memory_space=pl.ANY)][: len(extra)],
-            out_specs=[vmem()] * 9,
-            scratch_shapes=[
-                pltpu.SMEM((BLOCKS,), jnp.int32),
-                pltpu.SMEM((BLOCKS,), jnp.int32),
-                pltpu.VMEM((cm, FIELDS, rows, LANES), jnp.bfloat16),
-                pltpu.VMEM((STEPS, FIELDS, rows, LANES), jnp.float32),
-                pltpu.VMEM((rows, LANES), jnp.float32),
-                pltpu.SemaphoreType.DMA((3 + len(LOADS),)),
-            ],
-            compiler_params=SMALL,
-            name=f"front{k}",
-        )(far(block_order), far(block_flips), near(small), far(hat), far(mean_speed), *extra)
+        kernel = functools.partial(inner_kernel, k, masks_of[k][0])
+        shape = pltpu.VMEM((STEPS, FIELDS, half, LANES), jnp.float32)
+        keep[k], send[k], token = call(kernel, f"inner{k}", [shape] * 2, forcing, speed, token=token)
         arrived[k] = swap(send[k], masks_of[k][0])
-
-    peers = lax.axis_size("blk")
-    below = lax.ppermute(high, "blk", [(i, i + 1) for i in range(peers - 1)])
-    above = lax.ppermute(low, "blk", [(i + 1, i) for i in range(peers - 1)])
 
     def edges():
         nonlocal token
         kernel = functools.partial(edge_kernel, masks_of[2][0])
         shape = pltpu.VMEM((STEPS, K * FIELDS, TILE, LANES), jnp.float32)
-        args = (*ends, speed, below, above)
+        args = (forcing, speed, from_chip, from_far)
         keep[2], send[2], token = call(kernel, "edges", [shape] * 2, *args, token=token)
         arrived[2] = swap(send[2], masks_of[2][0])
 
@@ -462,8 +459,8 @@
     join(1)
     add(2, masks_of[2][1])
     analyse(0, whole[0], False)
+    analyse(1, whole[1], False)
     join(2)
-    analyse(1, whole[1], False)
     analyse(0, other[0], True)
     analyse(2, whole[2], False)
     analyse(1, other[1], True)

time: 75.6 us -> 65.5 us (0.87)
  waiting for transfers between devices: 27.9 us -> 18.1 us
  Pallas kernels: 19.9 us -> 18.4 us
  starting transfers between devices: 27 us -> 28.3 us
    ppermute x15, waiting for transfers between devices: 23.5 us -> 14.6 us  [swap(): return lax.ppermute(x, ('blk', 'freq'), pairs)]
    pallas_call x2 -> x1, Pallas kernels: 7.21 us -> 3.59 us  [local(): pl.pallas_call(synth_kernel, out_shape=[pltpu.VMEM((K, STEPS, FIELDS, row...]
    pallas_call x13 -> x15, Pallas kernels: 2.18 us -> 4.23 us  [call(): pl.pallas_call(kernel, out_shape=list(shapes) + [token_shape], in_specs=[...]
    ppermute x15, starting transfers between devices: 17.8 us -> 19.8 us  [swap(): return lax.ppermute(x, ('blk', 'freq'), pairs)]
    ppermute x2, waiting for transfers between devices: 4.33 us -> 3.5 us  [the longest x1 3.5 us: local(): lax.ppermute(far_edge, 'blk', joints + [(j, i) for i, j in joints])]
  transfers between devices with their start and end apart: 17 -> 17, of which waited for: 8 -> 9; matrix products, arithmetic and copies ran while one was open for 0% -> 0% of each run, Pallas kernels for 19% -> 18%
where the time goes in v3:
time: 65.5 us; the launch traced here: 65.4 us
  starting transfers between devices  28.3 us (43%)
  Pallas kernels  18.4 us (28%)
  waiting for transfers between devices  18.1 us (28%)
    ppermute x15, starting transfers between devices, swap(): return lax.ppermute(x, ('blk', 'freq'), pairs)  19.8 us
    ppermute x15, waiting for transfers between devices, swap(): return lax.ppermute(x, ('blk', 'freq'), pairs)  14.6 us
    pallas_call x6, Pallas kernels, analyse(): pl.pallas_call(functools.partial(analysis_kernel, first_tile, i * FIELDS...  10.6 us
    ppermute x1, starting transfers between devices, local(): lax.ppermute(far_edge, 'blk', joints + [(j, i) for i, j in joints])  8 us
    pallas_call x15, Pallas kernels, call(): pl.pallas_call(kernel, out_shape=list(shapes) + [token_shape], in_specs=[...  4.23 us
    pallas_call x1, Pallas kernels, local(): pl.pallas_call(synth_kernel, out_shape=[pltpu.VMEM((K, STEPS, FIELDS, row...  3.59 us
    ppermute x1, waiting for transfers between devices, local(): lax.ppermute(far_edge, 'blk', joints + [(j, i) for i, j in joints])  3.5 us
  transfers between devices with their start and end apart: 17, of which 9 were waited for; matrix products, arithmetic and copies ran while one was open for 0% of the time, Pallas kernels for 18%

profile of v3, /device:TPU:24, one launch (start us, length us, event | category | flops | bytes accessed | tf_op | source)
XLA Modules:
  0.0 65.4 jit_solution(8642985202783643915)
XLA Ops:
  0.2 3.6 %synthesis.1 = (f32[2,8,5,64,128]{4,3,2,1,0:T(8,128)S(1)}, f32[41,8,128]{2,1,0:T(8,128)S(1)}, f32[41,8,128]{2,1,0:T(8,128)S(1)}, f32[64,128]{1,0:T(8,128)S(1)}, ...) custom-call(s32[4]{0:T(128)} %order_hbm.1, s32[4]{0:T(128)} %flips_hbm.1, ...), custom_call_target="tpu_custom_call" | custom-call | tf_op jit(solution)/shard_map/synthesis/pallas_call | solution.py:350
  3.9 1.1 %inner0.1 = (f32[8,5,24,128]{3,2,1,0:T(8,128)S(1)}, f32[8,5,24,128]{3,2,1,0:T(8,128)S(1)}, f32[8,128]{1,0:T(8,128)S(1)}) custom-call(f32[2,8,5,64,128]{4,3,2,1,0:T(8,128)S(1)} %get-tuple-element.61.forcing, f32[64,128]{1,0:T(8,128)S(1)} %get-tuple-element.62.speed, f32[8,128]{1,0:T(8,128)S(1)} %get-tuple-element.65._), custom_call_target="tpu_custom_call" | custom-call | tf_op jit(solution)/shard_map/inner0/pallas_call | solution.py:338
  4.9 1.6 %collective-permute-start.2 = (f32[8,5,24,128]{3,2,1,0:T(8,128)S(1)}, f32[8,5,24,128]{3,2,1,0:T(8,128)S(1)}, u32[]{:S(2)}, u32[]{:S(2)}) collective-permute-start(f32[8,5,24,128]{3,2,1,0:T(8,128)S(1)} %get-tuple-element.67), channel_id=1, source_target_pairs={{0,2},{1,3},{2,0},{3,1},{4,6},{5,7},{6,4},{7,5},{8,14},{9,15},{10,... | collective-permute-start | bytes 1474568 | tf_op jit(solution)/shard_map/ppermute | solution.py:308
  6.5 1.1 %inner1.1 = (f32[8,5,24,128]{3,2,1,0:T(8,128)S(1)}, f32[8,5,24,128]{3,2,1,0:T(8,128)S(1)}, f32[8,128]{1,0:T(8,128)S(1)}) custom-call(f32[2,8,5,64,128]{4,3,2,1,0:T(8,128)S(1)} %get-tuple-element.61.forcing, f32[64,128]{1,0:T(8,128)S(1)} %get-tuple-element.62.speed, f32[8,128]{1,0:T(8,128)S(1)} %get-tuple-element.68._), custom_call_target="tpu_custom_call" | custom-call | tf_op jit(solution)/shard_map/inner1/pallas_call | solution.py:338
  7.6 0.6 collective-permute-start.4
  8.7 8.0 %collective-permute-start.1 = (f32[41,8,128]{2,1,0:T(8,128)S(1)}, f32[41,8,128]{2,1,0:T(8,128)S(1)}, u32[]{:S(2)}, u32[]{:S(2)}) collective-permute-start(f32[41,8,128]{2,1,0:T(8,128)S(1)} %get-tuple-element.64), channel_id=1, source_target_pairs={{8,16},{24,32},{40,48},{56,64},{72,80},{88,96},{104,112},{120,128}... | collective-permute-start | bytes 503816 | tf_op jit(solution)/shard_map/ppermute | solution.py:377
  16.8 1.1 %collective-permute-start.6 = (f32[4,5,24,128]{3,2,1,0:T(8,128)S(1)}, f32[4,5,24,128]{3,2,1,0:T(8,128)S(1)}, u32[]{:S(2)}, u32[]{:S(2)}) collective-permute-start(f32[4,5,24,128]{3,2,1,0:T(8,128)S(1)} %get-tuple-element.79), channel_id=1, source_target_pairs={{0,1},{1,0},{2,3},{3,2},{4,5},{5,4},{6,7},{7,6},{8,9},{9,8},{10,11... | collective-permute-start | bytes 737288 | tf_op jit(solution)/shard_map/ppermute | solution.py:308
  17.9 3.5 %collective-permute-done.1.from_far = f32[41,8,128]{2,1,0:T(8,128)S(1)} collective-permute-done((f32[41,8,128]{2,1,0:T(8,128)S(1)}, f32[41,8,128]{2,1,0:T(8,128)S(1)}, u32[]{:S(2)}, u32[]{:S(2)}) %collective-permute-start.1) | collective-permute-done | bytes 167968 | tf_op jit(solution)/shard_map/ppermute | solution.py:377
  21.4 1.6 %edges.1 = (f32[8,10,8,128]{3,2,1,0:T(8,128)S(1)}, f32[8,10,8,128]{3,2,1,0:T(8,128)S(1)}, f32[8,128]{1,0:T(8,128)S(1)}) custom-call(f32[2,8,5,64,128]{4,3,2,1,0:T(8,128)S(1)} %get-tuple-element.61.forcing, f32[64,128]{1,0:T(8,128)S(1)} %get-tuple-element.62.speed, f32[41,8,128]{2,1,0:T(8,128)S(1)} %collective-permute-done.from_chip, ...), custom_call_target="tpu_custom_call" | custom-call | tf_op jit(solution)/shard_map/edges/pallas_call | solution.py:338
  23.1 1.4 %collective-permute-start.5 = (f32[4,5,24,128]{3,2,1,0:T(8,128)S(1)}, f32[4,5,24,128]{3,2,1,0:T(8,128)S(1)}, u32[]{:S(2)}, u32[]{:S(2)}) collective-permute-start(f32[4,5,24,128]{3,2,1,0:T(8,128)S(1)} %get-tuple-element.77), channel_id=1, source_target_pairs={{0,1},{1,0},{2,3},{3,2},{4,5},{5,4},{6,7},{7,6},{8,9},{9,8},{10,11... | collective-permute-start | bytes 737288 | tf_op jit(solution)/shard_map/ppermute | solution.py:308
  24.5 1.4 %collective-permute-start.3 = (f32[8,10,8,128]{3,2,1,0:T(8,128)S(1)}, f32[8,10,8,128]{3,2,1,0:T(8,128)S(1)}, u32[]{:S(2)}, u32[]{:S(2)}) collective-permute-start(f32[8,10,8,128]{3,2,1,0:T(8,128)S(1)} %get-tuple-element.72), channel_id=1, source_target_pairs={{0,2},{1,3},{2,0},{3,1},{4,6},{5,7},{6,4},{7,5},{8,14},{9,15},{10,... | collective-permute-start | bytes 983048 | tf_op jit(solution)/shard_map/ppermute | solution.py:308
  25.9 2.2 %collective-permute-start.9 = (f32[4,5,24,128]{3,2,1,0:T(8,128)S(1)}, f32[4,5,24,128]{3,2,1,0:T(8,128)S(1)}, u32[]{:S(2)}, u32[]{:S(2)}) collective-permute-start(f32[4,5,24,128]{3,2,1,0:T(8,128)S(1)} %get-tuple-element.86.mine), channel_id=1, source_target_pairs={{0,6},{1,7},{2,4},{3,5},{4,2},{5,3},{6,0},{7,1},{8,10},{9,11},{10,... | collective-permute-start | bytes 737288 | tf_op jit(solution)/shard_map/ppermute | solution.py:308
  28.1 1.5 %collective-permute-done.5.arrived = f32[4,5,24,128]{3,2,1,0:T(8,128)S(1)} collective-permute-done((f32[4,5,24,128]{3,2,1,0:T(8,128)S(1)}, f32[4,5,24,128]{3,2,1,0:T(8,128)S(1)}, u32[]{:S(2)}, u32[]{:S(2)}) %collective-permute-start.5) | collective-permute-done | bytes 245792 | tf_op jit(solution)/shard_map/ppermute | solution.py:308
  29.7 2.8 %collective-permute-start.8 = (f32[4,5,24,128]{3,2,1,0:T(8,128)S(1)}, f32[4,5,24,128]{3,2,1,0:T(8,128)S(1)}, u32[]{:S(2)}, u32[]{:S(2)}) collective-permute-start(f32[4,5,24,128]{3,2,1,0:T(8,128)S(1)} %get-tuple-element.85.mine), channel_id=1, source_target_pairs={{0,6},{1,7},{2,4},{3,5},{4,2},{5,3},{6,0},{7,1},{8,10},{9,11},{10,... | collective-permute-start | bytes 737288 | tf_op jit(solution)/shard_map/ppermute | solution.py:308
  32.5 2.2 %collective-permute-done.3.arrived = f32[8,10,8,128]{3,2,1,0:T(8,128)S(1)} collective-permute-done((f32[8,10,8,128]{3,2,1,0:T(8,128)S(1)}, f32[8,10,8,128]{3,2,1,0:T(8,128)S(1)}, u32[]{:S(2)}, u32[]{:S(2)}) %collective-permute-start.3) | collective-permute-done | bytes 327712 | tf_op jit(solution)/shard_map/ppermute | solution.py:308
  34.8 1.1 %collective-permute-start.7 = (f32[4,10,8,128]{3,2,1,0:T(8,128)S(1)}, f32[4,10,8,128]{3,2,1,0:T(8,128)S(1)}, u32[]{:S(2)}, u32[]{:S(2)}) collective-permute-start(f32[4,10,8,128]{3,2,1,0:T(8,128)S(1)} %get-tuple-element.84), channel_id=1, source_target_pairs={{0,1},{1,0},{2,3},{3,2},{4,5},{5,4},{6,7},{7,6},{8,9},{9,8},{10,11... | collective-permute-start | bytes 491528 | tf_op jit(solution)/shard_map/ppermute | solution.py:308
  36.0 1.1 %collective-permute-start.12 = (f32[4,5,24,128]{3,2,1,0:T(8,128)S(1)}, f32[4,5,24,128]{3,2,1,0:T(8,128)S(1)}, u32[]{:S(2)}, u32[]{:S(2)}) collective-permute-start(f32[4,5,24,128]{3,2,1,0:T(8,128)S(1)} %get-tuple-element.92.mine), channel_id=1, source_target_pairs={{0,1},{1,0},{2,3},{3,2},{4,5},{5,4},{6,7},{7,6},{8,9},{9,8},{10,11... | collective-permute-start | bytes 737288 | tf_op jit(solution)/shard_map/ppermute | solution.py:308
  37.2 1.1 %collective-permute-start.11 = (f32[4,5,24,128]{3,2,1,0:T(8,128)S(1)}, f32[4,5,24,128]{3,2,1,0:T(8,128)S(1)}, u32[]{:S(2)}, u32[]{:S(2)}) collective-permute-start(f32[4,5,24,128]{3,2,1,0:T(8,128)S(1)} %get-tuple-element.91.mine), channel_id=1, source_target_pairs={{0,1},{1,0},{2,3},{3,2},{4,5},{5,4},{6,7},{7,6},{8,9},{9,8},{10,11... | collective-permute-start | bytes 737288 | tf_op jit(solution)/shard_map/ppermute | solution.py:308
  38.3 3.6 %collective-permute-done.7.arrived = f32[4,10,8,128]{3,2,1,0:T(8,128)S(1)} collective-permute-done((f32[4,10,8,128]{3,2,1,0:T(8,128)S(1)}, f32[4,10,8,128]{3,2,1,0:T(8,128)S(1)}, u32[]{:S(2)}, u32[]{:S(2)}) %collective-permute-start.7) | collective-permute-done | bytes 163872 | tf_op jit(solution)/shard_map/ppermute | solution.py:308
  41.9 1.3 %collective-permute-start.10 = (f32[4,10,8,128]{3,2,1,0:T(8,128)S(1)}, f32[4,10,8,128]{3,2,1,0:T(8,128)S(1)}, u32[]{:S(2)}, u32[]{:S(2)}) collective-permute-start(f32[4,10,8,128]{3,2,1,0:T(8,128)S(1)} %get-tuple-element.90.mine), channel_id=1, source_target_pairs={{0,6},{1,7},{2,4},{3,5},{4,2},{5,3},{6,0},{7,1},{8,10},{9,11},{10,... | collective-permute-start | bytes 491528 | tf_op jit(solution)/shard_map/ppermute | solution.py:308
  43.2 1.7 %collective-permute-done.12.arrived = f32[4,5,24,128]{3,2,1,0:T(8,128)S(1)} collective-permute-done((f32[4,5,24,128]{3,2,1,0:T(8,128)S(1)}, f32[4,5,24,128]{3,2,1,0:T(8,128)S(1)}, u32[]{:S(2)}, u32[]{:S(2)}) %collective-permute-start.12) | collective-permute-done | bytes 245792 | tf_op jit(solution)/shard_map/ppermute | solution.py:308
  45.0 0.6 collective-permute-start.16
  45.6 3.6 %collective-permute-done.11.arrived = f32[4,5,24,128]{3,2,1,0:T(8,128)S(1)} collective-permute-done((f32[4,5,24,128]{3,2,1,0:T(8,128)S(1)}, f32[4,5,24,128]{3,2,1,0:T(8,128)S(1)}, u32[]{:S(2)}, u32[]{:S(2)}) %collective-permute-start.11) | collective-permute-done | bytes 245792 | tf_op jit(solution)/shard_map/ppermute | solution.py:308
  49.3 1.6 %collective-permute-start.13 = (f32[4,10,8,128]{3,2,1,0:T(8,128)S(1)}, f32[4,10,8,128]{3,2,1,0:T(8,128)S(1)}, u32[]{:S(2)}, u32[]{:S(2)}) collective-permute-start(f32[4,10,8,128]{3,2,1,0:T(8,128)S(1)} %get-tuple-element.96.mine), channel_id=1, source_target_pairs={{0,1},{1,0},{2,3},{3,2},{4,5},{5,4},{6,7},{7,6},{8,9},{9,8},{10,11... | collective-permute-start | bytes 491528 | tf_op jit(solution)/shard_map/ppermute | solution.py:308
  50.9 1.8 %analysis0.2 = (f32[16,10,8,8,128]{4,3,2,1,0:T(8,128)}, f32[8,128]{1,0:T(8,128)S(1)}) custom-call(s32[8,128]{1,0:T(8,128)S(1)} %get-tuple-element.59.meta, bf16[128,192]{1,0:T(8,128)(2,1)S(1)} %get-tuple-element.60.table, f32[8,5,24,128]{3,2,1,0:T(8,128)S(1)} %get-tuple-element.98.history, f32[8,128]{1,0:T(8,128)S(1)} %get-tuple-element.99._), custom_call_target="tpu_custom_call" | custom-call | tf_op jit(solution)/shard_map/analysis0/pallas_call | solution.py:432
  52.7 1.8 %analysis1.2 = (f32[16,10,8,8,128]{4,3,2,1,0:T(8,128)}, f32[8,128]{1,0:T(8,128)S(1)}) custom-call(s32[8,128]{1,0:T(8,128)S(1)} %get-tuple-element.59.meta, bf16[128,192]{1,0:T(8,128)(2,1)S(1)} %get-tuple-element.60.table, f32[8,5,24,128]{3,2,1,0:T(8,128)S(1)} %get-tuple-element.97.history, ...), custom_call_target="tpu_custom_call", output_to_operand_aliasing={{0}: (4, {})} | custom-call | tf_op jit(solution)/shard_map/analysis1/pallas_call | solution.py:432
  54.8 1.9 %collective-permute-start.14 = (f32[8,10,8,128]{3,2,1,0:T(8,128)S(1)}, f32[8,10,8,128]{3,2,1,0:T(8,128)S(1)}, u32[]{:S(2)}, u32[]{:S(2)}) collective-permute-start(f32[8,10,8,128]{3,2,1,0:T(8,128)S(1)} %get-tuple-element.103.history), channel_id=1, source_target_pairs={{0,2},{1,3},{2,0},{3,1},{4,6},{5,7},{6,4},{7,5},{8,14},{9,15},{10,... | collective-permute-start | bytes 983048 | tf_op jit(solution)/shard_map/ppermute | solution.py:308
  56.7 1.8 %analysis0.3 = (f32[16,10,8,8,128]{4,3,2,1,0:T(8,128)}, f32[8,128]{1,0:T(8,128)S(1)}) custom-call(s32[8,128]{1,0:T(8,128)S(1)} %get-tuple-element.59.meta, bf16[128,192]{1,0:T(8,128)(2,1)S(1)} %get-tuple-element.60.table, f32[8,5,24,128]{3,2,1,0:T(8,128)S(1)} %collective-permute-done.16.history, ...), custom_call_target="tpu_custom_call", output_to_operand_aliasing={{0}: (4, {})} | custom-call | tf_op jit(solution)/shard_map/analysis0/pallas_call | solution.py:432
  58.5 1.4 %analysis2.2 = (f32[16,10,8,8,128]{4,3,2,1,0:T(8,128)}, f32[8,128]{1,0:T(8,128)S(1)}) custom-call(s32[8,128]{1,0:T(8,128)S(1)} %get-tuple-element.59.meta, bf16[128,192]{1,0:T(8,128)(2,1)S(1)} %get-tuple-element.60.table, f32[8,10,8,128]{3,2,1,0:T(8,128)S(1)} %get-tuple-element.103.history, ...), custom_call_target="tpu_custom_call", output_to_operand_aliasing={{0}: (4, {})} | custom-call | tf_op jit(solution)/shard_map/analysis2/pallas_call | solution.py:432
  59.9 1.8 %analysis1.3 = (f32[16,10,8,8,128]{4,3,2,1,0:T(8,128)}, f32[8,128]{1,0:T(8,128)S(1)}) custom-call(s32[8,128]{1,0:T(8,128)S(1)} %get-tuple-element.59.meta, bf16[128,192]{1,0:T(8,128)(2,1)S(1)} %get-tuple-element.60.table, f32[8,5,24,128]{3,2,1,0:T(8,128)S(1)} %collective-permute-done.15.history, ...), custom_call_target="tpu_custom_call", output_to_operand_aliasing={{0}: (4, {})} | custom-call | tf_op jit(solution)/shard_map/analysis1/pallas_call | solution.py:432
  61.7 1.5 %collective-permute-done.14.history = f32[8,10,8,128]{3,2,1,0:T(8,128)S(1)} collective-permute-done((f32[8,10,8,128]{3,2,1,0:T(8,128)S(1)}, f32[8,10,8,128]{3,2,1,0:T(8,128)S(1)}, u32[]{:S(2)}, u32[]{:S(2)}) %collective-permute-start.14) | collective-permute-done | bytes 327712 | tf_op jit(solution)/shard_map/ppermute | solution.py:308
  63.2 2.0 %analysis2.3 = (f32[16,10,8,8,128]{4,3,2,1,0:T(8,128)}, f32[8,128]{1,0:T(8,128)}) custom-call(s32[8,128]{1,0:T(8,128)S(1)} %get-tuple-element.59.meta, bf16[128,192]{1,0:T(8,128)(2,1)S(1)} %get-tuple-element.60.table, f32[8,10,8,128]{3,2,1,0:T(8,128)S(1)} %collective-permute-done.14.history, ...), custom_call_target="tpu_custom_call", output_to_operand_aliasing={{0}: (4, {})} | custom-call | tf_op jit(solution)/shard_map/analysis2/pallas_call | solution.py:432
  (33 shorter events, 1.5 us)
Async XLA Ops:
  4.9 11.8 %collective-permute-start.2 = (f32[8,5,24,128]{3,2,1,0:T(8,128)S(1)}, f32[8,5,24,128]{3,2,1,0:T(8,128)S(1)}, u32[]{:S(2)}, u32[]{:S(2)}) collective-permute-start(f32[8,5,24,128]{3,2,1,0:T(8,128)S(1)} %get-tuple-element.67), channel_id=1, source_target_pairs={{0,2},{1,3},{2,0},{3,1},{4,6},{5,7},{6,4},{7,5},{8,14},{9,15},{10,... | collective-permute-start | bytes 1474568 | tf_op jit(solution)/shard_map/ppermute | solution.py:308
  7.6 15.5 %collective-permute-start.4 = (f32[8,5,24,128]{3,2,1,0:T(8,128)S(1)}, f32[8,5,24,128]{3,2,1,0:T(8,128)S(1)}, u32[]{:S(2)}, u32[]{:S(2)}) collective-permute-start(f32[8,5,24,128]{3,2,1,0:T(8,128)S(1)} %get-tuple-element.74), channel_id=1, source_target_pairs={{0,2},{1,3},{2,0},{3,1},{4,6},{5,7},{6,4},{7,5},{8,14},{9,15},{10,... | collective-permute-start | bytes 1474568 | tf_op jit(solution)/shard_map/ppermute | solution.py:308
  8.2 9.7 %collective-permute-start = (f32[41,8,128]{2,1,0:T(8,128)S(1)}, f32[41,8,128]{2,1,0:T(8,128)S(1)}, u32[]{:S(2)}, u32[]{:S(2)}) collective-permute-start(f32[41,8,128]{2,1,0:T(8,128)S(1)} %get-tuple-element.63), channel_id=1, source_target_pairs={{0,8},{8,0},{16,24},{24,16},{32,40},{40,32},{48,56},{56,48},{64,72... | collective-permute-start | bytes 503816 | tf_op jit(solution)/shard_map/ppermute | solution.py:375
  8.7 12.7 %collective-permute-start.1 = (f32[41,8,128]{2,1,0:T(8,128)S(1)}, f32[41,8,128]{2,1,0:T(8,128)S(1)}, u32[]{:S(2)}, u32[]{:S(2)}) collective-permute-start(f32[41,8,128]{2,1,0:T(8,128)S(1)} %get-tuple-element.64), channel_id=1, source_target_pairs={{8,16},{24,32},{40,48},{56,64},{72,80},{88,96},{104,112},{120,128}... | collective-permute-start | bytes 503816 | tf_op jit(solution)/shard_map/ppermute | solution.py:377
  16.8 9.1 %collective-permute-start.6 = (f32[4,5,24,128]{3,2,1,0:T(8,128)S(1)}, f32[4,5,24,128]{3,2,1,0:T(8,128)S(1)}, u32[]{:S(2)}, u32[]{:S(2)}) collective-permute-start(f32[4,5,24,128]{3,2,1,0:T(8,128)S(1)} %get-tuple-element.79), channel_id=1, source_target_pairs={{0,1},{1,0},{2,3},{3,2},{4,5},{5,4},{6,7},{7,6},{8,9},{9,8},{10,11... | collective-permute-start | bytes 737288 | tf_op jit(solution)/shard_map/ppermute | solution.py:308
  23.1 6.5 %collective-permute-start.5 = (f32[4,5,24,128]{3,2,1,0:T(8,128)S(1)}, f32[4,5,24,128]{3,2,1,0:T(8,128)S(1)}, u32[]{:S(2)}, u32[]{:S(2)}) collective-permute-start(f32[4,5,24,128]{3,2,1,0:T(8,128)S(1)} %get-tuple-element.77), channel_id=1, source_target_pairs={{0,1},{1,0},{2,3},{3,2},{4,5},{5,4},{6,7},{7,6},{8,9},{9,8},{10,11... | collective-permute-start | bytes 737288 | tf_op jit(solution)/shard_map/ppermute | solution.py:308
  24.5 10.3 %collective-permute-start.3 = (f32[8,10,8,128]{3,2,1,0:T(8,128)S(1)}, f32[8,10,8,128]{3,2,1,0:T(8,128)S(1)}, u32[]{:S(2)}, u32[]{:S(2)}) collective-permute-start(f32[8,10,8,128]{3,2,1,0:T(8,128)S(1)} %get-tuple-element.72), channel_id=1, source_target_pairs={{0,2},{1,3},{2,0},{3,1},{4,6},{5,7},{6,4},{7,5},{8,14},{9,15},{10,... | collective-permute-start | bytes 983048 | tf_op jit(solution)/shard_map/ppermute | solution.py:308
  25.9 10.0 %collective-permute-start.9 = (f32[4,5,24,128]{3,2,1,0:T(8,128)S(1)}, f32[4,5,24,128]{3,2,1,0:T(8,128)S(1)}, u32[]{:S(2)}, u32[]{:S(2)}) collective-permute-start(f32[4,5,24,128]{3,2,1,0:T(8,128)S(1)} %get-tuple-element.86.mine), channel_id=1, source_target_pairs={{0,6},{1,7},{2,4},{3,5},{4,2},{5,3},{6,0},{7,1},{8,10},{9,11},{10,... | collective-permute-start | bytes 737288 | tf_op jit(solution)/shard_map/ppermute | solution.py:308
  29.7 7.5 %collective-permute-start.8 = (f32[4,5,24,128]{3,2,1,0:T(8,128)S(1)}, f32[4,5,24,128]{3,2,1,0:T(8,128)S(1)}, u32[]{:S(2)}, u32[]{:S(2)}) collective-permute-start(f32[4,5,24,128]{3,2,1,0:T(8,128)S(1)} %get-tuple-element.85.mine), channel_id=1, source_target_pairs={{0,6},{1,7},{2,4},{3,5},{4,2},{5,3},{6,0},{7,1},{8,10},{9,11},{10,... | collective-permute-start | bytes 737288 | tf_op jit(solution)/shard_map/ppermute | solution.py:308
  34.8 7.1 %collective-permute-start.7 = (f32[4,10,8,128]{3,2,1,0:T(8,128)S(1)}, f32[4,10,8,128]{3,2,1,0:T(8,128)S(1)}, u32[]{:S(2)}, u32[]{:S(2)}) collective-permute-start(f32[4,10,8,128]{3,2,1,0:T(8,128)S(1)} %get-tuple-element.84), channel_id=1, source_target_pairs={{0,1},{1,0},{2,3},{3,2},{4,5},{5,4},{6,7},{7,6},{8,9},{9,8},{10,11... | collective-permute-start | bytes 491528 | tf_op jit(solution)/shard_map/ppermute | solution.py:308
  36.0 9.0 %collective-permute-start.12 = (f32[4,5,24,128]{3,2,1,0:T(8,128)S(1)}, f32[4,5,24,128]{3,2,1,0:T(8,128)S(1)}, u32[]{:S(2)}, u32[]{:S(2)}) collective-permute-start(f32[4,5,24,128]{3,2,1,0:T(8,128)S(1)} %get-tuple-element.92.mine), channel_id=1, source_target_pairs={{0,1},{1,0},{2,3},{3,2},{4,5},{5,4},{6,7},{7,6},{8,9},{9,8},{10,11... | collective-permute-start | bytes 737288 | tf_op jit(solution)/shard_map/ppermute | solution.py:308
  37.2 12.0 %collective-permute-start.11 = (f32[4,5,24,128]{3,2,1,0:T(8,128)S(1)}, f32[4,5,24,128]{3,2,1,0:T(8,128)S(1)}, u32[]{:S(2)}, u32[]{:S(2)}) collective-permute-start(f32[4,5,24,128]{3,2,1,0:T(8,128)S(1)} %get-tuple-element.91.mine), channel_id=1, source_target_pairs={{0,1},{1,0},{2,3},{3,2},{4,5},{5,4},{6,7},{7,6},{8,9},{9,8},{10,11... | collective-permute-start | bytes 737288 | tf_op jit(solution)/shard_map/ppermute | solution.py:308
  41.9 7.4 %collective-permute-start.10 = (f32[4,10,8,128]{3,2,1,0:T(8,128)S(1)}, f32[4,10,8,128]{3,2,1,0:T(8,128)S(1)}, u32[]{:S(2)}, u32[]{:S(2)}) collective-permute-start(f32[4,10,8,128]{3,2,1,0:T(8,128)S(1)} %get-tuple-element.90.mine), channel_id=1, source_target_pairs={{0,6},{1,7},{2,4},{3,5},{4,2},{5,3},{6,0},{7,1},{8,10},{9,11},{10,... | collective-permute-start | bytes 491528 | tf_op jit(solution)/shard_map/ppermute | solution.py:308
  45.0 11.7 %collective-permute-start.16 = (f32[8,5,24,128]{3,2,1,0:T(8,128)S(1)}, f32[8,5,24,128]{3,2,1,0:T(8,128)S(1)}, u32[]{:S(2)}, u32[]{:S(2)}) collective-permute-start(f32[8,5,24,128]{3,2,1,0:T(8,128)S(1)} %get-tuple-element.98.history), channel_id=1, source_target_pairs={{0,2},{1,3},{2,0},{3,1},{4,6},{5,7},{6,4},{7,5},{8,14},{9,15},{10,... | collective-permute-start | bytes 1474568 | tf_op jit(solution)/shard_map/ppermute | solution.py:308
  49.3 5.4 %collective-permute-start.13 = (f32[4,10,8,128]{3,2,1,0:T(8,128)S(1)}, f32[4,10,8,128]{3,2,1,0:T(8,128)S(1)}, u32[]{:S(2)}, u32[]{:S(2)}) collective-permute-start(f32[4,10,8,128]{3,2,1,0:T(8,128)S(1)} %get-tuple-element.96.mine), channel_id=1, source_target_pairs={{0,1},{1,0},{2,3},{3,2},{4,5},{5,4},{6,7},{7,6},{8,9},{9,8},{10,11... | collective-permute-start | bytes 491528 | tf_op jit(solution)/shard_map/ppermute | solution.py:308
  50.9 9.0 %collective-permute-start.15 = (f32[8,5,24,128]{3,2,1,0:T(8,128)S(1)}, f32[8,5,24,128]{3,2,1,0:T(8,128)S(1)}, u32[]{:S(2)}, u32[]{:S(2)}) collective-permute-start(f32[8,5,24,128]{3,2,1,0:T(8,128)S(1)} %get-tuple-element.97.history), channel_id=1, source_target_pairs={{0,2},{1,3},{2,0},{3,1},{4,6},{5,7},{6,4},{7,5},{8,14},{9,15},{10,... | collective-permute-start | bytes 1474568 | tf_op jit(solution)/shard_map/ppermute | solution.py:308
  54.8 8.5 %collective-permute-start.14 = (f32[8,10,8,128]{3,2,1,0:T(8,128)S(1)}, f32[8,10,8,128]{3,2,1,0:T(8,128)S(1)}, u32[]{:S(2)}, u32[]{:S(2)}) collective-permute-start(f32[8,10,8,128]{3,2,1,0:T(8,128)S(1)} %get-tuple-element.103.history), channel_id=1, source_target_pairs={{0,2},{1,3},{2,0},{3,1},{4,6},{5,7},{6,4},{7,5},{8,14},{9,15},{10,... | collective-permute-start | bytes 983048 | tf_op jit(solution)/shard_map/ppermute | solution.py:308

commit v4 on v3

--- a/solution.py
+++ b/solution.py
@@ -279,8 +279,9 @@
                 out.at[:, pl.ds(first_unit + start, FIELDS), tile],
                 sems.at[len(copies)],
             )
-            copy.start()
             copies.append(copy)
+    for copy in copies:
+        copy.start()
     for copy in copies:
         copy.wait()
 

time: 65.5 us -> 65.4 us (level)
  waiting for transfers between devices: 18.1 us -> 20.1 us
  Pallas kernels: 18.4 us -> 16.9 us
    ppermute x15, waiting for transfers between devices: 14.6 us -> 16.6 us  [swap(): return lax.ppermute(x, ('blk', 'freq'), pairs)]
    pallas_call x6, Pallas kernels: 10.6 us -> 9.07 us  [analyse(): pl.pallas_call(functools.partial(analysis_kernel, first_tile, i * FIELDS...]
  transfers between devices with their start and end apart: 17 -> 17, of which waited for: 9 -> 10; matrix products, arithmetic and copies ran while one was open for 0% -> 0% of each run, Pallas kernels for 18% -> 16%
where the time goes in v4:
time: 65.4 us; the launch traced here: 65.3 us
  starting transfers between devices  27.7 us (42%)
  waiting for transfers between devices  20.1 us (31%)
  Pallas kernels  16.9 us (26%)
    ppermute x15, starting transfers between devices, swap(): return lax.ppermute(x, ('blk', 'freq'), pairs)  19.2 us
    ppermute x15, waiting for transfers between devices, swap(): return lax.ppermute(x, ('blk', 'freq'), pairs)  16.6 us
    pallas_call x6, Pallas kernels, analyse(): pl.pallas_call(functools.partial(analysis_kernel, first_tile, i * FIELDS...  9.07 us
    ppermute x1, starting transfers between devices, local(): lax.ppermute(far_edge, 'blk', joints + [(j, i) for i, j in joints])  8 us
    pallas_call x15, Pallas kernels, call(): pl.pallas_call(kernel, out_shape=list(shapes) + [token_shape], in_specs=[...  4.23 us
    pallas_call x1, Pallas kernels, local(): pl.pallas_call(synth_kernel, out_shape=[pltpu.VMEM((K, STEPS, FIELDS, row...  3.59 us
    ppermute x1, waiting for transfers between devices, local(): lax.ppermute(far_edge, 'blk', joints + [(j, i) for i, j in joints])  3.5 us
  transfers between devices with their start and end apart: 17, of which 10 were waited for; matrix products, arithmetic and copies ran while one was open for 0% of the time, Pallas kernels for 16%

profile of v4, /device:TPU:24, one launch (start us, length us, event | category | flops | bytes accessed | tf_op | source)
XLA Modules:
  0.0 65.3 jit_solution(376936279182947675)
XLA Ops:
  0.2 3.6 %synthesis.1 = (f32[2,8,5,64,128]{4,3,2,1,0:T(8,128)S(1)}, f32[41,8,128]{2,1,0:T(8,128)S(1)}, f32[41,8,128]{2,1,0:T(8,128)S(1)}, f32[64,128]{1,0:T(8,128)S(1)}, ...) custom-call(s32[4]{0:T(128)} %order_hbm.1, s32[4]{0:T(128)} %flips_hbm.1, ...), custom_call_target="tpu_custom_call" | custom-call | tf_op jit(solution)/shard_map/synthesis/pallas_call | solution.py:351
  3.9 1.1 %inner0.1 = (f32[8,5,24,128]{3,2,1,0:T(8,128)S(1)}, f32[8,5,24,128]{3,2,1,0:T(8,128)S(1)}, f32[8,128]{1,0:T(8,128)S(1)}) custom-call(f32[2,8,5,64,128]{4,3,2,1,0:T(8,128)S(1)} %get-tuple-element.61.forcing, f32[64,128]{1,0:T(8,128)S(1)} %get-tuple-element.62.speed, f32[8,128]{1,0:T(8,128)S(1)} %get-tuple-element.65._), custom_call_target="tpu_custom_call" | custom-call | tf_op jit(solution)/shard_map/inner0/pallas_call | solution.py:339
  4.9 1.6 %collective-permute-start.2 = (f32[8,5,24,128]{3,2,1,0:T(8,128)S(1)}, f32[8,5,24,128]{3,2,1,0:T(8,128)S(1)}, u32[]{:S(2)}, u32[]{:S(2)}) collective-permute-start(f32[8,5,24,128]{3,2,1,0:T(8,128)S(1)} %get-tuple-element.67), channel_id=1, source_target_pairs={{0,2},{1,3},{2,0},{3,1},{4,6},{5,7},{6,4},{7,5},{8,14},{9,15},{10,... | collective-permute-start | bytes 1474568 | tf_op jit(solution)/shard_map/ppermute | solution.py:309
  6.5 1.1 %inner1.1 = (f32[8,5,24,128]{3,2,1,0:T(8,128)S(1)}, f32[8,5,24,128]{3,2,1,0:T(8,128)S(1)}, f32[8,128]{1,0:T(8,128)S(1)}) custom-call(f32[2,8,5,64,128]{4,3,2,1,0:T(8,128)S(1)} %get-tuple-element.61.forcing, f32[64,128]{1,0:T(8,128)S(1)} %get-tuple-element.62.speed, f32[8,128]{1,0:T(8,128)S(1)} %get-tuple-element.68._), custom_call_target="tpu_custom_call" | custom-call | tf_op jit(solution)/shard_map/inner1/pallas_call | solution.py:339
  8.7 8.0 %collective-permute-start.1 = (f32[41,8,128]{2,1,0:T(8,128)S(1)}, f32[41,8,128]{2,1,0:T(8,128)S(1)}, u32[]{:S(2)}, u32[]{:S(2)}) collective-permute-start(f32[41,8,128]{2,1,0:T(8,128)S(1)} %get-tuple-element.64), channel_id=1, source_target_pairs={{8,16},{24,32},{40,48},{56,64},{72,80},{88,96},{104,112},{120,128}... | collective-permute-start | bytes 503816 | tf_op jit(solution)/shard_map/ppermute | solution.py:378
  16.8 1.1 %collective-permute-start.6 = (f32[4,5,24,128]{3,2,1,0:T(8,128)S(1)}, f32[4,5,24,128]{3,2,1,0:T(8,128)S(1)}, u32[]{:S(2)}, u32[]{:S(2)}) collective-permute-start(f32[4,5,24,128]{3,2,1,0:T(8,128)S(1)} %get-tuple-element.79), channel_id=1, source_target_pairs={{0,1},{1,0},{2,3},{3,2},{4,5},{5,4},{6,7},{7,6},{8,9},{9,8},{10,11... | collective-permute-start | bytes 737288 | tf_op jit(solution)/shard_map/ppermute | solution.py:309
  17.9 3.5 %collective-permute-done.1.from_far = f32[41,8,128]{2,1,0:T(8,128)S(1)} collective-permute-done((f32[41,8,128]{2,1,0:T(8,128)S(1)}, f32[41,8,128]{2,1,0:T(8,128)S(1)}, u32[]{:S(2)}, u32[]{:S(2)}) %collective-permute-start.1) | collective-permute-done | bytes 167968 | tf_op jit(solution)/shard_map/ppermute | solution.py:378
  21.4 1.6 %edges.1 = (f32[8,10,8,128]{3,2,1,0:T(8,128)S(1)}, f32[8,10,8,128]{3,2,1,0:T(8,128)S(1)}, f32[8,128]{1,0:T(8,128)S(1)}) custom-call(f32[2,8,5,64,128]{4,3,2,1,0:T(8,128)S(1)} %get-tuple-element.61.forcing, f32[64,128]{1,0:T(8,128)S(1)} %get-tuple-element.62.speed, f32[41,8,128]{2,1,0:T(8,128)S(1)} %collective-permute-done.from_chip, ...), custom_call_target="tpu_custom_call" | custom-call | tf_op jit(solution)/shard_map/edges/pallas_call | solution.py:339
  23.1 1.4 %collective-permute-start.5 = (f32[4,5,24,128]{3,2,1,0:T(8,128)S(1)}, f32[4,5,24,128]{3,2,1,0:T(8,128)S(1)}, u32[]{:S(2)}, u32[]{:S(2)}) collective-permute-start(f32[4,5,24,128]{3,2,1,0:T(8,128)S(1)} %get-tuple-element.77), channel_id=1, source_target_pairs={{0,1},{1,0},{2,3},{3,2},{4,5},{5,4},{6,7},{7,6},{8,9},{9,8},{10,11... | collective-permute-start | bytes 737288 | tf_op jit(solution)/shard_map/ppermute | solution.py:309
  24.5 1.4 %collective-permute-start.3 = (f32[8,10,8,128]{3,2,1,0:T(8,128)S(1)}, f32[8,10,8,128]{3,2,1,0:T(8,128)S(1)}, u32[]{:S(2)}, u32[]{:S(2)}) collective-permute-start(f32[8,10,8,128]{3,2,1,0:T(8,128)S(1)} %get-tuple-element.72), channel_id=1, source_target_pairs={{0,2},{1,3},{2,0},{3,1},{4,6},{5,7},{6,4},{7,5},{8,14},{9,15},{10,... | collective-permute-start | bytes 983048 | tf_op jit(solution)/shard_map/ppermute | solution.py:309
  25.9 2.2 %collective-permute-start.9 = (f32[4,5,24,128]{3,2,1,0:T(8,128)S(1)}, f32[4,5,24,128]{3,2,1,0:T(8,128)S(1)}, u32[]{:S(2)}, u32[]{:S(2)}) collective-permute-start(f32[4,5,24,128]{3,2,1,0:T(8,128)S(1)} %get-tuple-element.86.mine), channel_id=1, source_target_pairs={{0,6},{1,7},{2,4},{3,5},{4,2},{5,3},{6,0},{7,1},{8,10},{9,11},{10,... | collective-permute-start | bytes 737288 | tf_op jit(solution)/shard_map/ppermute | solution.py:309
  28.1 1.5 %collective-permute-done.5.arrived = f32[4,5,24,128]{3,2,1,0:T(8,128)S(1)} collective-permute-done((f32[4,5,24,128]{3,2,1,0:T(8,128)S(1)}, f32[4,5,24,128]{3,2,1,0:T(8,128)S(1)}, u32[]{:S(2)}, u32[]{:S(2)}) %collective-permute-start.5) | collective-permute-done | bytes 245792 | tf_op jit(solution)/shard_map/ppermute | solution.py:309
  29.7 2.8 %collective-permute-start.8 = (f32[4,5,24,128]{3,2,1,0:T(8,128)S(1)}, f32[4,5,24,128]{3,2,1,0:T(8,128)S(1)}, u32[]{:S(2)}, u32[]{:S(2)}) collective-permute-start(f32[4,5,24,128]{3,2,1,0:T(8,128)S(1)} %get-tuple-element.85.mine), channel_id=1, source_target_pairs={{0,6},{1,7},{2,4},{3,5},{4,2},{5,3},{6,0},{7,1},{8,10},{9,11},{10,... | collective-permute-start | bytes 737288 | tf_op jit(solution)/shard_map/ppermute | solution.py:309
  32.5 2.2 %collective-permute-done.3.arrived = f32[8,10,8,128]{3,2,1,0:T(8,128)S(1)} collective-permute-done((f32[8,10,8,128]{3,2,1,0:T(8,128)S(1)}, f32[8,10,8,128]{3,2,1,0:T(8,128)S(1)}, u32[]{:S(2)}, u32[]{:S(2)}) %collective-permute-start.3) | collective-permute-done | bytes 327712 | tf_op jit(solution)/shard_map/ppermute | solution.py:309
  34.8 1.1 %collective-permute-start.7 = (f32[4,10,8,128]{3,2,1,0:T(8,128)S(1)}, f32[4,10,8,128]{3,2,1,0:T(8,128)S(1)}, u32[]{:S(2)}, u32[]{:S(2)}) collective-permute-start(f32[4,10,8,128]{3,2,1,0:T(8,128)S(1)} %get-tuple-element.84), channel_id=1, source_target_pairs={{0,1},{1,0},{2,3},{3,2},{4,5},{5,4},{6,7},{7,6},{8,9},{9,8},{10,11... | collective-permute-start | bytes 491528 | tf_op jit(solution)/shard_map/ppermute | solution.py:309
  36.0 1.1 %collective-permute-start.12 = (f32[4,5,24,128]{3,2,1,0:T(8,128)S(1)}, f32[4,5,24,128]{3,2,1,0:T(8,128)S(1)}, u32[]{:S(2)}, u32[]{:S(2)}) collective-permute-start(f32[4,5,24,128]{3,2,1,0:T(8,128)S(1)} %get-tuple-element.92.mine), channel_id=1, source_target_pairs={{0,1},{1,0},{2,3},{3,2},{4,5},{5,4},{6,7},{7,6},{8,9},{9,8},{10,11... | collective-permute-start | bytes 737288 | tf_op jit(solution)/shard_map/ppermute | solution.py:309
  37.2 1.1 %collective-permute-start.11 = (f32[4,5,24,128]{3,2,1,0:T(8,128)S(1)}, f32[4,5,24,128]{3,2,1,0:T(8,128)S(1)}, u32[]{:S(2)}, u32[]{:S(2)}) collective-permute-start(f32[4,5,24,128]{3,2,1,0:T(8,128)S(1)} %get-tuple-element.91.mine), channel_id=1, source_target_pairs={{0,1},{1,0},{2,3},{3,2},{4,5},{5,4},{6,7},{7,6},{8,9},{9,8},{10,11... | collective-permute-start | bytes 737288 | tf_op jit(solution)/shard_map/ppermute | solution.py:309
  38.3 3.6 %collective-permute-done.7.arrived = f32[4,10,8,128]{3,2,1,0:T(8,128)S(1)} collective-permute-done((f32[4,10,8,128]{3,2,1,0:T(8,128)S(1)}, f32[4,10,8,128]{3,2,1,0:T(8,128)S(1)}, u32[]{:S(2)}, u32[]{:S(2)}) %collective-permute-start.7) | collective-permute-done | bytes 163872 | tf_op jit(solution)/shard_map/ppermute | solution.py:309
  41.9 1.3 %collective-permute-start.10 = (f32[4,10,8,128]{3,2,1,0:T(8,128)S(1)}, f32[4,10,8,128]{3,2,1,0:T(8,128)S(1)}, u32[]{:S(2)}, u32[]{:S(2)}) collective-permute-start(f32[4,10,8,128]{3,2,1,0:T(8,128)S(1)} %get-tuple-element.90.mine), channel_id=1, source_target_pairs={{0,6},{1,7},{2,4},{3,5},{4,2},{5,3},{6,0},{7,1},{8,10},{9,11},{10,... | collective-permute-start | bytes 491528 | tf_op jit(solution)/shard_map/ppermute | solution.py:309
  43.2 1.7 %collective-permute-done.12.arrived = f32[4,5,24,128]{3,2,1,0:T(8,128)S(1)} collective-permute-done((f32[4,5,24,128]{3,2,1,0:T(8,128)S(1)}, f32[4,5,24,128]{3,2,1,0:T(8,128)S(1)}, u32[]{:S(2)}, u32[]{:S(2)}) %collective-permute-start.12) | collective-permute-done | bytes 245792 | tf_op jit(solution)/shard_map/ppermute | solution.py:309
  45.6 3.6 %collective-permute-done.11.arrived = f32[4,5,24,128]{3,2,1,0:T(8,128)S(1)} collective-permute-done((f32[4,5,24,128]{3,2,1,0:T(8,128)S(1)}, f32[4,5,24,128]{3,2,1,0:T(8,128)S(1)}, u32[]{:S(2)}, u32[]{:S(2)}) %collective-permute-start.11) | collective-permute-done | bytes 245792 | tf_op jit(solution)/shard_map/ppermute | solution.py:309
  49.3 1.6 %collective-permute-start.13 = (f32[4,10,8,128]{3,2,1,0:T(8,128)S(1)}, f32[4,10,8,128]{3,2,1,0:T(8,128)S(1)}, u32[]{:S(2)}, u32[]{:S(2)}) collective-permute-start(f32[4,10,8,128]{3,2,1,0:T(8,128)S(1)} %get-tuple-element.96.mine), channel_id=1, source_target_pairs={{0,1},{1,0},{2,3},{3,2},{4,5},{5,4},{6,7},{7,6},{8,9},{9,8},{10,11... | collective-permute-start | bytes 491528 | tf_op jit(solution)/shard_map/ppermute | solution.py:309
  50.9 1.5 %analysis0.2 = (f32[16,10,8,8,128]{4,3,2,1,0:T(8,128)}, f32[8,128]{1,0:T(8,128)S(1)}) custom-call(s32[8,128]{1,0:T(8,128)S(1)} %get-tuple-element.59.meta, bf16[128,192]{1,0:T(8,128)(2,1)S(1)} %get-tuple-element.60.table, f32[8,5,24,128]{3,2,1,0:T(8,128)S(1)} %get-tuple-element.98.history, f32[8,128]{1,0:T(8,128)S(1)} %get-tuple-element.99._), custom_call_target="tpu_custom_call" | custom-call | tf_op jit(solution)/shard_map/analysis0/pallas_call | solution.py:433
  52.4 1.5 %analysis1.2 = (f32[16,10,8,8,128]{4,3,2,1,0:T(8,128)}, f32[8,128]{1,0:T(8,128)S(1)}) custom-call(s32[8,128]{1,0:T(8,128)S(1)} %get-tuple-element.59.meta, bf16[128,192]{1,0:T(8,128)(2,1)S(1)} %get-tuple-element.60.table, f32[8,5,24,128]{3,2,1,0:T(8,128)S(1)} %get-tuple-element.97.history, ...), custom_call_target="tpu_custom_call", output_to_operand_aliasing={{0}: (4, {})} | custom-call | tf_op jit(solution)/shard_map/analysis1/pallas_call | solution.py:433
  53.9 0.9 %collective-permute-done.13.arrived = f32[4,10,8,128]{3,2,1,0:T(8,128)S(1)} collective-permute-done((f32[4,10,8,128]{3,2,1,0:T(8,128)S(1)}, f32[4,10,8,128]{3,2,1,0:T(8,128)S(1)}, u32[]{:S(2)}, u32[]{:S(2)}) %collective-permute-start.13) | collective-permute-done | bytes 163872 | tf_op jit(solution)/shard_map/ppermute | solution.py:309
  54.8 1.3 %collective-permute-start.14 = (f32[8,10,8,128]{3,2,1,0:T(8,128)S(1)}, f32[8,10,8,128]{3,2,1,0:T(8,128)S(1)}, u32[]{:S(2)}, u32[]{:S(2)}) collective-permute-start(f32[8,10,8,128]{3,2,1,0:T(8,128)S(1)} %get-tuple-element.103.history), channel_id=1, source_target_pairs={{0,2},{1,3},{2,0},{3,1},{4,6},{5,7},{6,4},{7,5},{8,14},{9,15},{10,... | collective-permute-start | bytes 983048 | tf_op jit(solution)/shard_map/ppermute | solution.py:309
  56.1 1.5 %analysis0.3 = (f32[16,10,8,8,128]{4,3,2,1,0:T(8,128)}, f32[8,128]{1,0:T(8,128)S(1)}) custom-call(s32[8,128]{1,0:T(8,128)S(1)} %get-tuple-element.59.meta, bf16[128,192]{1,0:T(8,128)(2,1)S(1)} %get-tuple-element.60.table, f32[8,5,24,128]{3,2,1,0:T(8,128)S(1)} %collective-permute-done.16.history, ...), custom_call_target="tpu_custom_call", output_to_operand_aliasing={{0}: (4, {})} | custom-call | tf_op jit(solution)/shard_map/analysis0/pallas_call | solution.py:433
  57.5 1.3 %analysis2.2 = (f32[16,10,8,8,128]{4,3,2,1,0:T(8,128)}, f32[8,128]{1,0:T(8,128)S(1)}) custom-call(s32[8,128]{1,0:T(8,128)S(1)} %get-tuple-element.59.meta, bf16[128,192]{1,0:T(8,128)(2,1)S(1)} %get-tuple-element.60.table, f32[8,10,8,128]{3,2,1,0:T(8,128)S(1)} %get-tuple-element.103.history, ...), custom_call_target="tpu_custom_call", output_to_operand_aliasing={{0}: (4, {})} | custom-call | tf_op jit(solution)/shard_map/analysis2/pallas_call | solution.py:433
  58.8 0.9 %collective-permute-done.15.history = f32[8,5,24,128]{3,2,1,0:T(8,128)S(1)} collective-permute-done((f32[8,5,24,128]{3,2,1,0:T(8,128)S(1)}, f32[8,5,24,128]{3,2,1,0:T(8,128)S(1)}, u32[]{:S(2)}, u32[]{:S(2)}) %collective-permute-start.15) | collective-permute-done | bytes 491552 | tf_op jit(solution)/shard_map/ppermute | solution.py:309
  59.7 1.5 %analysis1.3 = (f32[16,10,8,8,128]{4,3,2,1,0:T(8,128)}, f32[8,128]{1,0:T(8,128)S(1)}) custom-call(s32[8,128]{1,0:T(8,128)S(1)} %get-tuple-element.59.meta, bf16[128,192]{1,0:T(8,128)(2,1)S(1)} %get-tuple-element.60.table, f32[8,5,24,128]{3,2,1,0:T(8,128)S(1)} %collective-permute-done.15.history, ...), custom_call_target="tpu_custom_call", output_to_operand_aliasing={{0}: (4, {})} | custom-call | tf_op jit(solution)/shard_map/analysis1/pallas_call | solution.py:433
  61.2 2.0 %collective-permute-done.14.history = f32[8,10,8,128]{3,2,1,0:T(8,128)S(1)} collective-permute-done((f32[8,10,8,128]{3,2,1,0:T(8,128)S(1)}, f32[8,10,8,128]{3,2,1,0:T(8,128)S(1)}, u32[]{:S(2)}, u32[]{:S(2)}) %collective-permute-start.14) | collective-permute-done | bytes 327712 | tf_op jit(solution)/shard_map/ppermute | solution.py:309
  63.2 1.9 %analysis2.3 = (f32[16,10,8,8,128]{4,3,2,1,0:T(8,128)}, f32[8,128]{1,0:T(8,128)}) custom-call(s32[8,128]{1,0:T(8,128)S(1)} %get-tuple-element.59.meta, bf16[128,192]{1,0:T(8,128)(2,1)S(1)} %get-tuple-element.60.table, f32[8,10,8,128]{3,2,1,0:T(8,128)S(1)} %collective-permute-done.14.history, ...), custom_call_target="tpu_custom_call", output_to_operand_aliasing={{0}: (4, {})} | custom-call | tf_op jit(solution)/shard_map/analysis2/pallas_call | solution.py:433
  (33 shorter events, 2.5 us)
Async XLA Ops:
  4.9 11.8 %collective-permute-start.2 = (f32[8,5,24,128]{3,2,1,0:T(8,128)S(1)}, f32[8,5,24,128]{3,2,1,0:T(8,128)S(1)}, u32[]{:S(2)}, u32[]{:S(2)}) collective-permute-start(f32[8,5,24,128]{3,2,1,0:T(8,128)S(1)} %get-tuple-element.67), channel_id=1, source_target_pairs={{0,2},{1,3},{2,0},{3,1},{4,6},{5,7},{6,4},{7,5},{8,14},{9,15},{10,... | collective-permute-start | bytes 1474568 | tf_op jit(solution)/shard_map/ppermute | solution.py:309
  7.6 15.5 %collective-permute-start.4 = (f32[8,5,24,128]{3,2,1,0:T(8,128)S(1)}, f32[8,5,24,128]{3,2,1,0:T(8,128)S(1)}, u32[]{:S(2)}, u32[]{:S(2)}) collective-permute-start(f32[8,5,24,128]{3,2,1,0:T(8,128)S(1)} %get-tuple-element.74), channel_id=1, source_target_pairs={{0,2},{1,3},{2,0},{3,1},{4,6},{5,7},{6,4},{7,5},{8,14},{9,15},{10,... | collective-permute-start | bytes 1474568 | tf_op jit(solution)/shard_map/ppermute | solution.py:309
  8.2 9.7 %collective-permute-start = (f32[41,8,128]{2,1,0:T(8,128)S(1)}, f32[41,8,128]{2,1,0:T(8,128)S(1)}, u32[]{:S(2)}, u32[]{:S(2)}) collective-permute-start(f32[41,8,128]{2,1,0:T(8,128)S(1)} %get-tuple-element.63), channel_id=1, source_target_pairs={{0,8},{8,0},{16,24},{24,16},{32,40},{40,32},{48,56},{56,48},{64,72... | collective-permute-start | bytes 503816 | tf_op jit(solution)/shard_map/ppermute | solution.py:376
  8.7 12.7 %collective-permute-start.1 = (f32[41,8,128]{2,1,0:T(8,128)S(1)}, f32[41,8,128]{2,1,0:T(8,128)S(1)}, u32[]{:S(2)}, u32[]{:S(2)}) collective-permute-start(f32[41,8,128]{2,1,0:T(8,128)S(1)} %get-tuple-element.64), channel_id=1, source_target_pairs={{8,16},{24,32},{40,48},{56,64},{72,80},{88,96},{104,112},{120,128}... | collective-permute-start | bytes 503816 | tf_op jit(solution)/shard_map/ppermute | solution.py:378
  16.8 9.1 %collective-permute-start.6 = (f32[4,5,24,128]{3,2,1,0:T(8,128)S(1)}, f32[4,5,24,128]{3,2,1,0:T(8,128)S(1)}, u32[]{:S(2)}, u32[]{:S(2)}) collective-permute-start(f32[4,5,24,128]{3,2,1,0:T(8,128)S(1)} %get-tuple-element.79), channel_id=1, source_target_pairs={{0,1},{1,0},{2,3},{3,2},{4,5},{5,4},{6,7},{7,6},{8,9},{9,8},{10,11... | collective-permute-start | bytes 737288 | tf_op jit(solution)/shard_map/ppermute | solution.py:309
  23.1 6.5 %collective-permute-start.5 = (f32[4,5,24,128]{3,2,1,0:T(8,128)S(1)}, f32[4,5,24,128]{3,2,1,0:T(8,128)S(1)}, u32[]{:S(2)}, u32[]{:S(2)}) collective-permute-start(f32[4,5,24,128]{3,2,1,0:T(8,128)S(1)} %get-tuple-element.77), channel_id=1, source_target_pairs={{0,1},{1,0},{2,3},{3,2},{4,5},{5,4},{6,7},{7,6},{8,9},{9,8},{10,11... | collective-permute-start | bytes 737288 | tf_op jit(solution)/shard_map/ppermute | solution.py:309
  24.5 10.3 %collective-permute-start.3 = (f32[8,10,8,128]{3,2,1,0:T(8,128)S(1)}, f32[8,10,8,128]{3,2,1,0:T(8,128)S(1)}, u32[]{:S(2)}, u32[]{:S(2)}) collective-permute-start(f32[8,10,8,128]{3,2,1,0:T(8,128)S(1)} %get-tuple-element.72), channel_id=1, source_target_pairs={{0,2},{1,3},{2,0},{3,1},{4,6},{5,7},{6,4},{7,5},{8,14},{9,15},{10,... | collective-permute-start | bytes 983048 | tf_op jit(solution)/shard_map/ppermute | solution.py:309
  25.9 10.0 %collective-permute-start.9 = (f32[4,5,24,128]{3,2,1,0:T(8,128)S(1)}, f32[4,5,24,128]{3,2,1,0:T(8,128)S(1)}, u32[]{:S(2)}, u32[]{:S(2)}) collective-permute-start(f32[4,5,24,128]{3,2,1,0:T(8,128)S(1)} %get-tuple-element.86.mine), channel_id=1, source_target_pairs={{0,6},{1,7},{2,4},{3,5},{4,2},{5,3},{6,0},{7,1},{8,10},{9,11},{10,... | collective-permute-start | bytes 737288 | tf_op jit(solution)/shard_map/ppermute | solution.py:309
  29.7 7.5 %collective-permute-start.8 = (f32[4,5,24,128]{3,2,1,0:T(8,128)S(1)}, f32[4,5,24,128]{3,2,1,0:T(8,128)S(1)}, u32[]{:S(2)}, u32[]{:S(2)}) collective-permute-start(f32[4,5,24,128]{3,2,1,0:T(8,128)S(1)} %get-tuple-element.85.mine), channel_id=1, source_target_pairs={{0,6},{1,7},{2,4},{3,5},{4,2},{5,3},{6,0},{7,1},{8,10},{9,11},{10,... | collective-permute-start | bytes 737288 | tf_op jit(solution)/shard_map/ppermute | solution.py:309
  34.8 7.1 %collective-permute-start.7 = (f32[4,10,8,128]{3,2,1,0:T(8,128)S(1)}, f32[4,10,8,128]{3,2,1,0:T(8,128)S(1)}, u32[]{:S(2)}, u32[]{:S(2)}) collective-permute-start(f32[4,10,8,128]{3,2,1,0:T(8,128)S(1)} %get-tuple-element.84), channel_id=1, source_target_pairs={{0,1},{1,0},{2,3},{3,2},{4,5},{5,4},{6,7},{7,6},{8,9},{9,8},{10,11... | collective-permute-start | bytes 491528 | tf_op jit(solution)/shard_map/ppermute | solution.py:309
  36.0 9.0 %collective-permute-start.12 = (f32[4,5,24,128]{3,2,1,0:T(8,128)S(1)}, f32[4,5,24,128]{3,2,1,0:T(8,128)S(1)}, u32[]{:S(2)}, u32[]{:S(2)}) collective-permute-start(f32[4,5,24,128]{3,2,1,0:T(8,128)S(1)} %get-tuple-element.92.mine), channel_id=1, source_target_pairs={{0,1},{1,0},{2,3},{3,2},{4,5},{5,4},{6,7},{7,6},{8,9},{9,8},{10,11... | collective-permute-start | bytes 737288 | tf_op jit(solution)/shard_map/ppermute | solution.py:309
  37.2 12.0 %collective-permute-start.11 = (f32[4,5,24,128]{3,2,1,0:T(8,128)S(1)}, f32[4,5,24,128]{3,2,1,0:T(8,128)S(1)}, u32[]{:S(2)}, u32[]{:S(2)}) collective-permute-start(f32[4,5,24,128]{3,2,1,0:T(8,128)S(1)} %get-tuple-element.91.mine), channel_id=1, source_target_pairs={{0,1},{1,0},{2,3},{3,2},{4,5},{5,4},{6,7},{7,6},{8,9},{9,8},{10,11... | collective-permute-start | bytes 737288 | tf_op jit(solution)/shard_map/ppermute | solution.py:309
  41.9 7.4 %collective-permute-start.10 = (f32[4,10,8,128]{3,2,1,0:T(8,128)S(1)}, f32[4,10,8,128]{3,2,1,0:T(8,128)S(1)}, u32[]{:S(2)}, u32[]{:S(2)}) collective-permute-start(f32[4,10,8,128]{3,2,1,0:T(8,128)S(1)} %get-tuple-element.90.mine), channel_id=1, source_target_pairs={{0,6},{1,7},{2,4},{3,5},{4,2},{5,3},{6,0},{7,1},{8,10},{9,11},{10,... | collective-permute-start | bytes 491528 | tf_op jit(solution)/shard_map/ppermute | solution.py:309
  45.0 11.1 %collective-permute-start.16 = (f32[8,5,24,128]{3,2,1,0:T(8,128)S(1)}, f32[8,5,24,128]{3,2,1,0:T(8,128)S(1)}, u32[]{:S(2)}, u32[]{:S(2)}) collective-permute-start(f32[8,5,24,128]{3,2,1,0:T(8,128)S(1)} %get-tuple-element.98.history), channel_id=1, source_target_pairs={{0,2},{1,3},{2,0},{3,1},{4,6},{5,7},{6,4},{7,5},{8,14},{9,15},{10,... | collective-permute-start | bytes 1474568 | tf_op jit(solution)/shard_map/ppermute | solution.py:309
  49.3 5.4 %collective-permute-start.13 = (f32[4,10,8,128]{3,2,1,0:T(8,128)S(1)}, f32[4,10,8,128]{3,2,1,0:T(8,128)S(1)}, u32[]{:S(2)}, u32[]{:S(2)}) collective-permute-start(f32[4,10,8,128]{3,2,1,0:T(8,128)S(1)} %get-tuple-element.96.mine), channel_id=1, source_target_pairs={{0,1},{1,0},{2,3},{3,2},{4,5},{5,4},{6,7},{7,6},{8,9},{9,8},{10,11... | collective-permute-start | bytes 491528 | tf_op jit(solution)/shard_map/ppermute | solution.py:309
  50.9 8.8 %collective-permute-start.15 = (f32[8,5,24,128]{3,2,1,0:T(8,128)S(1)}, f32[8,5,24,128]{3,2,1,0:T(8,128)S(1)}, u32[]{:S(2)}, u32[]{:S(2)}) collective-permute-start(f32[8,5,24,128]{3,2,1,0:T(8,128)S(1)} %get-tuple-element.97.history), channel_id=1, source_target_pairs={{0,2},{1,3},{2,0},{3,1},{4,6},{5,7},{6,4},{7,5},{8,14},{9,15},{10,... | collective-permute-start | bytes 1474568 | tf_op jit(solution)/shard_map/ppermute | solution.py:309
  54.8 8.5 %collective-permute-start.14 = (f32[8,10,8,128]{3,2,1,0:T(8,128)S(1)}, f32[8,10,8,128]{3,2,1,0:T(8,128)S(1)}, u32[]{:S(2)}, u32[]{:S(2)}) collective-permute-start(f32[8,10,8,128]{3,2,1,0:T(8,128)S(1)} %get-tuple-element.103.history), channel_id=1, source_target_pairs={{0,2},{1,3},{2,0},{3,1},{4,6},{5,7},{6,4},{7,5},{8,14},{9,15},{10,... | collective-permute-start | bytes 983048 | tf_op jit(solution)/shard_map/ppermute | solution.py:309
